TPU v7x, 128 devices: a whole 4x4x4 slice. The times are simulated.
128 devices in a mesh: grp: 2 (over y_hi), rows: 64 (over y_lo, z, x, core).
Axes of the slice: x: 4, y: 4 (y_hi: 2, y_lo: 2; y = y_hi * 2 + y_lo), z: 4, core: 2. Of those that a mesh axis runs over, the one named last changes fastest.
Arguments:
- bvals: bfloat16 [2, 98304, 6144], P('grp', 'rows'), may hold values from -16 to 16
- gap: float32 [2, 98304], P('grp', 'rows'), may hold values from 0.2 to 2
- live: int32 [2, 64], P('grp', 'rows'), may hold values from 192 to 1536, as said below
- laplace: int32 [1], replicated, may hold values from 0 to 5
Outputs:
- panels: bfloat16 [2, 98304, 512], P('grp', 'rows')
Inputs may be any that keep to these rules, and one draw needn't show every extreme that they name: Each device's live rows are its first ones; live[0, d] lies between 1152 and 1536, live[1, d] between 192 and 512.
All inputs are finite; a program needn't handle non-finite values.
Results may differ from a plain program's by a relative error of at most 0.0057.
Values may be sent and summed in bfloat16 or wider, within the bound.
No kernel may reach another device: no remote copies, remote signals or barrier semaphores. Data moves between devices by JAX's collectives and lax.ppermute only.
A program may use at most 192 MiB of HBM per device.

v0:
```python
import jax
import jax.numpy as jnp
from jax import lax
from jax.sharding import PartitionSpec as P

PANEL = 512


def from_partner(array, axis, bit):
    return lax.ppermute(array, axis, [(i, i ^ 1 << bit) for i in range(lax.axis_size(axis))])


def block_length():
    return 384


def gram_piece(source, amount, live_count):
    block = block_length()
    block_count = (live_count + block - 1) // block

    def add_block(index, total):
        block_rows = lax.dynamic_slice_in_dim(source, index * block, block, 0)
        return total + lax.dot_general(
            block_rows,
            block_rows[:, :PANEL],
            (((0,), (0,)), ((), ())),
            preferred_element_type=jnp.float32,
        )

    return lax.fori_loop(0, block_count, add_block, jnp.zeros((amount, PANEL), jnp.float32))


def on_device(bvals, gap, live, laplace):
    rows_here = bvals.shape[1]
    aux_count = bvals.shape[2]
    moment = 0.15 * jnp.exp(laplace[0].astype(jnp.float32) * jnp.log(jnp.float32(1.5)))
    count_live = live[0, 0]
    position = jnp.arange(rows_here, dtype=jnp.int32)
    factor = jnp.where(position < count_live, jnp.exp(-(gap[0] * moment) * 0.5), 0.0)
    scaled = (bvals[0] * factor[:, None]).astype(jnp.bfloat16)
    total_rows = rows_here * lax.axis_size("rows")
    summed = lax.psum_scatter(
        gram_piece(scaled, aux_count // lax.axis_size("rows") * lax.axis_size("rows"), count_live),
        "rows",
        scatter_dimension=0,
        tiled=True,
    )
    share_own = (summed / total_rows).astype(jnp.bfloat16)
    share_other = from_partner(share_own, "grp", 0)
    result = jnp.dot(
        scaled,
        lax.all_gather(share_other, "rows", axis=0, tiled=True),
        preferred_element_type=jnp.float32,
    )
    return result.astype(jnp.bfloat16)[None]


def solution(mesh):
    in_specs = (P("grp", "rows", None), P("grp", "rows"), P("grp", "rows"), P())
    out_specs = P("grp", "rows", None)
    return jax.shard_map(
        on_device, mesh=mesh, in_specs=in_specs, out_specs=out_specs, check_vma=False
    )
```

profile of v0, /device:TPU:1, one launch (start us, length us, event | category | flops | bytes accessed | tf_op | source)
XLA Modules:
  0.0 532.5 jit_solution(2159950049091060938)
XLA Ops:
  6.5 0.0 reduce-scatter.2.cloned.1.call-start
  7.9 0.7 exponential_reduce_fusion
  8.6 17.9 %fusion.3 = bf16[1536,6144]{1,0:T(8,128)(2,1)} fusion(bf16[1,1536,6144]{2,1,0:T(8,128)(2,1)} %param.6, f32[1536]{0:T(1024)S(1)} %fusion.5), kind=kLoop, calls=%fused_computation.5 | loop fusion | flops 28311552 | bytes 37754880 | tf_op jit(solution)/shard_map/convert_element_type | solution.py:40
  26.6 6.2 %broadcast_in_dim.12 = f32[6144,512]{1,0:T(8,128)} broadcast(f32[]{:T(128)} %constant.31.clone.1), dimensions={} | broadcast | bytes 12582916 | tf_op jit(solution)/shard_map/broadcast_in_dim | solution.py:30
  32.7 56.7 %while.10 = (s32[]{:T(128)}, f32[6144,512]{1,0:T(8,128)}, s32[]{:T(128)}, bf16[1536,6144]{1,0:T(8,128)(2,1)}, s32[]{:T(128)}, /*index=5*/s32[]{:T(128)}, s32[]{:T(128)}, s32[]{:T(128)}) while((s32[]{:T(128)}, f32[6144,512]{1,0:T(8,128)}, s32[]{:T(128)}, bf16[1536,6144]{1,0:T(8,128)(2,1)}, s32[]{:T(128)}, /*index=5*/s32[]{:T(128)}, s32[]{:T(128)}, ...), condition=%wide.region_1.2_spmd, body=%wide.region_0.1_spmd.sunk | while | flops 2419064832 | bytes 30278788 | solution.py:30
  32.7 14.2 %convolution_add_fusion.2 = f32[6144,512]{1,0:T(8,128)} fusion(f32[6144,512]{1,0:T(8,128)} %get-tuple-element.72, bf16[1536,6144]{1,0:T(8,128)(2,1)} %get-tuple-element.82, s32[]{:T(128)S(6)} %select_n.20), kind=kOutput, calls=%fused_computation.clone.1 | convolution fusion | flops 2419064832 | bytes 30278656 | tf_op jit(solution)/shard_map/while/body/dot_general | solution.py:23
  46.9 14.2 %convolution_add_fusion.2 = f32[6144,512]{1,0:T(8,128)} fusion(f32[6144,512]{1,0:T(8,128)} %get-tuple-element.72, bf16[1536,6144]{1,0:T(8,128)(2,1)} %get-tuple-element.82, s32[]{:T(128)S(6)} %select_n.20), kind=kOutput, calls=%fused_computation.clone.1 | convolution fusion | flops 2419064832 | bytes 30278656 | tf_op jit(solution)/shard_map/while/body/dot_general | solution.py:23
  61.1 14.2 %convolution_add_fusion.2 = f32[6144,512]{1,0:T(8,128)} fusion(f32[6144,512]{1,0:T(8,128)} %get-tuple-element.72, bf16[1536,6144]{1,0:T(8,128)(2,1)} %get-tuple-element.82, s32[]{:T(128)S(6)} %select_n.20), kind=kOutput, calls=%fused_computation.clone.1 | convolution fusion | flops 2419064832 | bytes 30278656 | tf_op jit(solution)/shard_map/while/body/dot_general | solution.py:23
  75.3 14.2 %convolution_add_fusion.2 = f32[6144,512]{1,0:T(8,128)} fusion(f32[6144,512]{1,0:T(8,128)} %get-tuple-element.72, bf16[1536,6144]{1,0:T(8,128)(2,1)} %get-tuple-element.82, s32[]{:T(128)S(6)} %select_n.20), kind=kOutput, calls=%fused_computation.clone.1 | convolution fusion | flops 2419064832 | bytes 30278656 | tf_op jit(solution)/shard_map/while/body/dot_general | solution.py:23
  89.5 0.0 reduce-scatter.2.cloned.1.call-update
  89.5 0.0 all-gather.2.cloned.1.call-start
  89.5 300.5 %reduce-scatter.2.cloned.1.call-done = f32[96,512]{1,0:T(8,128)} async-done(((f32[6144,512]{1,0:T(8,128)}), f32[96,512]{1,0:T(8,128)}) %reduce-scatter.2.cloned.1.call-update) | async-done | bytes 196624 | tf_op jit(solution)/shard_map/reduce_scatter | solution.py:42
  390.1 0.9 multiply_convert_fusion
  391.0 2.8 collective-permute-start
  393.8 2.2 collective-permute-done
  396.1 0.0 copy-start
  396.1 0.6 copy-done
  396.7 0.0 all-gather.2.cloned.1.call-update
  396.7 112.5 %all-gather.2.cloned.1.call-done = bf16[6144,512]{1,0:T(8,128)(2,1)} async-done(((bf16[96,512]{1,0:T(8,128)(2,1)}), bf16[6144,512]{1,0:T(8,128)(2,1)}) %all-gather.2.cloned.1.call-update) | async-done | bytes 6291472 | tf_op jit(solution)/shard_map/all_gather | solution.py:52
  509.2 16.4 %fusion.4 = bf16[1,1536,512]{2,1,0:T(8,128)(2,1)} fusion(bf16[1536,6144]{1,0:T(8,128)(2,1)} %get-tuple-element.91, bf16[6144,512]{1,0:T(8,128)(2,1)} %all-gather.2.cloned.1.call-done), kind=kOutput, calls=%fused_computation.7 | convolution fusion | flops 9664462848 | bytes 26738688 | tf_op jit(solution)/shard_map/dot_general | solution.py:50
  (1 shorter events, 0.0 us)
Async XLA Ops:
  6.5 383.5 %reduce-scatter.2.cloned.1.call-start = ((), (), s32[]{:S(2)}) async-start(), calls=%async_computation.1 | async-start | bytes 12779520 | tf_op jit(solution)/shard_map/reduce_scatter | solution.py:42
  89.5 419.7 %all-gather.2.cloned.1.call-start = ((), (), s32[]{:S(2)}) async-start(), calls=%async_computation.2 | async-start | bytes 6389760 | tf_op jit(solution)/shard_map/all_gather | solution.py:52
  391.0 5.1 collective-permute-start
  396.1 0.6 copy-start
Sparse Core Ops, SparseCore 0:
  89.6 300.4 reduce-scatter.1
  396.9 112.3 all-gather.1
where the time goes:
time: 533 us; the launch traced here: 532 us
  waiting for transfers between devices  415 us (78%)
  matrix products  73.1 us (14%)
  other arithmetic  19.6 us (4%)
  between operations  14.8 us (3%)
  local copies, waits for them, and re-layouts  6.82 us (1%)
    reduce_scatter x1, waiting for transfers between devices, on_device(): lax.psum_scatter(gram_piece(scaled, aux_count // lax.axis_size('rows') *...  301 us
    all_gather x1, waiting for transfers between devices, on_device(): lax.all_gather(share_other, 'rows', axis=0, tiled=True)  112 us
    dot_general x4, matrix products, add_block(): lax.dot_general(block_rows, block_rows[:, :PANEL], (((0,), (0,)), ((), ()...  56.7 us
    convert_element_type x1, other arithmetic, on_device(): scaled = (bvals[0] * factor[:, None]).astype(jnp.bfloat16)  17.9 us
    dot_general x1, matrix products, on_device(): jnp.dot(scaled, lax.all_gather(share_other, 'rows', axis=0, tiled=True),...  16.4 us
  transfers between devices with their start and end apart: 3, of which 3 were waited for; matrix products, arithmetic and copies ran while one was open for 0% of the time, Pallas kernels for 0%

commit v1 on v0

v1 whole, which is shorter than its diff:
```python
import jax
import jax.numpy as jnp
import numpy as np
from jax import lax
from jax.experimental import pallas as pl
from jax.experimental.pallas import tpu as pltpu
from jax.sharding import PartitionSpec as P

PANEL = 512
LANES = 128
SPOTS = 4
GROUP = 384
F32 = jnp.float32
BF16 = jnp.bfloat16
SIDES = (2, 2, SPOTS, SPOTS, 2)
AXES = ("grp", "rows")


def shifted(array, **steps):
    names = ("grp", "y", "z", "x", "core")
    pairs = []
    for source in range(int(np.prod(SIDES))):
        spot = np.unravel_index(source, SIDES)
        goal = [(a + steps.get(n, 0)) % s for a, n, s in zip(spot, names, SIDES)]
        pairs.append((source, int(np.ravel_multi_index(goal, SIDES))))
    return lax.ppermute(array, AXES, pairs)


def scale_into(target, source, factor, width):
    for k in range(width // LANES):
        cut = slice(k * LANES, (k + 1) * LANES)
        target[:, cut] = (source[:, cut].astype(F32) * factor[...]).astype(BF16)


def gram_body(groups_ref, core_ref, b_ref, mine_ref, theirs_ref, f_ref, ma, mb, ta, tb, panel, block):
    @pl.when(pl.program_id(0) == 0)
    def _():
        scale_into(panel.at[:, :256], mine_ref, f_ref, 256)
        scale_into(panel.at[:, 256:], theirs_ref, f_ref, 256)

    scale_into(block, b_ref, f_ref, GROUP)
    product = lax.dot_general(block[...], panel[...], (((0,), (0,)), ((), ())), preferred_element_type=F32)
    for k, out in enumerate((ma, mb, ta, tb)):
        out[0, 0] = product[:, k * LANES : (k + 1) * LANES].astype(BF16)


def gram_parts(groups, core, bvals, factor):
    rows, aux = bvals.shape
    shape = jax.ShapeDtypeStruct((SPOTS, SPOTS, GROUP, LANES), BF16)
    first = pl.BlockSpec((1, 1, GROUP, LANES), lambda s, g, c: (s // SPOTS, s % SPOTS, 0, 0))
    second = pl.BlockSpec((1, 1, GROUP, LANES), lambda s, g, c: (s % SPOTS, s // SPOTS, 0, 0))
    return pl.pallas_call(
        gram_body,
        grid_spec=pltpu.PrefetchScalarGridSpec(
            num_scalar_prefetch=2,
            grid=(SPOTS * SPOTS,),
            in_specs=[
                pl.BlockSpec((rows, GROUP), lambda s, g, c: (0, g[s])),
                pl.BlockSpec((rows, 256), lambda s, g, c: (0, c[0])),
                pl.BlockSpec((rows, 256), lambda s, g, c: (0, 1 - c[0])),
                pl.BlockSpec((rows, LANES), lambda s, g, c: (0, 0)),
            ],
            out_specs=[first, second, first, second],
            scratch_shapes=[pltpu.VMEM((rows, PANEL), BF16), pltpu.VMEM((rows, GROUP), BF16)],
        ),
        out_shape=[shape] * 4,
        compiler_params=pltpu.CompilerParams(vmem_limit_bytes=32 << 20),
        cost_estimate=pl.CostEstimate(flops=2 * rows * aux * PANEL, bytes_accessed=2 * rows * aux, transcendentals=0),
    )(groups, core, bvals, bvals, bvals, factor)


def panel_body(groups_ref, core_ref, b_ref, f_ref, *refs):
    parts, (out_ref, gram, block) = refs[:16], refs[16:]

    @pl.when(pl.program_id(0) == 0)
    def _():
        core = core_ref[0]
        for owner in range(2):
            start = pl.multiple_of(jnp.where(core == owner, 0, 256), 256)
            place = jnp.where(owner == 0, core, 1 - core)
            for i in range(SPOTS):
                for j in range(SPOTS):
                    row = pl.multiple_of(groups_ref[i * SPOTS + j] * GROUP, GROUP)
                    column = pl.multiple_of(place * 256, 256)
                    gram[pl.ds(row, GROUP), pl.ds(column, LANES)] = parts[owner * 8 + i][j]
                    gram[pl.ds(row, GROUP), pl.ds(column + LANES, LANES)] = parts[owner * 8 + 4 + j][i]

    scale_into(block, b_ref, f_ref, block.shape[1])
    out_ref[...] = jnp.dot(block[...], gram[...], preferred_element_type=F32).astype(BF16)


def panel_rows(groups, core, bvals, factor, parts):
    rows, aux = bvals.shape
    step = 256
    whole = pl.BlockSpec((SPOTS, GROUP, LANES), lambda s, g, c: (0, 0, 0))
    return pl.pallas_call(
        panel_body,
        grid_spec=pltpu.PrefetchScalarGridSpec(
            num_scalar_prefetch=2,
            grid=(rows // step,),
            in_specs=[
                pl.BlockSpec((step, aux), lambda s, g, c: (s, 0)),
                pl.BlockSpec((step, LANES), lambda s, g, c: (s, 0)),
            ]
            + [whole] * 16,
            out_specs=pl.BlockSpec((step, PANEL), lambda s, g, c: (s, 0)),
            scratch_shapes=[pltpu.VMEM((aux, PANEL), BF16), pltpu.VMEM((step, aux), BF16)],
        ),
        out_shape=jax.ShapeDtypeStruct((rows, PANEL), BF16),
        compiler_params=pltpu.CompilerParams(vmem_limit_bytes=48 << 20),
        cost_estimate=pl.CostEstimate(flops=2 * rows * aux * PANEL, bytes_accessed=2 * rows * aux, transcendentals=0),
    )(groups, core, bvals, factor, *parts)


def reduced(mine, theirs, first, second):
    got = shifted(theirs, core=1)
    pair = [mine[k].astype(F32) + got[k].astype(F32) for k in range(SPOTS)]
    held = pair[0]
    for arrived in [shifted(pair[k].astype(BF16), **{first: k}) for k in range(1, SPOTS)]:
        held = held + arrived.astype(F32)
    owned = held[0]
    for arrived in [shifted(held[k].astype(BF16), **{second: k}) for k in range(1, SPOTS)]:
        owned = owned + arrived.astype(F32)
    return owned.astype(BF16)


def gathered(owned, first, second):
    row = [owned] + [shifted(owned, **{first: SPOTS - k}) for k in range(1, SPOTS)]
    row = jnp.stack(row)
    plane = [row] + [shifted(row, **{second: SPOTS - k}) for k in range(1, SPOTS)]
    return plane, [shifted(part, core=1) for part in plane]


def on_device(bvals, gap, live, laplace):
    rows_here = bvals.shape[1]
    total_rows = rows_here * lax.axis_size("rows")
    moment = 0.15 * jnp.exp(laplace[0].astype(F32) * jnp.log(F32(1.5)))
    position = jnp.arange(rows_here, dtype=jnp.int32)
    factor = jnp.where(position < live[0, 0], jnp.exp(-(gap[0] * moment) * 0.5), 0.0)
    factor = jnp.broadcast_to(factor[:, None], (rows_here, LANES))
    here = lax.axis_index("rows")
    core, x, z = here % 2, here // 2 % SPOTS, here // 8 % SPOTS
    steps = jnp.arange(SPOTS, dtype=jnp.int32)
    groups = ((x + steps[:, None]) % SPOTS * SPOTS + (z + steps[None, :]) % SPOTS).reshape(-1)
    core = core.reshape(1)

    mine_a, mine_b, theirs_a, theirs_b = gram_parts(groups, core, bvals[0], factor)
    share = jnp.stack([reduced(mine_a, theirs_a, "x", "z"), reduced(mine_b, theirs_b, "z", "x")])
    near, far = shifted(share, grp=1, y=1), shifted(share, grp=1)
    whole = ((near.astype(F32) + far.astype(F32)) / total_rows).astype(BF16)
    own_a, other_a = gathered(whole[0], "z", "x")
    own_b, other_b = gathered(whole[1], "x", "z")
    return panel_rows(groups, core, bvals[0], factor, own_a + own_b + other_a + other_b)[None]


def solution(mesh):
    in_specs = (P("grp", "rows", None), P("grp", "rows"), P("grp", "rows"), P())
    out_specs = P("grp", "rows", None)
    return jax.shard_map(
        on_device, mesh=mesh, in_specs=in_specs, out_specs=out_specs, check_vma=False
    )
```

time: 533 us -> 155 us (0.29)
  waiting for transfers between devices: 415 us -> 61.1 us
  matrix products: 73.1 us -> 0 us
  starting transfers between devices: 2.86 us -> 52.9 us
  Pallas kernels: 0 us -> 36.5 us
  other arithmetic: 19.6 us -> 2.25 us
  between operations: 14.8 us -> 1.52 us
  local copies, waits for them, and re-layouts: 6.82 us -> 0.45 us
    reduce_scatter x1 -> x0, waiting for transfers between devices: 301 us -> none  [on_device(): lax.psum_scatter(gram_piece(scaled, aux_count // lax.axis_size('rows') *...]
    all_gather x1 -> x0, waiting for transfers between devices: 112 us -> none  [on_device(): lax.all_gather(share_other, 'rows', axis=0, tiled=True)]
    dot_general x5 -> x0, matrix products: 73.1 us -> none  [the longest x4 56.7 us: add_block(): lax.dot_general(block_rows, block_rows[:, :PANEL], (((0,), (0,)), ((), ()...]
    ppermute x1 -> x36, waiting for transfers between devices: 2.23 us -> 61.1 us  [shifted(): return lax.ppermute(array, AXES, pairs)]
    ppermute x1 -> x36, starting transfers between devices: 2.82 us -> 52.9 us  [shifted(): return lax.ppermute(array, AXES, pairs)]
    pallas_call x0 -> x2, Pallas kernels: none -> 36.5 us  [the longest x1 20.7 us: gram_parts(): pl.pallas_call(gram_body, grid_spec=pltpu.PrefetchScalarGridSpec(num_scal...]
    convert_element_type x2 -> x3, other arithmetic: 18.9 us -> 0.68 us  [the longest x2 0.62 us: reduced(): pair[k].astype(BF16)]
    broadcast_in_dim x1, local copies, waits for them, and re-layouts: 6.18 us -> 0.26 us  [on_device(): factor = jnp.broadcast_to(factor[:, None], (rows_here, LANES))]
  transfers between devices with their start and end apart: 3 -> 36, of which waited for: 3 -> 17; matrix products, arithmetic and copies ran while one was open for 0% -> 1% of each run, Pallas kernels for 0% -> 0%
where the time goes in v1:
time: 155 us
  waiting for transfers between devices  61.1 us (39%)
  starting transfers between devices  52.9 us (34%)
  Pallas kernels  36.5 us (24%)
  other arithmetic  2.25 us (1%)
    ppermute x36, waiting for transfers between devices, shifted(): return lax.ppermute(array, AXES, pairs)  61.1 us
    ppermute x36, starting transfers between devices, shifted(): return lax.ppermute(array, AXES, pairs)  52.9 us
    pallas_call x1, Pallas kernels, gram_parts(): pl.pallas_call(gram_body, grid_spec=pltpu.PrefetchScalarGridSpec(num_scal...  20.7 us
    pallas_call x1, Pallas kernels, panel_rows(): pl.pallas_call(panel_body, grid_spec=pltpu.PrefetchScalarGridSpec(num_sca...  15.7 us
  transfers between devices with their start and end apart: 36, of which 17 were waited for; matrix products, arithmetic and copies ran while one was open for 1% of the time, Pallas kernels for 0%

profile of v1, /device:TPU:1, one launch (start us, length us, event | category | flops | bytes accessed | tf_op | source)
XLA Modules:
  0.0 154.6 jit_solution(4837473782803055892)
XLA Ops:
  1.4 0.1 broadcast_add_fusion
  1.4 0.1 add.159.groups_ref
  1.5 0.7 exponential_reduce_fusion
  2.3 0.3 broadcast_in_dim.16.f_ref
  2.5 20.7 %shard_map.46 = (bf16[4,4,384,128]{3,2,1,0:T(8,128)(2,1)S(1)}, bf16[4,4,384,128]{3,2,1,0:T(8,128)(2,1)S(1)}, bf16[4,4,384,128]{3,2,1,0:T(8,128)(2,1)S(1)}, bf16[4,4,384,128]{3,2,1,0:T(8,128)(2,1)S(1)}) custom-call(s32[16]{0:T(128)S(1)} %add.159.groups_ref, s32[1]{0:T(128)} %bitcast.core_ref, bf16[1536,6144]{1,0:T(8,128)(2,1)} %bitcast.82, ...), custom_call_target="tpu_custom_call" | custom-call | flops 9663676416 | bytes 18874368 | tf_op jit(solution)/shard_map/pallas_call | solution.py:52
  23.3 1.5 collective-permute-start
  24.8 0.1 collective-permute-start.7
  24.9 2.9 %collective-permute-done = bf16[4,4,384,128]{3,2,1,0:T(8,128)(2,1)S(1)} collective-permute-done((bf16[4,4,384,128]{3,2,1,0:T(8,128)(2,1)S(1)}, bf16[4,4,384,128]{3,2,1,0:T(8,128)(2,1)S(1)}, u32[]{:S(2)}, u32[]{:S(2)}) %collective-permute-start) | collective-permute-done | bytes 1572896 | tf_op jit(solution)/shard_map/ppermute | solution.py:26
  27.8 0.3 fusion.4
  28.1 1.4 collective-permute-start.1
  29.5 1.4 collective-permute-start.3
  30.9 1.6 %collective-permute-start.2 = (bf16[4,384,128]{2,1,0:T(8,128)(2,1)S(1)}, bf16[4,384,128]{2,1,0:T(8,128)(2,1)S(1)}, u32[]{:S(2)}, u32[]{:S(2)}) collective-permute-start(bf16[4,384,128]{2,1,0:T(8,128)(2,1)S(1)} %get-tuple-element.19), channel_id=1, source_target_pairs={{0,4},{1,5},{2,6},{3,7},{4,0},{5,1},{6,2},{7,3},{8,12},{9,13},{10,... | collective-permute-start | bytes 1179656 | tf_op jit(solution)/shard_map/ppermute | solution.py:26
  32.5 0.3 fusion.7
  32.8 1.7 %collective-permute-start.8 = (bf16[4,384,128]{2,1,0:T(8,128)(2,1)S(1)}, bf16[4,384,128]{2,1,0:T(8,128)(2,1)S(1)}, u32[]{:S(2)}, u32[]{:S(2)}) collective-permute-start(bf16[4,384,128]{2,1,0:T(8,128)(2,1)S(1)} %get-tuple-element.20), channel_id=1, source_target_pairs={{0,8},{1,9},{2,10},{3,11},{4,12},{5,13},{6,14},{7,15},{8,16},{9,17... | collective-permute-start | bytes 1179656 | tf_op jit(solution)/shard_map/ppermute | solution.py:26
  34.5 2.2 %collective-permute-start.10 = (bf16[4,384,128]{2,1,0:T(8,128)(2,1)S(1)}, bf16[4,384,128]{2,1,0:T(8,128)(2,1)S(1)}, u32[]{:S(2)}, u32[]{:S(2)}) collective-permute-start(bf16[4,384,128]{2,1,0:T(8,128)(2,1)S(1)} %get-tuple-element.21), channel_id=1, source_target_pairs={{0,24},{1,25},{2,26},{3,27},{4,28},{5,29},{6,30},{7,31},{8,0},{9,1... | collective-permute-start | bytes 1179656 | tf_op jit(solution)/shard_map/ppermute | solution.py:26
  36.7 3.0 %collective-permute-done.1 = bf16[4,384,128]{2,1,0:T(8,128)(2,1)S(1)} collective-permute-done((bf16[4,384,128]{2,1,0:T(8,128)(2,1)S(1)}, bf16[4,384,128]{2,1,0:T(8,128)(2,1)S(1)}, u32[]{:S(2)}, u32[]{:S(2)}) %collective-permute-start.1) | collective-permute-done | bytes 393248 | tf_op jit(solution)/shard_map/ppermute | solution.py:26
  39.7 3.7 %collective-permute-start.9 = (bf16[4,384,128]{2,1,0:T(8,128)(2,1)S(1)}, bf16[4,384,128]{2,1,0:T(8,128)(2,1)S(1)}, u32[]{:S(2)}, u32[]{:S(2)}) collective-permute-start(bf16[4,384,128]{2,1,0:T(8,128)(2,1)S(1)} %get-tuple-element.22), channel_id=1, source_target_pairs={{0,16},{1,17},{2,18},{3,19},{4,20},{5,21},{6,22},{7,23},{8,24},{9,... | collective-permute-start | bytes 1179656 | tf_op jit(solution)/shard_map/ppermute | solution.py:26
  43.4 5.8 %collective-permute-done.2 = bf16[4,384,128]{2,1,0:T(8,128)(2,1)S(1)} collective-permute-done((bf16[4,384,128]{2,1,0:T(8,128)(2,1)S(1)}, bf16[4,384,128]{2,1,0:T(8,128)(2,1)S(1)}, u32[]{:S(2)}, u32[]{:S(2)}) %collective-permute-start.2) | collective-permute-done | bytes 393248 | tf_op jit(solution)/shard_map/ppermute | solution.py:26
  49.2 0.3 fusion.24
  49.5 1.7 %collective-permute-start.4 = (bf16[384,128]{1,0:T(8,128)(2,1)S(1)}, bf16[384,128]{1,0:T(8,128)(2,1)S(1)}, u32[]{:S(2)}, u32[]{:S(2)}) collective-permute-start(bf16[384,128]{1,0:T(8,128)(2,1)S(1)} %get-tuple-element.23), channel_id=1, source_target_pairs={{0,8},{1,9},{2,10},{3,11},{4,12},{5,13},{6,14},{7,15},{8,16},{9,17... | collective-permute-start | bytes 294920 | tf_op jit(solution)/shard_map/ppermute | solution.py:26
  51.2 2.2 %collective-permute-start.6 = (bf16[384,128]{1,0:T(8,128)(2,1)S(1)}, bf16[384,128]{1,0:T(8,128)(2,1)S(1)}, u32[]{:S(2)}, u32[]{:S(2)}) collective-permute-start(bf16[384,128]{1,0:T(8,128)(2,1)S(1)} %get-tuple-element.24), channel_id=1, source_target_pairs={{0,24},{1,25},{2,26},{3,27},{4,28},{5,29},{6,30},{7,31},{8,0},{9,1... | collective-permute-start | bytes 294920 | tf_op jit(solution)/shard_map/ppermute | solution.py:26
  53.4 1.2 collective-permute-start.5
  54.7 0.3 fusion.26
  55.0 0.6 collective-permute-start.11
  55.6 2.1 %collective-permute-start.13 = (bf16[384,128]{1,0:T(8,128)(2,1)S(1)}, bf16[384,128]{1,0:T(8,128)(2,1)S(1)}, u32[]{:S(2)}, u32[]{:S(2)}) collective-permute-start(bf16[384,128]{1,0:T(8,128)(2,1)S(1)} %get-tuple-element.27), channel_id=1, source_target_pairs={{0,6},{1,7},{2,0},{3,1},{4,2},{5,3},{6,4},{7,5},{8,14},{9,15},{10,... | collective-permute-start | bytes 294920 | tf_op jit(solution)/shard_map/ppermute | solution.py:26
  57.7 0.4 collective-permute-done.4
  58.2 2.1 %collective-permute-start.12 = (bf16[384,128]{1,0:T(8,128)(2,1)S(1)}, bf16[384,128]{1,0:T(8,128)(2,1)S(1)}, u32[]{:S(2)}, u32[]{:S(2)}) collective-permute-start(bf16[384,128]{1,0:T(8,128)(2,1)S(1)} %get-tuple-element.28), channel_id=1, source_target_pairs={{0,4},{1,5},{2,6},{3,7},{4,0},{5,1},{6,2},{7,3},{8,12},{9,13},{10,... | collective-permute-start | bytes 294920 | tf_op jit(solution)/shard_map/ppermute | solution.py:26
  60.2 0.1 fusion.18
  60.3 3.1 %collective-permute-done.12 = bf16[384,128]{1,0:T(8,128)(2,1)S(1)} collective-permute-done((bf16[384,128]{1,0:T(8,128)(2,1)S(1)}, bf16[384,128]{1,0:T(8,128)(2,1)S(1)}, u32[]{:S(2)}, u32[]{:S(2)}) %collective-permute-start.12) | collective-permute-done | bytes 98336 | tf_op jit(solution)/shard_map/ppermute | solution.py:26
  63.5 3.0 %collective-permute-start.15 = (bf16[2,384,128]{2,1,0:T(8,128)(2,1)S(1)}, bf16[2,384,128]{2,1,0:T(8,128)(2,1)S(1)}, u32[]{:S(2)}, u32[]{:S(2)}) collective-permute-start(bf16[2,384,128]{2,1,0:T(8,128)(2,1)S(1)} %pad_maximum_fusion.2), channel_id=1, source_target_pairs={{0,64},{1,65},{2,66},{3,67},{4,68},{5,69},{6,70},{7,71},{8,72},{9,... | collective-permute-start | bytes 589832 | tf_op jit(solution)/shard_map/ppermute | solution.py:26
  66.5 0.8 collective-permute-start.14
  67.3 2.3 %collective-permute-done.15 = bf16[2,384,128]{2,1,0:T(8,128)(2,1)S(1)} collective-permute-done((bf16[2,384,128]{2,1,0:T(8,128)(2,1)S(1)}, bf16[2,384,128]{2,1,0:T(8,128)(2,1)S(1)}, u32[]{:S(2)}, u32[]{:S(2)}) %collective-permute-start.15) | collective-permute-done | bytes 196640 | tf_op jit(solution)/shard_map/ppermute | solution.py:26
  69.6 5.5 %collective-permute-done.14 = bf16[2,384,128]{2,1,0:T(8,128)(2,1)S(1)} collective-permute-done((bf16[2,384,128]{2,1,0:T(8,128)(2,1)S(1)}, bf16[2,384,128]{2,1,0:T(8,128)(2,1)S(1)}, u32[]{:S(2)}, u32[]{:S(2)}) %collective-permute-start.14) | collective-permute-done | bytes 196640 | tf_op jit(solution)/shard_map/ppermute | solution.py:26
  75.1 0.1 multiply_convert_fusion
  75.2 0.1 fusion.28
  75.3 0.1 collective-permute-start.24
  75.4 2.5 %collective-permute-start.23 = (bf16[384,128]{1,0:T(8,128)(2,1)S(1)}, bf16[384,128]{1,0:T(8,128)(2,1)S(1)}, u32[]{:S(2)}, u32[]{:S(2)}) collective-permute-start(bf16[384,128]{1,0:T(8,128)(2,1)S(1)} %get-tuple-element.31), channel_id=1, source_target_pairs={{0,4},{1,5},{2,6},{3,7},{4,0},{5,1},{6,2},{7,3},{8,12},{9,13},{10,... | collective-permute-start | bytes 294920 | tf_op jit(solution)/shard_map/ppermute | solution.py:26
  77.8 2.0 %collective-permute-start.22 = (bf16[384,128]{1,0:T(8,128)(2,1)S(1)}, bf16[384,128]{1,0:T(8,128)(2,1)S(1)}, u32[]{:S(2)}, u32[]{:S(2)}) collective-permute-start(bf16[384,128]{1,0:T(8,128)(2,1)S(1)} %get-tuple-element.31), channel_id=1, source_target_pairs={{0,6},{1,7},{2,0},{3,1},{4,2},{5,3},{6,4},{7,5},{8,14},{9,15},{10,... | collective-permute-start | bytes 294920 | tf_op jit(solution)/shard_map/ppermute | solution.py:26
  79.8 0.9 collective-permute-done.24
  80.7 0.8 collective-permute-done.23
  81.4 0.5 collective-permute-done.22
  82.0 3.3 %collective-permute-start.32 = (bf16[4,384,128]{2,1,0:T(8,128)(2,1)S(1)}, bf16[4,384,128]{2,1,0:T(8,128)(2,1)S(1)}, u32[]{:S(2)}, u32[]{:S(2)}) collective-permute-start(bf16[4,384,128]{2,1,0:T(8,128)(2,1)S(1)} %pad_maximum_fusion.1.refs_4_), channel_id=1, source_target_pairs={{0,1},{1,0},{2,3},{3,2},{4,5},{5,4},{6,7},{7,6},{8,9},{9,8},{10,11... | collective-permute-start | bytes 1179656 | tf_op jit(solution)/shard_map/ppermute | solution.py:26
  85.3 0.8 collective-permute-start.27
  86.0 1.2 collective-permute-start.26
  87.2 1.6 %collective-permute-start.25 = (bf16[4,384,128]{2,1,0:T(8,128)(2,1)S(1)}, bf16[4,384,128]{2,1,0:T(8,128)(2,1)S(1)}, u32[]{:S(2)}, u32[]{:S(2)}) collective-permute-start(bf16[4,384,128]{2,1,0:T(8,128)(2,1)S(1)} %pad_maximum_fusion.1.refs_4_), channel_id=1, source_target_pairs={{0,24},{1,25},{2,26},{3,27},{4,28},{5,29},{6,30},{7,31},{8,0},{9,1... | collective-permute-start | bytes 1179656 | tf_op jit(solution)/shard_map/ppermute | solution.py:26
  88.8 1.5 collective-permute-start.17
  90.3 16.7 %collective-permute-done.17 = bf16[384,128]{1,0:T(8,128)(2,1)S(1)} collective-permute-done((bf16[384,128]{1,0:T(8,128)(2,1)S(1)}, bf16[384,128]{1,0:T(8,128)(2,1)S(1)}, u32[]{:S(2)}, u32[]{:S(2)}) %collective-permute-start.17) | collective-permute-done | bytes 98336 | tf_op jit(solution)/shard_map/ppermute | solution.py:26
  107.0 3.4 %collective-permute-start.16 = (bf16[384,128]{1,0:T(8,128)(2,1)S(1)}, bf16[384,128]{1,0:T(8,128)(2,1)S(1)}, u32[]{:S(2)}, u32[]{:S(2)}) collective-permute-start(bf16[384,128]{1,0:T(8,128)(2,1)S(1)} %get-tuple-element.30), channel_id=1, source_target_pairs={{0,24},{1,25},{2,26},{3,27},{4,28},{5,29},{6,30},{7,31},{8,0},{9,1... | collective-permute-start | bytes 294920 | tf_op jit(solution)/shard_map/ppermute | solution.py:26
  110.4 1.6 %collective-permute-done.16 = bf16[384,128]{1,0:T(8,128)(2,1)S(1)} collective-permute-done((bf16[384,128]{1,0:T(8,128)(2,1)S(1)}, bf16[384,128]{1,0:T(8,128)(2,1)S(1)}, u32[]{:S(2)}, u32[]{:S(2)}) %collective-permute-start.16) | collective-permute-done | bytes 98336 | tf_op jit(solution)/shard_map/ppermute | solution.py:26
  112.1 2.3 %collective-permute-start.28 = (bf16[4,384,128]{2,1,0:T(8,128)(2,1)S(1)}, bf16[4,384,128]{2,1,0:T(8,128)(2,1)S(1)}, u32[]{:S(2)}, u32[]{:S(2)}) collective-permute-start(bf16[4,384,128]{2,1,0:T(8,128)(2,1)S(1)} %pad_maximum_fusion.refs_0_), channel_id=1, source_target_pairs={{0,1},{1,0},{2,3},{3,2},{4,5},{5,4},{6,7},{7,6},{8,9},{9,8},{10,11... | collective-permute-start | bytes 1179656 | tf_op jit(solution)/shard_map/ppermute | solution.py:26
  114.4 1.2 collective-permute-start.21
  115.6 2.4 %collective-permute-start.20 = (bf16[4,384,128]{2,1,0:T(8,128)(2,1)S(1)}, bf16[4,384,128]{2,1,0:T(8,128)(2,1)S(1)}, u32[]{:S(2)}, u32[]{:S(2)}) collective-permute-start(bf16[4,384,128]{2,1,0:T(8,128)(2,1)S(1)} %pad_maximum_fusion.refs_0_), channel_id=1, source_target_pairs={{0,4},{1,5},{2,6},{3,7},{4,0},{5,1},{6,2},{7,3},{8,12},{9,13},{10,... | collective-permute-start | bytes 1179656 | tf_op jit(solution)/shard_map/ppermute | solution.py:26
  118.0 0.3 collective-permute-start.19
  118.3 0.9 collective-permute-start.35
  119.2 0.1 collective-permute-start.34
  119.3 7.0 %collective-permute-done.21.refs_3_ = bf16[4,384,128]{2,1,0:T(8,128)(2,1)S(1)} collective-permute-done((bf16[4,384,128]{2,1,0:T(8,128)(2,1)S(1)}, bf16[4,384,128]{2,1,0:T(8,128)(2,1)S(1)}, u32[]{:S(2)}, u32[]{:S(2)}) %collective-permute-start.21) | collective-permute-done | bytes 393248 | tf_op jit(solution)/shard_map/ppermute | solution.py:26
  126.3 0.9 collective-permute-start.33
  127.1 8.5 %collective-permute-done.20.refs_2_ = bf16[4,384,128]{2,1,0:T(8,128)(2,1)S(1)} collective-permute-done((bf16[4,384,128]{2,1,0:T(8,128)(2,1)S(1)}, bf16[4,384,128]{2,1,0:T(8,128)(2,1)S(1)}, u32[]{:S(2)}, u32[]{:S(2)}) %collective-permute-start.20) | collective-permute-done | bytes 393248 | tf_op jit(solution)/shard_map/ppermute | solution.py:26
  135.6 0.9 collective-permute-start.31
  136.5 0.5 collective-permute-start.29
  137.0 0.8 collective-permute-done.31.refs_11_
  137.8 0.6 collective-permute-done.30.refs_10_
  138.4 0.6 collective-permute-done.29.refs_9_
  138.9 15.7 %shard_map.47 = bf16[1536,512]{1,0:T(8,128)(2,1)} custom-call(s32[16]{0:T(128)S(1)} %add.159.groups_ref, s32[1]{0:T(128)} %bitcast.core_ref, bf16[1536,6144]{1,0:T(8,128)(2,1)} %bitcast.85, f32[1536,128]{1,0:T(8,128)} %copy-done, bf16[4,384,128]{2,1,0:T(8,128)(2,1)S(1)} %pad_maximum_fusion.refs_0_, bf16[4,384,128]{2,1,0:T(8,128)(2,1)S(1)} %collective-permute-done.19.refs_1_, ...), custom_call_target="tpu_custom_call" | custom-call | flops 9663676416 | bytes 18874368 | tf_op jit(solution)/shard_map/pallas_call | solution.py:96
  (33 shorter events, 0.3 us)
Async XLA Ops:
  2.5 20.8 %copy-start = (f32[1536,128]{1,0:T(8,128)}, f32[1536,128]{1,0:T(8,128)S(1)}, u32[]{:S(2)}) copy-start(f32[1536,128]{1,0:T(8,128)S(1)} %broadcast_in_dim.16.f_ref) | copy-start | bytes 2359300
  23.3 4.5 %collective-permute-start = (bf16[4,4,384,128]{3,2,1,0:T(8,128)(2,1)S(1)}, bf16[4,4,384,128]{3,2,1,0:T(8,128)(2,1)S(1)}, u32[]{:S(2)}, u32[]{:S(2)}) collective-permute-start(bf16[4,4,384,128]{3,2,1,0:T(8,128)(2,1)S(1)} %get-tuple-element.10), channel_id=1, source_target_pairs={{0,1},{1,0},{2,3},{3,2},{4,5},{5,4},{6,7},{7,6},{8,9},{9,8},{10,11... | collective-permute-start | bytes 4718600 | tf_op jit(solution)/shard_map/ppermute | solution.py:26
  24.8 7.7 %collective-permute-start.7 = (bf16[4,4,384,128]{3,2,1,0:T(8,128)(2,1)S(1)}, bf16[4,4,384,128]{3,2,1,0:T(8,128)(2,1)S(1)}, u32[]{:S(2)}, u32[]{:S(2)}) collective-permute-start(bf16[4,4,384,128]{3,2,1,0:T(8,128)(2,1)S(1)} %get-tuple-element.12), channel_id=1, source_target_pairs={{0,1},{1,0},{2,3},{3,2},{4,5},{5,4},{6,7},{7,6},{8,9},{9,8},{10,11... | collective-permute-start | bytes 4718600 | tf_op jit(solution)/shard_map/ppermute | solution.py:26
  28.1 11.6 %collective-permute-start.1 = (bf16[4,384,128]{2,1,0:T(8,128)(2,1)S(1)}, bf16[4,384,128]{2,1,0:T(8,128)(2,1)S(1)}, u32[]{:S(2)}, u32[]{:S(2)}) collective-permute-start(bf16[4,384,128]{2,1,0:T(8,128)(2,1)S(1)} %get-tuple-element.17), channel_id=1, source_target_pairs={{0,2},{1,3},{2,4},{3,5},{4,6},{5,7},{6,0},{7,1},{8,10},{9,11},{10,... | collective-permute-start | bytes 1179656 | tf_op jit(solution)/shard_map/ppermute | solution.py:26
  29.5 13.9 %collective-permute-start.3 = (bf16[4,384,128]{2,1,0:T(8,128)(2,1)S(1)}, bf16[4,384,128]{2,1,0:T(8,128)(2,1)S(1)}, u32[]{:S(2)}, u32[]{:S(2)}) collective-permute-start(bf16[4,384,128]{2,1,0:T(8,128)(2,1)S(1)} %get-tuple-element.18), channel_id=1, source_target_pairs={{0,6},{1,7},{2,0},{3,1},{4,2},{5,3},{6,4},{7,5},{8,14},{9,15},{10,... | collective-permute-start | bytes 1179656 | tf_op jit(solution)/shard_map/ppermute | solution.py:26
  30.9 18.3 %collective-permute-start.2 = (bf16[4,384,128]{2,1,0:T(8,128)(2,1)S(1)}, bf16[4,384,128]{2,1,0:T(8,128)(2,1)S(1)}, u32[]{:S(2)}, u32[]{:S(2)}) collective-permute-start(bf16[4,384,128]{2,1,0:T(8,128)(2,1)S(1)} %get-tuple-element.19), channel_id=1, source_target_pairs={{0,4},{1,5},{2,6},{3,7},{4,0},{5,1},{6,2},{7,3},{8,12},{9,13},{10,... | collective-permute-start | bytes 1179656 | tf_op jit(solution)/shard_map/ppermute | solution.py:26
  32.8 20.6 %collective-permute-start.8 = (bf16[4,384,128]{2,1,0:T(8,128)(2,1)S(1)}, bf16[4,384,128]{2,1,0:T(8,128)(2,1)S(1)}, u32[]{:S(2)}, u32[]{:S(2)}) collective-permute-start(bf16[4,384,128]{2,1,0:T(8,128)(2,1)S(1)} %get-tuple-element.20), channel_id=1, source_target_pairs={{0,8},{1,9},{2,10},{3,11},{4,12},{5,13},{6,14},{7,15},{8,16},{9,17... | collective-permute-start | bytes 1179656 | tf_op jit(solution)/shard_map/ppermute | solution.py:26
  34.5 20.2 %collective-permute-start.10 = (bf16[4,384,128]{2,1,0:T(8,128)(2,1)S(1)}, bf16[4,384,128]{2,1,0:T(8,128)(2,1)S(1)}, u32[]{:S(2)}, u32[]{:S(2)}) collective-permute-start(bf16[4,384,128]{2,1,0:T(8,128)(2,1)S(1)} %get-tuple-element.21), channel_id=1, source_target_pairs={{0,24},{1,25},{2,26},{3,27},{4,28},{5,29},{6,30},{7,31},{8,0},{9,1... | collective-permute-start | bytes 1179656 | tf_op jit(solution)/shard_map/ppermute | solution.py:26
  39.7 14.9 %collective-permute-start.9 = (bf16[4,384,128]{2,1,0:T(8,128)(2,1)S(1)}, bf16[4,384,128]{2,1,0:T(8,128)(2,1)S(1)}, u32[]{:S(2)}, u32[]{:S(2)}) collective-permute-start(bf16[4,384,128]{2,1,0:T(8,128)(2,1)S(1)} %get-tuple-element.22), channel_id=1, source_target_pairs={{0,16},{1,17},{2,18},{3,19},{4,20},{5,21},{6,22},{7,23},{8,24},{9,... | collective-permute-start | bytes 1179656 | tf_op jit(solution)/shard_map/ppermute | solution.py:26
  49.5 8.6 %collective-permute-start.4 = (bf16[384,128]{1,0:T(8,128)(2,1)S(1)}, bf16[384,128]{1,0:T(8,128)(2,1)S(1)}, u32[]{:S(2)}, u32[]{:S(2)}) collective-permute-start(bf16[384,128]{1,0:T(8,128)(2,1)S(1)} %get-tuple-element.23), channel_id=1, source_target_pairs={{0,8},{1,9},{2,10},{3,11},{4,12},{5,13},{6,14},{7,15},{8,16},{9,17... | collective-permute-start | bytes 294920 | tf_op jit(solution)/shard_map/ppermute | solution.py:26
  51.2 9.0 %collective-permute-start.6 = (bf16[384,128]{1,0:T(8,128)(2,1)S(1)}, bf16[384,128]{1,0:T(8,128)(2,1)S(1)}, u32[]{:S(2)}, u32[]{:S(2)}) collective-permute-start(bf16[384,128]{1,0:T(8,128)(2,1)S(1)} %get-tuple-element.24), channel_id=1, source_target_pairs={{0,24},{1,25},{2,26},{3,27},{4,28},{5,29},{6,30},{7,31},{8,0},{9,1... | collective-permute-start | bytes 294920 | tf_op jit(solution)/shard_map/ppermute | solution.py:26
  53.4 6.8 %collective-permute-start.5 = (bf16[384,128]{1,0:T(8,128)(2,1)S(1)}, bf16[384,128]{1,0:T(8,128)(2,1)S(1)}, u32[]{:S(2)}, u32[]{:S(2)}) collective-permute-start(bf16[384,128]{1,0:T(8,128)(2,1)S(1)} %get-tuple-element.25), channel_id=1, source_target_pairs={{0,16},{1,17},{2,18},{3,19},{4,20},{5,21},{6,22},{7,23},{8,24},{9,... | collective-permute-start | bytes 294920 | tf_op jit(solution)/shard_map/ppermute | solution.py:26
  55.0 5.3 %collective-permute-start.11 = (bf16[384,128]{1,0:T(8,128)(2,1)S(1)}, bf16[384,128]{1,0:T(8,128)(2,1)S(1)}, u32[]{:S(2)}, u32[]{:S(2)}) collective-permute-start(bf16[384,128]{1,0:T(8,128)(2,1)S(1)} %get-tuple-element.26), channel_id=1, source_target_pairs={{0,2},{1,3},{2,4},{3,5},{4,6},{5,7},{6,0},{7,1},{8,10},{9,11},{10,... | collective-permute-start | bytes 294920 | tf_op jit(solution)/shard_map/ppermute | solution.py:26
  55.6 4.8 %collective-permute-start.13 = (bf16[384,128]{1,0:T(8,128)(2,1)S(1)}, bf16[384,128]{1,0:T(8,128)(2,1)S(1)}, u32[]{:S(2)}, u32[]{:S(2)}) collective-permute-start(bf16[384,128]{1,0:T(8,128)(2,1)S(1)} %get-tuple-element.27), channel_id=1, source_target_pairs={{0,6},{1,7},{2,0},{3,1},{4,2},{5,3},{6,4},{7,5},{8,14},{9,15},{10,... | collective-permute-start | bytes 294920 | tf_op jit(solution)/shard_map/ppermute | solution.py:26
  58.2 5.3 %collective-permute-start.12 = (bf16[384,128]{1,0:T(8,128)(2,1)S(1)}, bf16[384,128]{1,0:T(8,128)(2,1)S(1)}, u32[]{:S(2)}, u32[]{:S(2)}) collective-permute-start(bf16[384,128]{1,0:T(8,128)(2,1)S(1)} %get-tuple-element.28), channel_id=1, source_target_pairs={{0,4},{1,5},{2,6},{3,7},{4,0},{5,1},{6,2},{7,3},{8,12},{9,13},{10,... | collective-permute-start | bytes 294920 | tf_op jit(solution)/shard_map/ppermute | solution.py:26
  63.5 6.1 %collective-permute-start.15 = (bf16[2,384,128]{2,1,0:T(8,128)(2,1)S(1)}, bf16[2,384,128]{2,1,0:T(8,128)(2,1)S(1)}, u32[]{:S(2)}, u32[]{:S(2)}) collective-permute-start(bf16[2,384,128]{2,1,0:T(8,128)(2,1)S(1)} %pad_maximum_fusion.2), channel_id=1, source_target_pairs={{0,64},{1,65},{2,66},{3,67},{4,68},{5,69},{6,70},{7,71},{8,72},{9,... | collective-permute-start | bytes 589832 | tf_op jit(solution)/shard_map/ppermute | solution.py:26
  66.5 8.6 %collective-permute-start.14 = (bf16[2,384,128]{2,1,0:T(8,128)(2,1)S(1)}, bf16[2,384,128]{2,1,0:T(8,128)(2,1)S(1)}, u32[]{:S(2)}, u32[]{:S(2)}) collective-permute-start(bf16[2,384,128]{2,1,0:T(8,128)(2,1)S(1)} %pad_maximum_fusion.2), channel_id=1, source_target_pairs={{0,96},{1,97},{2,98},{3,99},{4,100},{5,101},{6,102},{7,103},{8,104... | collective-permute-start | bytes 589832 | tf_op jit(solution)/shard_map/ppermute | solution.py:26
  75.3 5.4 %collective-permute-start.24 = (bf16[384,128]{1,0:T(8,128)(2,1)S(1)}, bf16[384,128]{1,0:T(8,128)(2,1)S(1)}, u32[]{:S(2)}, u32[]{:S(2)}) collective-permute-start(bf16[384,128]{1,0:T(8,128)(2,1)S(1)} %get-tuple-element.31), channel_id=1, source_target_pairs={{0,2},{1,3},{2,4},{3,5},{4,6},{5,7},{6,0},{7,1},{8,10},{9,11},{10,... | collective-permute-start | bytes 294920 | tf_op jit(solution)/shard_map/ppermute | solution.py:26
  75.4 6.1 %collective-permute-start.23 = (bf16[384,128]{1,0:T(8,128)(2,1)S(1)}, bf16[384,128]{1,0:T(8,128)(2,1)S(1)}, u32[]{:S(2)}, u32[]{:S(2)}) collective-permute-start(bf16[384,128]{1,0:T(8,128)(2,1)S(1)} %get-tuple-element.31), channel_id=1, source_target_pairs={{0,4},{1,5},{2,6},{3,7},{4,0},{5,1},{6,2},{7,3},{8,12},{9,13},{10,... | collective-permute-start | bytes 294920 | tf_op jit(solution)/shard_map/ppermute | solution.py:26
  77.8 4.1 %collective-permute-start.22 = (bf16[384,128]{1,0:T(8,128)(2,1)S(1)}, bf16[384,128]{1,0:T(8,128)(2,1)S(1)}, u32[]{:S(2)}, u32[]{:S(2)}) collective-permute-start(bf16[384,128]{1,0:T(8,128)(2,1)S(1)} %get-tuple-element.31), channel_id=1, source_target_pairs={{0,6},{1,7},{2,0},{3,1},{4,2},{5,3},{6,4},{7,5},{8,14},{9,15},{10,... | collective-permute-start | bytes 294920 | tf_op jit(solution)/shard_map/ppermute | solution.py:26
  79.8 9.0 %collective-permute-start.18 = (bf16[384,128]{1,0:T(8,128)(2,1)S(1)}, bf16[384,128]{1,0:T(8,128)(2,1)S(1)}, u32[]{:S(2)}, u32[]{:S(2)}) collective-permute-start(bf16[384,128]{1,0:T(8,128)(2,1)S(1)} %get-tuple-element.30), channel_id=1, source_target_pairs={{0,8},{1,9},{2,10},{3,11},{4,12},{5,13},{6,14},{7,15},{8,16},{9,17... | collective-permute-start | bytes 294920 | tf_op jit(solution)/shard_map/ppermute | solution.py:26
  82.0 32.4 %collective-permute-start.32 = (bf16[4,384,128]{2,1,0:T(8,128)(2,1)S(1)}, bf16[4,384,128]{2,1,0:T(8,128)(2,1)S(1)}, u32[]{:S(2)}, u32[]{:S(2)}) collective-permute-start(bf16[4,384,128]{2,1,0:T(8,128)(2,1)S(1)} %pad_maximum_fusion.1.refs_4_), channel_id=1, source_target_pairs={{0,1},{1,0},{2,3},{3,2},{4,5},{5,4},{6,7},{7,6},{8,9},{9,8},{10,11... | collective-permute-start | bytes 1179656 | tf_op jit(solution)/shard_map/ppermute | solution.py:26
  85.3 30.3 %collective-permute-start.27 = (bf16[4,384,128]{2,1,0:T(8,128)(2,1)S(1)}, bf16[4,384,128]{2,1,0:T(8,128)(2,1)S(1)}, u32[]{:S(2)}, u32[]{:S(2)}) collective-permute-start(bf16[4,384,128]{2,1,0:T(8,128)(2,1)S(1)} %pad_maximum_fusion.1.refs_4_), channel_id=1, source_target_pairs={{0,8},{1,9},{2,10},{3,11},{4,12},{5,13},{6,14},{7,15},{8,16},{9,17... | collective-permute-start | bytes 1179656 | tf_op jit(solution)/shard_map/ppermute | solution.py:26
  86.0 31.9 %collective-permute-start.26 = (bf16[4,384,128]{2,1,0:T(8,128)(2,1)S(1)}, bf16[4,384,128]{2,1,0:T(8,128)(2,1)S(1)}, u32[]{:S(2)}, u32[]{:S(2)}) collective-permute-start(bf16[4,384,128]{2,1,0:T(8,128)(2,1)S(1)} %pad_maximum_fusion.1.refs_4_), channel_id=1, source_target_pairs={{0,16},{1,17},{2,18},{3,19},{4,20},{5,21},{6,22},{7,23},{8,24},{9,... | collective-permute-start | bytes 1179656 | tf_op jit(solution)/shard_map/ppermute | solution.py:26
  87.2 31.0 %collective-permute-start.25 = (bf16[4,384,128]{2,1,0:T(8,128)(2,1)S(1)}, bf16[4,384,128]{2,1,0:T(8,128)(2,1)S(1)}, u32[]{:S(2)}, u32[]{:S(2)}) collective-permute-start(bf16[4,384,128]{2,1,0:T(8,128)(2,1)S(1)} %pad_maximum_fusion.1.refs_4_), channel_id=1, source_target_pairs={{0,24},{1,25},{2,26},{3,27},{4,28},{5,29},{6,30},{7,31},{8,0},{9,1... | collective-permute-start | bytes 1179656 | tf_op jit(solution)/shard_map/ppermute | solution.py:26
  88.8 18.2 %collective-permute-start.17 = (bf16[384,128]{1,0:T(8,128)(2,1)S(1)}, bf16[384,128]{1,0:T(8,128)(2,1)S(1)}, u32[]{:S(2)}, u32[]{:S(2)}) collective-permute-start(bf16[384,128]{1,0:T(8,128)(2,1)S(1)} %get-tuple-element.30), channel_id=1, source_target_pairs={{0,16},{1,17},{2,18},{3,19},{4,20},{5,21},{6,22},{7,23},{8,24},{9,... | collective-permute-start | bytes 294920 | tf_op jit(solution)/shard_map/ppermute | solution.py:26
  107.0 5.0 %collective-permute-start.16 = (bf16[384,128]{1,0:T(8,128)(2,1)S(1)}, bf16[384,128]{1,0:T(8,128)(2,1)S(1)}, u32[]{:S(2)}, u32[]{:S(2)}) collective-permute-start(bf16[384,128]{1,0:T(8,128)(2,1)S(1)} %get-tuple-element.30), channel_id=1, source_target_pairs={{0,24},{1,25},{2,26},{3,27},{4,28},{5,29},{6,30},{7,31},{8,0},{9,1... | collective-permute-start | bytes 294920 | tf_op jit(solution)/shard_map/ppermute | solution.py:26
  112.1 7.1 %collective-permute-start.28 = (bf16[4,384,128]{2,1,0:T(8,128)(2,1)S(1)}, bf16[4,384,128]{2,1,0:T(8,128)(2,1)S(1)}, u32[]{:S(2)}, u32[]{:S(2)}) collective-permute-start(bf16[4,384,128]{2,1,0:T(8,128)(2,1)S(1)} %pad_maximum_fusion.refs_0_), channel_id=1, source_target_pairs={{0,1},{1,0},{2,3},{3,2},{4,5},{5,4},{6,7},{7,6},{8,9},{9,8},{10,11... | collective-permute-start | bytes 1179656 | tf_op jit(solution)/shard_map/ppermute | solution.py:26
  114.4 11.9 %collective-permute-start.21 = (bf16[4,384,128]{2,1,0:T(8,128)(2,1)S(1)}, bf16[4,384,128]{2,1,0:T(8,128)(2,1)S(1)}, u32[]{:S(2)}, u32[]{:S(2)}) collective-permute-start(bf16[4,384,128]{2,1,0:T(8,128)(2,1)S(1)} %pad_maximum_fusion.refs_0_), channel_id=1, source_target_pairs={{0,2},{1,3},{2,4},{3,5},{4,6},{5,7},{6,0},{7,1},{8,10},{9,11},{10,... | collective-permute-start | bytes 1179656 | tf_op jit(solution)/shard_map/ppermute | solution.py:26
  115.6 20.0 %collective-permute-start.20 = (bf16[4,384,128]{2,1,0:T(8,128)(2,1)S(1)}, bf16[4,384,128]{2,1,0:T(8,128)(2,1)S(1)}, u32[]{:S(2)}, u32[]{:S(2)}) collective-permute-start(bf16[4,384,128]{2,1,0:T(8,128)(2,1)S(1)} %pad_maximum_fusion.refs_0_), channel_id=1, source_target_pairs={{0,4},{1,5},{2,6},{3,7},{4,0},{5,1},{6,2},{7,3},{8,12},{9,13},{10,... | collective-permute-start | bytes 1179656 | tf_op jit(solution)/shard_map/ppermute | solution.py:26
  118.0 18.5 %collective-permute-start.19 = (bf16[4,384,128]{2,1,0:T(8,128)(2,1)S(1)}, bf16[4,384,128]{2,1,0:T(8,128)(2,1)S(1)}, u32[]{:S(2)}, u32[]{:S(2)}) collective-permute-start(bf16[4,384,128]{2,1,0:T(8,128)(2,1)S(1)} %pad_maximum_fusion.refs_0_), channel_id=1, source_target_pairs={{0,6},{1,7},{2,0},{3,1},{4,2},{5,3},{6,4},{7,5},{8,14},{9,15},{10,... | collective-permute-start | bytes 1179656 | tf_op jit(solution)/shard_map/ppermute | solution.py:26
  118.3 18.2 %collective-permute-start.35 = (bf16[4,384,128]{2,1,0:T(8,128)(2,1)S(1)}, bf16[4,384,128]{2,1,0:T(8,128)(2,1)S(1)}, u32[]{:S(2)}, u32[]{:S(2)}) collective-permute-start(bf16[4,384,128]{2,1,0:T(8,128)(2,1)S(1)} %collective-permute-done.27.refs_7_), channel_id=1, source_target_pairs={{0,1},{1,0},{2,3},{3,2},{4,5},{5,4},{6,7},{7,6},{8,9},{9,8},{10,11... | collective-permute-start | bytes 1179656 | tf_op jit(solution)/shard_map/ppermute | solution.py:26
  119.2 17.8 %collective-permute-start.34 = (bf16[4,384,128]{2,1,0:T(8,128)(2,1)S(1)}, bf16[4,384,128]{2,1,0:T(8,128)(2,1)S(1)}, u32[]{:S(2)}, u32[]{:S(2)}) collective-permute-start(bf16[4,384,128]{2,1,0:T(8,128)(2,1)S(1)} %collective-permute-done.26.refs_6_), channel_id=1, source_target_pairs={{0,1},{1,0},{2,3},{3,2},{4,5},{5,4},{6,7},{7,6},{8,9},{9,8},{10,11... | collective-permute-start | bytes 1179656 | tf_op jit(solution)/shard_map/ppermute | solution.py:26
  126.3 10.7 %collective-permute-start.33 = (bf16[4,384,128]{2,1,0:T(8,128)(2,1)S(1)}, bf16[4,384,128]{2,1,0:T(8,128)(2,1)S(1)}, u32[]{:S(2)}, u32[]{:S(2)}) collective-permute-start(bf16[4,384,128]{2,1,0:T(8,128)(2,1)S(1)} %collective-permute-done.25.refs_5_), channel_id=1, source_target_pairs={{0,1},{1,0},{2,3},{3,2},{4,5},{5,4},{6,7},{7,6},{8,9},{9,8},{10,11... | collective-permute-start | bytes 1179656 | tf_op jit(solution)/shard_map/ppermute | solution.py:26
  135.6 2.2 %collective-permute-start.31 = (bf16[4,384,128]{2,1,0:T(8,128)(2,1)S(1)}, bf16[4,384,128]{2,1,0:T(8,128)(2,1)S(1)}, u32[]{:S(2)}, u32[]{:S(2)}) collective-permute-start(bf16[4,384,128]{2,1,0:T(8,128)(2,1)S(1)} %collective-permute-done.21.refs_3_), channel_id=1, source_target_pairs={{0,1},{1,0},{2,3},{3,2},{4,5},{5,4},{6,7},{7,6},{8,9},{9,8},{10,11... | collective-permute-start | bytes 1179656 | tf_op jit(solution)/shard_map/ppermute | solution.py:26
  136.5 1.9 %collective-permute-start.30 = (bf16[4,384,128]{2,1,0:T(8,128)(2,1)S(1)}, bf16[4,384,128]{2,1,0:T(8,128)(2,1)S(1)}, u32[]{:S(2)}, u32[]{:S(2)}) collective-permute-start(bf16[4,384,128]{2,1,0:T(8,128)(2,1)S(1)} %collective-permute-done.20.refs_2_), channel_id=1, source_target_pairs={{0,1},{1,0},{2,3},{3,2},{4,5},{5,4},{6,7},{7,6},{8,9},{9,8},{10,11... | collective-permute-start | bytes 1179656 | tf_op jit(solution)/shard_map/ppermute | solution.py:26
  136.5 2.5 %copy-start.1 = (bf16[4,384,128]{2,1,0:T(8,128)(2,1)}, bf16[4,384,128]{2,1,0:T(8,128)(2,1)S(1)}, u32[]{:S(2)}) copy-start(bf16[4,384,128]{2,1,0:T(8,128)(2,1)S(1)} %collective-permute-done.35.refs_15_) | copy-start | bytes 1179652
  136.5 2.5 %collective-permute-start.29 = (bf16[4,384,128]{2,1,0:T(8,128)(2,1)S(1)}, bf16[4,384,128]{2,1,0:T(8,128)(2,1)S(1)}, u32[]{:S(2)}, u32[]{:S(2)}) collective-permute-start(bf16[4,384,128]{2,1,0:T(8,128)(2,1)S(1)} %collective-permute-done.19.refs_1_), channel_id=1, source_target_pairs={{0,1},{1,0},{2,3},{3,2},{4,5},{5,4},{6,7},{7,6},{8,9},{9,8},{10,11... | collective-permute-start | bytes 1179656 | tf_op jit(solution)/shard_map/ppermute | solution.py:26

commit v2 on v0

v2 whole, which is shorter than its diff:
```python
import jax
import jax.numpy as jnp
import numpy as np
from jax import lax
from jax.experimental import pallas as pl
from jax.experimental.pallas import tpu as pltpu
from jax.sharding import PartitionSpec as P

PANEL = 512
HALF = 256
LANES = 128
SPOTS = 4
GROUP = 384
F32 = jnp.float32
BF16 = jnp.bfloat16
SIDES = (2, 2, SPOTS, SPOTS, 2)
NAMES = ("grp", "y", "z", "x", "core")


def shifted(array, steps):
    pairs = []
    for source in range(int(np.prod(SIDES))):
        spot = np.unravel_index(source, SIDES)
        step = steps[spot[-1]]
        goal = [(a + step.get(n, 0)) % s for a, n, s in zip(spot, NAMES, SIDES)]
        pairs.append((source, int(np.ravel_multi_index(goal, SIDES))))
    return lax.ppermute(array, ("grp", "rows"), pairs)


def along_first(array, step):
    return shifted(array, ({"x": step}, {"z": step}))


def along_second(array, step):
    return shifted(array, ({"z": step}, {"x": step}))


def to_pair(array):
    return shifted(array, ({"core": 1}, {"core": 1}))


def across(array, step):
    return shifted(array, ({"grp": 1, "y": step},) * 2)


WHOLE = pl.BlockSpec(memory_space=pltpu.VMEM)
TABLE = pl.BlockSpec(memory_space=pltpu.SMEM)
FAR = pl.BlockSpec(memory_space=pltpu.HBM)
LARGE = pltpu.CompilerParams(vmem_limit_bytes=48 << 20)


def place_of(here):
    return here % 2, here // 2 % SPOTS, here // 8 % SPOTS


def group_of(core, x, z, k, m):
    by_x = jnp.where(core == 0, k, m)
    by_z = jnp.where(core == 0, m, k)
    return (x + by_x) % SPOTS * SPOTS + (z + by_z) % SPOTS


def gram_body(here_ref, live_ref, laplace_ref, gap_ref, b_ref, *refs):
    theirs, mine = refs[:SPOTS], refs[SPOTS : 2 * SPOTS]
    f_ref, panel, wide, buffers, sems, wide_sem = refs[2 * SPOTS :]
    core, x, z = place_of(here_ref[0])

    def copies(k, h):
        for i in range(2):
            column = pl.multiple_of(group_of(core, x, z, k, 2 * h + i) * GROUP, LANES)
            source = b_ref.at[:, pl.ds(column, GROUP)]
            yield pltpu.make_async_copy(source, buffers.at[h, :, pl.ds(i * GROUP, GROUP)], sems.at[h, i])

    first = pltpu.make_async_copy(b_ref.at[:, :PANEL], wide, wide_sem)
    first.start()
    for h in range(2):
        for copy in copies(0, h):
            copy.start()

    gap = gap_ref[...]
    moment = 0.15 * jnp.exp(jnp.full(gap.shape, laplace_ref[0], jnp.int32).astype(F32) * np.log(np.float32(1.5)))
    position = lax.broadcasted_iota(jnp.int32, gap.shape, 1)
    factor = jnp.where(position < live_ref[0, 0], jnp.exp(-(gap * moment) * 0.5), 0.0)
    f_ref[...] = jnp.broadcast_to(factor, (LANES, gap.shape[1])).T

    first.wait()
    for half, owner in enumerate((1 - core, core)):
        for c in range(0, HALF, LANES):
            piece = wide[:, pl.ds(pl.multiple_of(owner * HALF + c, LANES), LANES)].astype(F32)
            square = f_ref[...] * f_ref[...]
            panel[:, half * HALF + c : half * HALF + c + LANES] = (piece * square).astype(BF16)

    def some(k, unused):
        for h in range(2):
            for copy in copies(k, h):
                copy.wait()
            product = lax.dot_general(
                buffers[h], panel[...], (((0,), (0,)), ((), ())), preferred_element_type=F32
            ).astype(BF16)
            for i in range(2):
                rows = slice(i * GROUP, (i + 1) * GROUP)
                theirs[2 * h + i][k] = product[rows, :HALF]
                for step in range(SPOTS):

                    @pl.when(k == step)
                    def _():
                        mine[step][2 * h + i] = product[rows, HALF:]

            @pl.when(k + 1 < SPOTS)
            def _():
                for copy in copies(k + 1, h):
                    copy.start()

        return unused

    lax.fori_loop(0, SPOTS, some, 0)


def gram_parts(here, live, laplace, gap, bvals):
    rows = bvals.shape[0]
    part = jax.ShapeDtypeStruct((SPOTS, GROUP, HALF), BF16)
    return pl.pallas_call(
        gram_body,
        in_specs=[TABLE, TABLE, TABLE, WHOLE, FAR],
        out_specs=[WHOLE] * (2 * SPOTS + 1),
        out_shape=[part] * (2 * SPOTS) + [jax.ShapeDtypeStruct((rows, LANES), F32)],
        scratch_shapes=[
            pltpu.VMEM((rows, PANEL), BF16),
            pltpu.VMEM((rows, PANEL), BF16),
            pltpu.VMEM((2, rows, 2 * GROUP), BF16),
            pltpu.SemaphoreType.DMA((2, 2)),
            pltpu.SemaphoreType.DMA,
        ],
        compiler_params=LARGE,
    )(here, live, laplace, gap, bvals)


def panel_body(here_ref, b_ref, f_ref, *refs):
    parts, (out_ref, gram) = refs[:-2], refs[-2:]

    @pl.when(pl.program_id(0) == 0)
    def _():
        core, x, z = place_of(here_ref[0])
        for whose, owner in enumerate((1 - core, core)):
            for k in range(SPOTS):
                for m in range(SPOTS):
                    row = pl.multiple_of(group_of(owner, x, z, k, m) * GROUP, GROUP)
                    column = pl.multiple_of(owner * HALF, HALF)
                    gram[pl.ds(row, GROUP), pl.ds(column, HALF)] = parts[whose * SPOTS + k][m]

    total = jnp.dot(b_ref[...], gram[...], preferred_element_type=F32)
    for c in range(0, PANEL, LANES):
        out_ref[:, c : c + LANES] = (total[:, c : c + LANES] * f_ref[...]).astype(BF16)


def panel_rows(here, bvals, factor, parts):
    rows, aux = bvals.shape
    step = 256
    return pl.pallas_call(
        panel_body,
        grid=(rows // step,),
        in_specs=[
            TABLE,
            pl.BlockSpec((step, aux), lambda s: (s, 0)),
            pl.BlockSpec((step, LANES), lambda s: (s, 0)),
        ]
        + [WHOLE] * len(parts),
        out_specs=pl.BlockSpec((step, PANEL), lambda s: (s, 0)),
        out_shape=jax.ShapeDtypeStruct((rows, PANEL), BF16),
        scratch_shapes=[pltpu.VMEM((aux, PANEL), BF16)],
        compiler_params=LARGE,
    )(here, bvals, factor, *parts)


def total_of(arrays):
    total = arrays[0].astype(F32)
    for array in arrays[1:]:
        total = total + array.astype(F32)
    return total


def on_device(bvals, gap, live, laplace):
    bvals = bvals[0]
    total_rows = bvals.shape[0] * lax.axis_size("rows")
    here = lax.axis_index("rows").reshape(1)
    parts = gram_parts(here, live, laplace, gap, bvals)
    theirs, mine, factor = parts[:SPOTS], parts[SPOTS : 2 * SPOTS], parts[-1]

    pairs = {k: total_of([mine[k], to_pair(theirs[k])]) for k in (2, 1, 3, 0)}
    held = total_of([pairs[0]] + [along_first(pairs[k].astype(BF16), k) for k in (2, 1, 3)])
    share = total_of([held[0]] + [along_second(held[k].astype(BF16), k) for k in (2, 1, 3)]).astype(BF16)
    whole = (total_of([across(share, 0), across(share, 1)]) / total_rows).astype(BF16)
    row = jnp.stack([whole] + [along_second(whole, SPOTS - k) for k in range(1, SPOTS)])
    own = [row] + [along_first(row, SPOTS - k) for k in range(1, SPOTS)]
    return panel_rows(here, bvals, factor, [to_pair(part) for part in own] + own)[None]


def solution(mesh):
    in_specs = (P("grp", "rows", None), P("grp", "rows"), P("grp", "rows"), P())
    out_specs = P("grp", "rows", None)
    return jax.shard_map(
        on_device, mesh=mesh, in_specs=in_specs, out_specs=out_specs, check_vma=False
    )
```

time: 533 us -> 124 us (0.23)
  the two profiles are of different devices: /device:TPU:1 before, /device:TPU:45 now
where the time goes in v2:
time: 124 us
  starting transfers between devices  52.4 us (42%)
  waiting for transfers between devices  36.2 us (29%)
  Pallas kernels  31.3 us (25%)
  other arithmetic  1.43 us (1%)
  between operations  1.4 us (1%)
    ppermute x22, starting transfers between devices, shifted(): return lax.ppermute(array, ('grp', 'rows'), pairs)  52.4 us
    ppermute x22, waiting for transfers between devices, shifted(): return lax.ppermute(array, ('grp', 'rows'), pairs)  36.2 us
    pallas_call x1, Pallas kernels, gram_parts(): pl.pallas_call(gram_body, in_specs=[TABLE, TABLE, TABLE, WHOLE, FAR], out...  16.4 us
    pallas_call x1, Pallas kernels, panel_rows(): pl.pallas_call(panel_body, grid=(rows // step,), in_specs=[TABLE, pl.Bloc...  14.9 us
  transfers between devices with their start and end apart: 22, of which 13 were waited for; matrix products, arithmetic and copies ran while one was open for 0% of the time, Pallas kernels for 0%

profile of v2, /device:TPU:45, one launch (start us, length us, event | category | flops | bytes accessed | tf_op | source)
XLA Modules:
  0.0 123.5 jit_solution(12426385771639848311)
XLA Ops:
  1.3 0.0 copy-start.1
  1.3 0.7 copy-done.1
  2.0 16.4 %shard_map.46 = (bf16[4,384,256]{2,1,0:T(8,128)(2,1)S(1)}, bf16[4,384,256]{2,1,0:T(8,128)(2,1)S(1)}, bf16[4,384,256]{2,1,0:T(8,128)(2,1)S(1)}, bf16[4,384,256]{2...) custom-call(s32[1]{0:T(128)} %bitcast.here_ref, ...), custom_call_target="tpu_custom_call" | custom-call | tf_op jit(solution)/shard_map/pallas_call | solution.py:121
  18.4 0.8 collective-permute-start.1
  19.1 0.1 collective-permute-start.3
  19.2 0.4 collective-permute-start.5
  19.6 0.1 collective-permute-start
  19.7 1.3 %collective-permute-done.1 = bf16[4,384,256]{2,1,0:T(8,128)(2,1)S(1)} collective-permute-done((bf16[4,384,256]{2,1,0:T(8,128)(2,1)S(1)}, bf16[4,384,256]{2,1,0:T(8,128)(2,1)S(1)}, u32[]{:S(2)}, u32[]{:S(2)}) %collective-permute-start.1) | collective-permute-done | bytes 786464 | tf_op jit(solution)/shard_map/ppermute | solution.py:27
  21.0 0.2 add_convert_fusion.2
  21.2 0.0 copy-start.4
  21.3 2.8 %collective-permute-start.2 = (bf16[4,384,256]{2,1,0:T(8,128)(2,1)S(1)}, bf16[4,384,256]{2,1,0:T(8,128)(2,1)S(1)}, u32[]{:S(2)}, u32[]{:S(2)}) collective-permute-start(bf16[4,384,256]{2,1,0:T(8,128)(2,1)S(1)} %add_convert_fusion.2), channel_id=1, source_target_pairs={{0,4},{1,17},{2,6},{3,19},{4,0},{5,21},{6,2},{7,23},{8,12},{9,25},... | collective-permute-start | bytes 2359304 | tf_op jit(solution)/shard_map/ppermute | solution.py:27
  24.0 0.0 collective-permute-done.3
  24.0 0.2 add_convert_fusion.1
  24.3 0.1 collective-permute-start.4
  24.3 0.0 collective-permute-done.5
  24.3 0.0 copy-done.4
  24.4 0.2 add_convert_fusion
  24.6 1.5 %collective-permute-start.6 = (bf16[4,384,256]{2,1,0:T(8,128)(2,1)S(1)}, bf16[4,384,256]{2,1,0:T(8,128)(2,1)S(1)}, u32[]{:S(2)}, u32[]{:S(2)}) collective-permute-start(bf16[4,384,256]{2,1,0:T(8,128)(2,1)S(1)} %add_convert_fusion), channel_id=1, source_target_pairs={{0,6},{1,25},{2,0},{3,27},{4,2},{5,29},{6,4},{7,31},{8,14},{9,1},{... | collective-permute-start | bytes 2359304 | tf_op jit(solution)/shard_map/ppermute | solution.py:27
  26.1 0.0 collective-permute-done
  26.1 7.9 %collective-permute-done.2 = bf16[4,384,256]{2,1,0:T(8,128)(2,1)S(1)} collective-permute-done((bf16[4,384,256]{2,1,0:T(8,128)(2,1)S(1)}, bf16[4,384,256]{2,1,0:T(8,128)(2,1)S(1)}, u32[]{:S(2)}, u32[]{:S(2)}) %collective-permute-start.2) | collective-permute-done | bytes 786464 | tf_op jit(solution)/shard_map/ppermute | solution.py:27
  34.0 8.8 %collective-permute-done.4 = bf16[4,384,256]{2,1,0:T(8,128)(2,1)S(1)} collective-permute-done((bf16[4,384,256]{2,1,0:T(8,128)(2,1)S(1)}, bf16[4,384,256]{2,1,0:T(8,128)(2,1)S(1)}, u32[]{:S(2)}, u32[]{:S(2)}) %collective-permute-start.4) | collective-permute-done | bytes 786464 | tf_op jit(solution)/shard_map/ppermute | solution.py:27
  42.8 0.0 collective-permute-done.6
  42.8 0.6 fusion.4
  43.5 0.4 collective-permute-start.7
  43.8 1.9 %collective-permute-start.9 = (bf16[384,256]{1,0:T(8,128)(2,1)S(1)}, bf16[384,256]{1,0:T(8,128)(2,1)S(1)}, u32[]{:S(2)}, u32[]{:S(2)}) collective-permute-start(bf16[384,256]{1,0:T(8,128)(2,1)S(1)} %get-tuple-element.26), channel_id=1, source_target_pairs={{0,24},{1,7},{2,26},{3,1},{4,28},{5,3},{6,30},{7,5},{8,0},{9,15},{... | collective-permute-start | bytes 589832 | tf_op jit(solution)/shard_map/ppermute | solution.py:27
  45.7 0.0 collective-permute-start.8
  45.7 4.2 %collective-permute-done.7 = bf16[384,256]{1,0:T(8,128)(2,1)S(1)} collective-permute-done((bf16[384,256]{1,0:T(8,128)(2,1)S(1)}, bf16[384,256]{1,0:T(8,128)(2,1)S(1)}, u32[]{:S(2)}, u32[]{:S(2)}) %collective-permute-start.7) | collective-permute-done | bytes 196640 | tf_op jit(solution)/shard_map/ppermute | solution.py:27
  49.9 1.3 %collective-permute-done.9 = bf16[384,256]{1,0:T(8,128)(2,1)S(1)} collective-permute-done((bf16[384,256]{1,0:T(8,128)(2,1)S(1)}, bf16[384,256]{1,0:T(8,128)(2,1)S(1)}, u32[]{:S(2)}, u32[]{:S(2)}) %collective-permute-start.9) | collective-permute-done | bytes 196640 | tf_op jit(solution)/shard_map/ppermute | solution.py:27
  51.1 0.8 collective-permute-done.8
  52.0 0.0 copy-start
  52.0 0.1 fusion.3
  52.1 1.4 %collective-permute-start.11 = (bf16[384,256]{1,0:T(8,128)(2,1)S(1)}, bf16[384,256]{1,0:T(8,128)(2,1)S(1)}, u32[]{:S(2)}, u32[]{:S(2)}) collective-permute-start(bf16[384,256]{1,0:T(8,128)(2,1)S(1)} %fusion.3), channel_id=1, source_target_pairs={{0,96},{1,97},{2,98},{3,99},{4,100},{5,101},{6,102},{7,103},{8,104... | collective-permute-start | bytes 589832 | tf_op jit(solution)/shard_map/ppermute | solution.py:27
  53.4 0.8 collective-permute-start.10
  54.2 4.0 %collective-permute-done.11 = bf16[384,256]{1,0:T(8,128)(2,1)S(1)} collective-permute-done((bf16[384,256]{1,0:T(8,128)(2,1)S(1)}, bf16[384,256]{1,0:T(8,128)(2,1)S(1)}, u32[]{:S(2)}, u32[]{:S(2)}) %collective-permute-start.11) | collective-permute-done | bytes 196640 | tf_op jit(solution)/shard_map/ppermute | solution.py:27
  58.3 1.3 %collective-permute-done.10 = bf16[384,256]{1,0:T(8,128)(2,1)S(1)} collective-permute-done((bf16[384,256]{1,0:T(8,128)(2,1)S(1)}, bf16[384,256]{1,0:T(8,128)(2,1)S(1)}, u32[]{:S(2)}, u32[]{:S(2)}) %collective-permute-start.10) | collective-permute-done | bytes 196640 | tf_op jit(solution)/shard_map/ppermute | solution.py:27
  59.6 0.1 multiply_convert_fusion
  59.6 0.8 collective-permute-start.14
  60.4 1.5 %collective-permute-start.13 = (bf16[384,256]{1,0:T(8,128)(2,1)S(1)}, bf16[384,256]{1,0:T(8,128)(2,1)S(1)}, u32[]{:S(2)}, u32[]{:S(2)}) collective-permute-start(bf16[384,256]{1,0:T(8,128)(2,1)S(1)} %multiply_convert_fusion), channel_id=1, source_target_pairs={{0,16},{1,5},{2,18},{3,7},{4,20},{5,1},{6,22},{7,3},{8,24},{9,13},... | collective-permute-start | bytes 589832 | tf_op jit(solution)/shard_map/ppermute | solution.py:27
  61.9 2.0 %collective-permute-start.12 = (bf16[384,256]{1,0:T(8,128)(2,1)S(1)}, bf16[384,256]{1,0:T(8,128)(2,1)S(1)}, u32[]{:S(2)}, u32[]{:S(2)}) collective-permute-start(bf16[384,256]{1,0:T(8,128)(2,1)S(1)} %multiply_convert_fusion), channel_id=1, source_target_pairs={{0,24},{1,7},{2,26},{3,1},{4,28},{5,3},{6,30},{7,5},{8,0},{9,15},{... | collective-permute-start | bytes 589832 | tf_op jit(solution)/shard_map/ppermute | solution.py:27
  63.9 0.3 collective-permute-done.14
  64.2 2.8 %collective-permute-done.13 = bf16[384,256]{1,0:T(8,128)(2,1)S(1)} collective-permute-done((bf16[384,256]{1,0:T(8,128)(2,1)S(1)}, bf16[384,256]{1,0:T(8,128)(2,1)S(1)}, u32[]{:S(2)}, u32[]{:S(2)}) %collective-permute-start.13) | collective-permute-done | bytes 196640 | tf_op jit(solution)/shard_map/ppermute | solution.py:27
  67.0 1.4 %collective-permute-done.12 = bf16[384,256]{1,0:T(8,128)(2,1)S(1)} collective-permute-done((bf16[384,256]{1,0:T(8,128)(2,1)S(1)}, bf16[384,256]{1,0:T(8,128)(2,1)S(1)}, u32[]{:S(2)}, u32[]{:S(2)}) %collective-permute-start.12) | collective-permute-done | bytes 196640 | tf_op jit(solution)/shard_map/ppermute | solution.py:27
  68.4 0.1 pad_maximum_fusion.refs_4_
  68.5 1.1 collective-permute-start.20
  69.6 1.0 collective-permute-start.18
  70.6 2.0 %collective-permute-start.16 = (bf16[4,384,256]{2,1,0:T(8,128)(2,1)S(1)}, bf16[4,384,256]{2,1,0:T(8,128)(2,1)S(1)}, u32[]{:S(2)}, u32[]{:S(2)}) collective-permute-start(bf16[4,384,256]{2,1,0:T(8,128)(2,1)S(1)} %pad_maximum_fusion.refs_4_), channel_id=1, source_target_pairs={{0,6},{1,25},{2,0},{3,27},{4,2},{5,29},{6,4},{7,31},{8,14},{9,1},{... | collective-permute-start | bytes 2359304 | tf_op jit(solution)/shard_map/ppermute | solution.py:27
  72.6 13.4 %collective-permute-start.15 = (bf16[4,384,256]{2,1,0:T(8,128)(2,1)S(1)}, bf16[4,384,256]{2,1,0:T(8,128)(2,1)S(1)}, u32[]{:S(2)}, u32[]{:S(2)}) collective-permute-start(bf16[4,384,256]{2,1,0:T(8,128)(2,1)S(1)} %pad_maximum_fusion.refs_4_), channel_id=1, source_target_pairs={{0,1},{1,0},{2,3},{3,2},{4,5},{5,4},{6,7},{7,6},{8,9},{9,8},{10,11... | collective-permute-start | bytes 2359304 | tf_op jit(solution)/shard_map/ppermute | solution.py:27
  86.0 0.0 collective-permute-done.20.refs_7_
  86.0 0.0 copy-start.2
  86.0 18.4 %collective-permute-start.21 = (bf16[4,384,256]{2,1,0:T(8,128)(2,1)S(1)}, bf16[4,384,256]{2,1,0:T(8,128)(2,1)S(1)}, u32[]{:S(2)}, u32[]{:S(2)}) collective-permute-start(bf16[4,384,256]{2,1,0:T(8,128)(2,1)S(1)} %collective-permute-done.20.refs_7_), channel_id=1, source_target_pairs={{0,1},{1,0},{2,3},{3,2},{4,5},{5,4},{6,7},{7,6},{8,9},{9,8},{10,11... | collective-permute-start | bytes 2359304 | tf_op jit(solution)/shard_map/ppermute | solution.py:27
  104.4 0.0 collective-permute-done.18.refs_6_
  104.4 0.0 copy-start.3
  104.4 0.1 collective-permute-start.19
  104.5 0.0 collective-permute-done.16.refs_5_
  104.5 2.0 %collective-permute-start.17 = (bf16[4,384,256]{2,1,0:T(8,128)(2,1)S(1)}, bf16[4,384,256]{2,1,0:T(8,128)(2,1)S(1)}, u32[]{:S(2)}, u32[]{:S(2)}) collective-permute-start(bf16[4,384,256]{2,1,0:T(8,128)(2,1)S(1)} %collective-permute-done.16.refs_5_), channel_id=1, source_target_pairs={{0,1},{1,0},{2,3},{3,2},{4,5},{5,4},{6,7},{7,6},{8,9},{9,8},{10,11... | collective-permute-start | bytes 2359304 | tf_op jit(solution)/shard_map/ppermute | solution.py:27
  106.5 0.0 collective-permute-done.15.refs_0_
  106.5 0.0 collective-permute-done.21.refs_3_
  106.5 0.9 collective-permute-done.19.refs_2_
  107.5 1.1 collective-permute-done.17.refs_1_
  108.6 0.0 copy-done.2
  108.6 0.0 copy-done.3
  108.6 0.0 copy-done
  108.6 14.9 %shard_map.47 = bf16[1536,512]{1,0:T(8,128)(2,1)} custom-call(s32[1]{0:T(128)} %bitcast.here_ref, bf16[1536,6144]{1,0:T(8,128)(2,1)} %bitcast.24, f32[1536,128]{1,0:T(8,128)S(1)} %copy-done, bf16[4,384,256]{2,1,0:T(8,128)(2,1)S(1)} %collective-permute-done.15.refs_0_, bf16[4,384,256]{2,1,0:T(8,128)(2,1)S(1)} %collective-permute-done.17.refs_1_, ...), custom_call_target="tpu_custom_call" | custom-call | tf_op jit(solution)/shard_map/pallas_call | solution.py:158
  (1 shorter events, 0.0 us)
Async XLA Ops:
  1.3 0.7 copy-start.1
  18.4 2.7 %collective-permute-start.1 = (bf16[4,384,256]{2,1,0:T(8,128)(2,1)S(1)}, bf16[4,384,256]{2,1,0:T(8,128)(2,1)S(1)}, u32[]{:S(2)}, u32[]{:S(2)}) collective-permute-start(bf16[4,384,256]{2,1,0:T(8,128)(2,1)S(1)} %get-tuple-element.18), channel_id=1, source_target_pairs={{0,1},{1,0},{2,3},{3,2},{4,5},{5,4},{6,7},{7,6},{8,9},{9,8},{10,11... | collective-permute-start | bytes 2359304 | tf_op jit(solution)/shard_map/ppermute | solution.py:27
  19.1 4.9 %collective-permute-start.3 = (bf16[4,384,256]{2,1,0:T(8,128)(2,1)S(1)}, bf16[4,384,256]{2,1,0:T(8,128)(2,1)S(1)}, u32[]{:S(2)}, u32[]{:S(2)}) collective-permute-start(bf16[4,384,256]{2,1,0:T(8,128)(2,1)S(1)} %get-tuple-element.20), channel_id=1, source_target_pairs={{0,1},{1,0},{2,3},{3,2},{4,5},{5,4},{6,7},{7,6},{8,9},{9,8},{10,11... | collective-permute-start | bytes 2359304 | tf_op jit(solution)/shard_map/ppermute | solution.py:27
  19.2 5.1 %collective-permute-start.5 = (bf16[4,384,256]{2,1,0:T(8,128)(2,1)S(1)}, bf16[4,384,256]{2,1,0:T(8,128)(2,1)S(1)}, u32[]{:S(2)}, u32[]{:S(2)}) collective-permute-start(bf16[4,384,256]{2,1,0:T(8,128)(2,1)S(1)} %get-tuple-element.22), channel_id=1, source_target_pairs={{0,1},{1,0},{2,3},{3,2},{4,5},{5,4},{6,7},{7,6},{8,9},{9,8},{10,11... | collective-permute-start | bytes 2359304 | tf_op jit(solution)/shard_map/ppermute | solution.py:27
  19.6 6.4 %collective-permute-start = (bf16[4,384,256]{2,1,0:T(8,128)(2,1)S(1)}, bf16[4,384,256]{2,1,0:T(8,128)(2,1)S(1)}, u32[]{:S(2)}, u32[]{:S(2)}) collective-permute-start(bf16[4,384,256]{2,1,0:T(8,128)(2,1)S(1)} %get-tuple-element.16), channel_id=1, source_target_pairs={{0,1},{1,0},{2,3},{3,2},{4,5},{5,4},{6,7},{7,6},{8,9},{9,8},{10,11... | collective-permute-start | bytes 2359304 | tf_op jit(solution)/shard_map/ppermute | solution.py:27
  21.2 3.1 %copy-start.4 = (bf16[4,384,256]{2,1,0:T(8,128)(2,1)S(1)}, bf16[4,384,256]{2,1,0:T(8,128)(2,1)}, u32[]{:S(2)}) copy-start(bf16[4,384,256]{2,1,0:T(8,128)(2,1)} %get-tuple-element.21) | copy-start | bytes 2359300
  21.3 12.8 %collective-permute-start.2 = (bf16[4,384,256]{2,1,0:T(8,128)(2,1)S(1)}, bf16[4,384,256]{2,1,0:T(8,128)(2,1)S(1)}, u32[]{:S(2)}, u32[]{:S(2)}) collective-permute-start(bf16[4,384,256]{2,1,0:T(8,128)(2,1)S(1)} %add_convert_fusion.2), channel_id=1, source_target_pairs={{0,4},{1,17},{2,6},{3,19},{4,0},{5,21},{6,2},{7,23},{8,12},{9,25},... | collective-permute-start | bytes 2359304 | tf_op jit(solution)/shard_map/ppermute | solution.py:27
  24.3 18.6 %collective-permute-start.4 = (bf16[4,384,256]{2,1,0:T(8,128)(2,1)S(1)}, bf16[4,384,256]{2,1,0:T(8,128)(2,1)S(1)}, u32[]{:S(2)}, u32[]{:S(2)}) collective-permute-start(bf16[4,384,256]{2,1,0:T(8,128)(2,1)S(1)} %add_convert_fusion.1), channel_id=1, source_target_pairs={{0,2},{1,9},{2,4},{3,11},{4,6},{5,13},{6,0},{7,15},{8,10},{9,17},{... | collective-permute-start | bytes 2359304 | tf_op jit(solution)/shard_map/ppermute | solution.py:27
  24.6 18.3 %collective-permute-start.6 = (bf16[4,384,256]{2,1,0:T(8,128)(2,1)S(1)}, bf16[4,384,256]{2,1,0:T(8,128)(2,1)S(1)}, u32[]{:S(2)}, u32[]{:S(2)}) collective-permute-start(bf16[4,384,256]{2,1,0:T(8,128)(2,1)S(1)} %add_convert_fusion), channel_id=1, source_target_pairs={{0,6},{1,25},{2,0},{3,27},{4,2},{5,29},{6,4},{7,31},{8,14},{9,1},{... | collective-permute-start | bytes 2359304 | tf_op jit(solution)/shard_map/ppermute | solution.py:27
  43.5 6.4 %collective-permute-start.7 = (bf16[384,256]{1,0:T(8,128)(2,1)S(1)}, bf16[384,256]{1,0:T(8,128)(2,1)S(1)}, u32[]{:S(2)}, u32[]{:S(2)}) collective-permute-start(bf16[384,256]{1,0:T(8,128)(2,1)S(1)} %get-tuple-element.25), channel_id=1, source_target_pairs={{0,16},{1,5},{2,18},{3,7},{4,20},{5,1},{6,22},{7,3},{8,24},{9,13},... | collective-permute-start | bytes 589832 | tf_op jit(solution)/shard_map/ppermute | solution.py:27
  43.8 7.3 %collective-permute-start.9 = (bf16[384,256]{1,0:T(8,128)(2,1)S(1)}, bf16[384,256]{1,0:T(8,128)(2,1)S(1)}, u32[]{:S(2)}, u32[]{:S(2)}) collective-permute-start(bf16[384,256]{1,0:T(8,128)(2,1)S(1)} %get-tuple-element.26), channel_id=1, source_target_pairs={{0,24},{1,7},{2,26},{3,1},{4,28},{5,3},{6,30},{7,5},{8,0},{9,15},{... | collective-permute-start | bytes 589832 | tf_op jit(solution)/shard_map/ppermute | solution.py:27
  45.7 6.3 %collective-permute-start.8 = (bf16[384,256]{1,0:T(8,128)(2,1)S(1)}, bf16[384,256]{1,0:T(8,128)(2,1)S(1)}, u32[]{:S(2)}, u32[]{:S(2)}) collective-permute-start(bf16[384,256]{1,0:T(8,128)(2,1)S(1)} %get-tuple-element.27), channel_id=1, source_target_pairs={{0,8},{1,3},{2,10},{3,5},{4,12},{5,7},{6,14},{7,1},{8,16},{9,11},{... | collective-permute-start | bytes 589832 | tf_op jit(solution)/shard_map/ppermute | solution.py:27
  52.0 56.6 %copy-start = (f32[1536,128]{1,0:T(8,128)S(1)}, f32[1536,128]{1,0:T(8,128)}, u32[]{:S(2)}) copy-start(f32[1536,128]{1,0:T(8,128)} %get-tuple-element.14.f_ref) | copy-start | bytes 2359300
  52.1 6.2 %collective-permute-start.11 = (bf16[384,256]{1,0:T(8,128)(2,1)S(1)}, bf16[384,256]{1,0:T(8,128)(2,1)S(1)}, u32[]{:S(2)}, u32[]{:S(2)}) collective-permute-start(bf16[384,256]{1,0:T(8,128)(2,1)S(1)} %fusion.3), channel_id=1, source_target_pairs={{0,96},{1,97},{2,98},{3,99},{4,100},{5,101},{6,102},{7,103},{8,104... | collective-permute-start | bytes 589832 | tf_op jit(solution)/shard_map/ppermute | solution.py:27
  53.4 6.1 %collective-permute-start.10 = (bf16[384,256]{1,0:T(8,128)(2,1)S(1)}, bf16[384,256]{1,0:T(8,128)(2,1)S(1)}, u32[]{:S(2)}, u32[]{:S(2)}) collective-permute-start(bf16[384,256]{1,0:T(8,128)(2,1)S(1)} %fusion.3), channel_id=1, source_target_pairs={{0,64},{1,65},{2,66},{3,67},{4,68},{5,69},{6,70},{7,71},{8,72},{9,... | collective-permute-start | bytes 589832 | tf_op jit(solution)/shard_map/ppermute | solution.py:27
  59.6 4.6 %collective-permute-start.14 = (bf16[384,256]{1,0:T(8,128)(2,1)S(1)}, bf16[384,256]{1,0:T(8,128)(2,1)S(1)}, u32[]{:S(2)}, u32[]{:S(2)}) collective-permute-start(bf16[384,256]{1,0:T(8,128)(2,1)S(1)} %multiply_convert_fusion), channel_id=1, source_target_pairs={{0,8},{1,3},{2,10},{3,5},{4,12},{5,7},{6,14},{7,1},{8,16},{9,11},{... | collective-permute-start | bytes 589832 | tf_op jit(solution)/shard_map/ppermute | solution.py:27
  60.4 6.6 %collective-permute-start.13 = (bf16[384,256]{1,0:T(8,128)(2,1)S(1)}, bf16[384,256]{1,0:T(8,128)(2,1)S(1)}, u32[]{:S(2)}, u32[]{:S(2)}) collective-permute-start(bf16[384,256]{1,0:T(8,128)(2,1)S(1)} %multiply_convert_fusion), channel_id=1, source_target_pairs={{0,16},{1,5},{2,18},{3,7},{4,20},{5,1},{6,22},{7,3},{8,24},{9,13},... | collective-permute-start | bytes 589832 | tf_op jit(solution)/shard_map/ppermute | solution.py:27
  61.9 6.5 %collective-permute-start.12 = (bf16[384,256]{1,0:T(8,128)(2,1)S(1)}, bf16[384,256]{1,0:T(8,128)(2,1)S(1)}, u32[]{:S(2)}, u32[]{:S(2)}) collective-permute-start(bf16[384,256]{1,0:T(8,128)(2,1)S(1)} %multiply_convert_fusion), channel_id=1, source_target_pairs={{0,24},{1,7},{2,26},{3,1},{4,28},{5,3},{6,30},{7,5},{8,0},{9,15},{... | collective-permute-start | bytes 589832 | tf_op jit(solution)/shard_map/ppermute | solution.py:27
  68.5 17.5 %collective-permute-start.20 = (bf16[4,384,256]{2,1,0:T(8,128)(2,1)S(1)}, bf16[4,384,256]{2,1,0:T(8,128)(2,1)S(1)}, u32[]{:S(2)}, u32[]{:S(2)}) collective-permute-start(bf16[4,384,256]{2,1,0:T(8,128)(2,1)S(1)} %pad_maximum_fusion.refs_4_), channel_id=1, source_target_pairs={{0,2},{1,9},{2,4},{3,11},{4,6},{5,13},{6,0},{7,15},{8,10},{9,17},{... | collective-permute-start | bytes 2359304 | tf_op jit(solution)/shard_map/ppermute | solution.py:27
  69.6 34.8 %collective-permute-start.18 = (bf16[4,384,256]{2,1,0:T(8,128)(2,1)S(1)}, bf16[4,384,256]{2,1,0:T(8,128)(2,1)S(1)}, u32[]{:S(2)}, u32[]{:S(2)}) collective-permute-start(bf16[4,384,256]{2,1,0:T(8,128)(2,1)S(1)} %pad_maximum_fusion.refs_4_), channel_id=1, source_target_pairs={{0,4},{1,17},{2,6},{3,19},{4,0},{5,21},{6,2},{7,23},{8,12},{9,25},... | collective-permute-start | bytes 2359304 | tf_op jit(solution)/shard_map/ppermute | solution.py:27
  70.6 33.9 %collective-permute-start.16 = (bf16[4,384,256]{2,1,0:T(8,128)(2,1)S(1)}, bf16[4,384,256]{2,1,0:T(8,128)(2,1)S(1)}, u32[]{:S(2)}, u32[]{:S(2)}) collective-permute-start(bf16[4,384,256]{2,1,0:T(8,128)(2,1)S(1)} %pad_maximum_fusion.refs_4_), channel_id=1, source_target_pairs={{0,6},{1,25},{2,0},{3,27},{4,2},{5,29},{6,4},{7,31},{8,14},{9,1},{... | collective-permute-start | bytes 2359304 | tf_op jit(solution)/shard_map/ppermute | solution.py:27
  72.6 33.9 %collective-permute-start.15 = (bf16[4,384,256]{2,1,0:T(8,128)(2,1)S(1)}, bf16[4,384,256]{2,1,0:T(8,128)(2,1)S(1)}, u32[]{:S(2)}, u32[]{:S(2)}) collective-permute-start(bf16[4,384,256]{2,1,0:T(8,128)(2,1)S(1)} %pad_maximum_fusion.refs_4_), channel_id=1, source_target_pairs={{0,1},{1,0},{2,3},{3,2},{4,5},{5,4},{6,7},{7,6},{8,9},{9,8},{10,11... | collective-permute-start | bytes 2359304 | tf_op jit(solution)/shard_map/ppermute | solution.py:27
  86.0 22.6 %copy-start.2 = (bf16[4,384,256]{2,1,0:T(8,128)(2,1)}, bf16[4,384,256]{2,1,0:T(8,128)(2,1)S(1)}, u32[]{:S(2)}) copy-start(bf16[4,384,256]{2,1,0:T(8,128)(2,1)S(1)} %collective-permute-done.20.refs_7_) | copy-start | bytes 2359300
  86.0 20.5 %collective-permute-start.21 = (bf16[4,384,256]{2,1,0:T(8,128)(2,1)S(1)}, bf16[4,384,256]{2,1,0:T(8,128)(2,1)S(1)}, u32[]{:S(2)}, u32[]{:S(2)}) collective-permute-start(bf16[4,384,256]{2,1,0:T(8,128)(2,1)S(1)} %collective-permute-done.20.refs_7_), channel_id=1, source_target_pairs={{0,1},{1,0},{2,3},{3,2},{4,5},{5,4},{6,7},{7,6},{8,9},{9,8},{10,11... | collective-permute-start | bytes 2359304 | tf_op jit(solution)/shard_map/ppermute | solution.py:27
  104.4 4.2 %copy-start.3 = (bf16[4,384,256]{2,1,0:T(8,128)(2,1)}, bf16[4,384,256]{2,1,0:T(8,128)(2,1)S(1)}, u32[]{:S(2)}) copy-start(bf16[4,384,256]{2,1,0:T(8,128)(2,1)S(1)} %collective-permute-done.18.refs_6_) | copy-start | bytes 2359300
  104.4 3.0 %collective-permute-start.19 = (bf16[4,384,256]{2,1,0:T(8,128)(2,1)S(1)}, bf16[4,384,256]{2,1,0:T(8,128)(2,1)S(1)}, u32[]{:S(2)}, u32[]{:S(2)}) collective-permute-start(bf16[4,384,256]{2,1,0:T(8,128)(2,1)S(1)} %collective-permute-done.18.refs_6_), channel_id=1, source_target_pairs={{0,1},{1,0},{2,3},{3,2},{4,5},{5,4},{6,7},{7,6},{8,9},{9,8},{10,11... | collective-permute-start | bytes 2359304 | tf_op jit(solution)/shard_map/ppermute | solution.py:27
  104.5 4.1 %collective-permute-start.17 = (bf16[4,384,256]{2,1,0:T(8,128)(2,1)S(1)}, bf16[4,384,256]{2,1,0:T(8,128)(2,1)S(1)}, u32[]{:S(2)}, u32[]{:S(2)}) collective-permute-start(bf16[4,384,256]{2,1,0:T(8,128)(2,1)S(1)} %collective-permute-done.16.refs_5_), channel_id=1, source_target_pairs={{0,1},{1,0},{2,3},{3,2},{4,5},{5,4},{6,7},{7,6},{8,9},{9,8},{10,11... | collective-permute-start | bytes 2359304 | tf_op jit(solution)/shard_map/ppermute | solution.py:27

commit v3 on v2

v3 whole, which is shorter than its diff:
```python
import jax
import jax.numpy as jnp
import numpy as np
from jax import lax
from jax.experimental import pallas as pl
from jax.experimental.pallas import tpu as pltpu
from jax.sharding import PartitionSpec as P

PANEL = 512
HALF = 256
LANES = 128
SPOTS = 4
GROUP = 384
F32 = jnp.float32
BF16 = jnp.bfloat16
SIDES = (2, 2, SPOTS, SPOTS, 2)
NAMES = ("grp", "y", "z", "x", "core")


def shifted(array, steps):
    pairs = []
    for source in range(int(np.prod(SIDES))):
        spot = np.unravel_index(source, SIDES)
        step = steps[spot[-1]]
        goal = [(a + step.get(n, 0)) % s for a, n, s in zip(spot, NAMES, SIDES)]
        pairs.append((source, int(np.ravel_multi_index(goal, SIDES))))
    return lax.ppermute(array, ("grp", "rows"), pairs)


def along_first(array, step):
    return shifted(array, ({"x": step}, {"z": step}))


def along_second(array, step):
    return shifted(array, ({"z": step}, {"x": step}))


def to_pair(array):
    return shifted(array, ({"core": 1}, {"core": 1}))


def across(array, step):
    return shifted(array, ({"grp": 1, "y": step},) * 2)


WHOLE = pl.BlockSpec(memory_space=pltpu.VMEM)
TABLE = pl.BlockSpec(memory_space=pltpu.SMEM)
FAR = pl.BlockSpec(memory_space=pltpu.HBM)
LARGE = pltpu.CompilerParams(vmem_limit_bytes=48 << 20)


def place_of(here):
    return here % 2, here // 2 % SPOTS, here // 8 % SPOTS


def group_of(core, x, z, k, m):
    by_x = jnp.where(core == 0, k, m)
    by_z = jnp.where(core == 0, m, k)
    return (x + by_x) % SPOTS * SPOTS + (z + by_z) % SPOTS


SPANS = ((0, 1), (1, 2), (2, 4), (4, 8), (8, 12), (12, 16))
AHEAD = 3


def gram_body(here_ref, live_ref, laplace_ref, gap_ref, b_ref, *refs):
    theirs, mine = refs[:SPOTS], refs[SPOTS : 2 * SPOTS]
    f_ref, panel, wide, gap_row, sems, wide_sem, gap_sem, *buffers = refs[2 * SPOTS :]
    core, x, z = place_of(here_ref[0])

    def copies(span):
        for spot in range(*SPANS[span]):
            column = pl.multiple_of(group_of(core, x, z, spot // SPOTS, spot % SPOTS) * GROUP, LANES)
            source = b_ref.at[:, pl.ds(column, GROUP)]
            place = (spot - SPANS[span][0]) * GROUP
            yield pltpu.make_async_copy(source, buffers[span].at[:, pl.ds(place, GROUP)], sems.at[spot])

    gap_copy = pltpu.make_async_copy(gap_ref, gap_row, gap_sem)
    gap_copy.start()
    first = pltpu.make_async_copy(b_ref.at[:, :PANEL], wide, wide_sem)
    first.start()
    for span in range(AHEAD):
        for copy in copies(span):
            copy.start()

    gap_copy.wait()
    gap = gap_row[...]
    moment = 0.15 * jnp.exp(jnp.full(gap.shape, laplace_ref[0], jnp.int32).astype(F32) * np.log(np.float32(1.5)))
    position = lax.broadcasted_iota(jnp.int32, gap.shape, 1)
    factor = jnp.where(position < live_ref[0, 0], jnp.exp(-(gap * moment) * 0.5), 0.0)
    f_ref[...] = jnp.broadcast_to(factor, (LANES, gap.shape[1])).T

    first.wait()
    for half, owner in enumerate((1 - core, core)):
        for c in range(0, HALF, LANES):
            piece = wide[:, pl.ds(pl.multiple_of(owner * HALF + c, LANES), LANES)].astype(F32)
            square = f_ref[...] * f_ref[...]
            panel[:, half * HALF + c : half * HALF + c + LANES] = (piece * square).astype(BF16)

    for span, (start, end) in enumerate(SPANS):
        for copy in copies(span):
            copy.wait()
        if span + AHEAD < len(SPANS):
            for copy in copies(span + AHEAD):
                copy.start()
        product = lax.dot_general(
            buffers[span][...], panel[...], (((0,), (0,)), ((), ())), preferred_element_type=F32
        ).astype(BF16)
        for spot in range(start, end):
            k, m = spot // SPOTS, spot % SPOTS
            rows = slice((spot - start) * GROUP, (spot - start + 1) * GROUP)
            theirs[m][k] = product[rows, :HALF]
            mine[k][m] = product[rows, HALF:]


def gram_parts(here, live, laplace, gap, bvals):
    rows = bvals.shape[0]
    part = jax.ShapeDtypeStruct((SPOTS, GROUP, HALF), BF16)
    return pl.pallas_call(
        gram_body,
        in_specs=[TABLE, TABLE, TABLE, FAR, FAR],
        out_specs=[WHOLE] * (2 * SPOTS + 1),
        out_shape=[part] * (2 * SPOTS) + [jax.ShapeDtypeStruct((rows, LANES), F32)],
        scratch_shapes=[
            pltpu.VMEM((rows, PANEL), BF16),
            pltpu.VMEM((rows, PANEL), BF16),
            pltpu.VMEM((1, rows), F32),
            pltpu.SemaphoreType.DMA((SPOTS * SPOTS,)),
            pltpu.SemaphoreType.DMA,
            pltpu.SemaphoreType.DMA,
        ]
        + [pltpu.VMEM((rows, (end - start) * GROUP), BF16) for start, end in SPANS],
        compiler_params=LARGE,
    )(here, live, laplace, gap, bvals)


BLOCKS = ((0, 128), (128, 384), (384, 768), (768, 1280), (1280, 1536))


def panel_body(here_ref, f_ref, b_ref, *refs):
    parts, (out_ref, gram, result, sems, out_sems, *buffers) = refs[: 4 * SPOTS // 2], refs[4 * SPOTS // 2 :]

    def copy(block):
        start, end = BLOCKS[block]
        return pltpu.make_async_copy(b_ref.at[pl.ds(start, end - start)], buffers[block], sems.at[block])

    def copy_out(block):
        start, end = BLOCKS[block]
        part = pl.ds(start, end - start)
        return pltpu.make_async_copy(result.at[part], out_ref.at[part], out_sems.at[block])

    for block in range(2):
        copy(block).start()
    core, x, z = place_of(here_ref[0])
    for whose, owner in enumerate((1 - core, core)):
        for k in range(SPOTS):
            for m in range(SPOTS):
                row = pl.multiple_of(group_of(owner, x, z, k, m) * GROUP, GROUP)
                column = pl.multiple_of(owner * HALF, HALF)
                gram[pl.ds(row, GROUP), pl.ds(column, HALF)] = parts[whose * SPOTS + k][m]
    for block, (start, end) in enumerate(BLOCKS):
        copy(block).wait()
        if block + 2 < len(BLOCKS):
            copy(block + 2).start()
        total = jnp.dot(buffers[block][...], gram[...], preferred_element_type=F32)
        for c in range(0, PANEL, LANES):
            result[start:end, c : c + LANES] = (total[:, c : c + LANES] * f_ref[start:end]).astype(BF16)
        copy_out(block).start()
    for block in range(len(BLOCKS)):
        copy_out(block).wait()


def panel_rows(here, bvals, factor, parts):
    rows, aux = bvals.shape
    return pl.pallas_call(
        panel_body,
        in_specs=[TABLE, WHOLE, FAR] + [WHOLE] * len(parts),
        out_specs=FAR,
        out_shape=jax.ShapeDtypeStruct((rows, PANEL), BF16),
        scratch_shapes=[
            pltpu.VMEM((aux, PANEL), BF16),
            pltpu.VMEM((rows, PANEL), BF16),
            pltpu.SemaphoreType.DMA((len(BLOCKS),)),
            pltpu.SemaphoreType.DMA((len(BLOCKS),)),
        ]
        + [pltpu.VMEM((end - start, aux), BF16) for start, end in BLOCKS],
        compiler_params=LARGE,
    )(here, factor, bvals, *parts)


def total_of(arrays):
    total = arrays[0].astype(F32)
    for array in arrays[1:]:
        total = total + array.astype(F32)
    return total


def on_device(bvals, gap, live, laplace):
    bvals = bvals[0]
    total_rows = bvals.shape[0] * lax.axis_size("rows")
    here = lax.axis_index("rows").reshape(1)
    parts = gram_parts(here, live, laplace, gap, bvals)
    theirs, mine, factor = parts[:SPOTS], parts[SPOTS : 2 * SPOTS], parts[-1]

    pairs = {k: total_of([mine[k], to_pair(theirs[k])]) for k in (1, 3, 2, 0)}
    held = total_of([pairs[0]] + [along_first(pairs[k].astype(BF16), k) for k in (1, 3, 2)])
    share = total_of([held[0]] + [along_second(held[k].astype(BF16), k) for k in (1, 3, 2)]).astype(BF16)
    whole = (total_of([across(share, 1), across(share, 0)]) / total_rows).astype(BF16)
    rows = {k: along_second(whole, SPOTS - k) for k in (1, 3, 2)}
    row = jnp.stack([whole] + [rows[k] for k in range(1, SPOTS)])
    own = {0: row, **{k: along_first(row, SPOTS - k) for k in (1, 3, 2)}}
    other = {k: to_pair(own[k]) for k in (0, 1, 3, 2)}
    parts = [other[k] for k in range(SPOTS)] + [own[k] for k in range(SPOTS)]
    return panel_rows(here, bvals, factor, parts)[None]


def solution(mesh):
    in_specs = (P("grp", "rows", None), P("grp", "rows"), P("grp", "rows"), P())
    out_specs = P("grp", "rows", None)
    return jax.shard_map(
        on_device, mesh=mesh, in_specs=in_specs, out_specs=out_specs, check_vma=False
    )
```

time: 124 us -> 117 us (0.944)
  the two profiles are of different devices: /device:TPU:45 before, /device:TPU:1 now
where the time goes in v3:
time: 117 us
  waiting for transfers between devices  48.4 us (41%)
  starting transfers between devices  35.8 us (31%)
  Pallas kernels  29.4 us (25%)
  between operations  1.54 us (1%)
  other arithmetic  1.41 us (1%)
    ppermute x22, waiting for transfers between devices, shifted(): return lax.ppermute(array, ('grp', 'rows'), pairs)  48.4 us
    ppermute x22, starting transfers between devices, shifted(): return lax.ppermute(array, ('grp', 'rows'), pairs)  35.8 us
    pallas_call x1, Pallas kernels, gram_parts(): pl.pallas_call(gram_body, in_specs=[TABLE, TABLE, TABLE, FAR, FAR], out_s...  14.8 us
    pallas_call x1, Pallas kernels, panel_rows(): pl.pallas_call(panel_body, in_specs=[TABLE, WHOLE, FAR] + [WHOLE] * len(p...  14.6 us
  transfers between devices with their start and end apart: 22, of which 15 were waited for; matrix products, arithmetic and copies ran while one was open for 1% of the time, Pallas kernels for 0%

profile of v3, /device:TPU:1, one launch (start us, length us, event | category | flops | bytes accessed | tf_op | source)
XLA Modules:
  0.0 117.3 jit_solution(12979392038348178342)
XLA Ops:
  1.3 0.0 copy-start.1
  1.3 0.7 copy-done.1
  2.0 14.8 %shard_map.46 = (bf16[4,384,256]{2,1,0:T(8,128)(2,1)S(1)}, bf16[4,384,256]{2,1,0:T(8,128)(2,1)S(1)}, bf16[4,384,256]{2,1,0:T(8,128)(2,1)S(1)}, bf16[4,384,256]{2...) custom-call(s32[1]{0:T(128)} %bitcast.here_ref, ...), custom_call_target="tpu_custom_call" | custom-call | tf_op jit(solution)/shard_map/pallas_call | solution.py:119
  16.8 0.0 copy-start.4
  16.8 1.5 %collective-permute-start.1 = (bf16[4,384,256]{2,1,0:T(8,128)(2,1)S(1)}, bf16[4,384,256]{2,1,0:T(8,128)(2,1)S(1)}, u32[]{:S(2)}, u32[]{:S(2)}) collective-permute-start(bf16[4,384,256]{2,1,0:T(8,128)(2,1)S(1)} %get-tuple-element.18), channel_id=1, source_target_pairs={{0,1},{1,0},{2,3},{3,2},{4,5},{5,4},{6,7},{7,6},{8,9},{9,8},{10,11... | collective-permute-start | bytes 2359304 | tf_op jit(solution)/shard_map/ppermute | solution.py:27
  18.3 0.1 collective-permute-start.3
  18.4 0.4 collective-permute-start.5
  18.8 0.1 collective-permute-start
  18.9 1.3 %collective-permute-done.1 = bf16[4,384,256]{2,1,0:T(8,128)(2,1)S(1)} collective-permute-done((bf16[4,384,256]{2,1,0:T(8,128)(2,1)S(1)}, bf16[4,384,256]{2,1,0:T(8,128)(2,1)S(1)}, u32[]{:S(2)}, u32[]{:S(2)}) %collective-permute-start.1) | collective-permute-done | bytes 786464 | tf_op jit(solution)/shard_map/ppermute | solution.py:27
  20.2 0.2 add_convert_fusion.2
  20.4 1.8 %collective-permute-start.2 = (bf16[4,384,256]{2,1,0:T(8,128)(2,1)S(1)}, bf16[4,384,256]{2,1,0:T(8,128)(2,1)S(1)}, u32[]{:S(2)}, u32[]{:S(2)}) collective-permute-start(bf16[4,384,256]{2,1,0:T(8,128)(2,1)S(1)} %add_convert_fusion.2), channel_id=1, source_target_pairs={{0,2},{1,9},{2,4},{3,11},{4,6},{5,13},{6,0},{7,15},{8,10},{9,17},{... | collective-permute-start | bytes 2359304 | tf_op jit(solution)/shard_map/ppermute | solution.py:27
  22.2 0.0 collective-permute-done.3
  22.2 0.0 copy-done.4
  22.2 0.2 add_convert_fusion.1
  22.4 3.0 %collective-permute-start.4 = (bf16[4,384,256]{2,1,0:T(8,128)(2,1)S(1)}, bf16[4,384,256]{2,1,0:T(8,128)(2,1)S(1)}, u32[]{:S(2)}, u32[]{:S(2)}) collective-permute-start(bf16[4,384,256]{2,1,0:T(8,128)(2,1)S(1)} %add_convert_fusion.1), channel_id=1, source_target_pairs={{0,6},{1,25},{2,0},{3,27},{4,2},{5,29},{6,4},{7,31},{8,14},{9,1},{... | collective-permute-start | bytes 2359304 | tf_op jit(solution)/shard_map/ppermute | solution.py:27
  25.4 0.0 collective-permute-done.5
  25.4 0.2 add_convert_fusion
  25.6 1.0 collective-permute-start.6
  26.6 0.0 collective-permute-done
  26.6 7.1 %collective-permute-done.2 = bf16[4,384,256]{2,1,0:T(8,128)(2,1)S(1)} collective-permute-done((bf16[4,384,256]{2,1,0:T(8,128)(2,1)S(1)}, bf16[4,384,256]{2,1,0:T(8,128)(2,1)S(1)}, u32[]{:S(2)}, u32[]{:S(2)}) %collective-permute-start.2) | collective-permute-done | bytes 786464 | tf_op jit(solution)/shard_map/ppermute | solution.py:27
  33.7 9.1 %collective-permute-done.4 = bf16[4,384,256]{2,1,0:T(8,128)(2,1)S(1)} collective-permute-done((bf16[4,384,256]{2,1,0:T(8,128)(2,1)S(1)}, bf16[4,384,256]{2,1,0:T(8,128)(2,1)S(1)}, u32[]{:S(2)}, u32[]{:S(2)}) %collective-permute-start.4) | collective-permute-done | bytes 786464 | tf_op jit(solution)/shard_map/ppermute | solution.py:27
  42.8 0.5 collective-permute-done.6
  43.3 0.6 fusion.4
  43.9 1.3 %collective-permute-start.7 = (bf16[384,256]{1,0:T(8,128)(2,1)S(1)}, bf16[384,256]{1,0:T(8,128)(2,1)S(1)}, u32[]{:S(2)}, u32[]{:S(2)}) collective-permute-start(bf16[384,256]{1,0:T(8,128)(2,1)S(1)} %get-tuple-element.25), channel_id=1, source_target_pairs={{0,8},{1,3},{2,10},{3,5},{4,12},{5,7},{6,14},{7,1},{8,16},{9,11},{... | collective-permute-start | bytes 589832 | tf_op jit(solution)/shard_map/ppermute | solution.py:27
  45.2 2.4 %collective-permute-start.9 = (bf16[384,256]{1,0:T(8,128)(2,1)S(1)}, bf16[384,256]{1,0:T(8,128)(2,1)S(1)}, u32[]{:S(2)}, u32[]{:S(2)}) collective-permute-start(bf16[384,256]{1,0:T(8,128)(2,1)S(1)} %get-tuple-element.26), channel_id=1, source_target_pairs={{0,16},{1,5},{2,18},{3,7},{4,20},{5,1},{6,22},{7,3},{8,24},{9,13},... | collective-permute-start | bytes 589832 | tf_op jit(solution)/shard_map/ppermute | solution.py:27
  47.6 1.2 collective-permute-start.8
  48.8 1.2 %collective-permute-done.7 = bf16[384,256]{1,0:T(8,128)(2,1)S(1)} collective-permute-done((bf16[384,256]{1,0:T(8,128)(2,1)S(1)}, bf16[384,256]{1,0:T(8,128)(2,1)S(1)}, u32[]{:S(2)}, u32[]{:S(2)}) %collective-permute-start.7) | collective-permute-done | bytes 196640 | tf_op jit(solution)/shard_map/ppermute | solution.py:27
  50.0 3.1 %collective-permute-done.9 = bf16[384,256]{1,0:T(8,128)(2,1)S(1)} collective-permute-done((bf16[384,256]{1,0:T(8,128)(2,1)S(1)}, bf16[384,256]{1,0:T(8,128)(2,1)S(1)}, u32[]{:S(2)}, u32[]{:S(2)}) %collective-permute-start.9) | collective-permute-done | bytes 196640 | tf_op jit(solution)/shard_map/ppermute | solution.py:27
  53.1 0.0 collective-permute-done.8
  53.1 0.0 copy-start
  53.1 0.1 fusion.3
  53.2 3.0 %collective-permute-start.11 = (bf16[384,256]{1,0:T(8,128)(2,1)S(1)}, bf16[384,256]{1,0:T(8,128)(2,1)S(1)}, u32[]{:S(2)}, u32[]{:S(2)}) collective-permute-start(bf16[384,256]{1,0:T(8,128)(2,1)S(1)} %fusion.3), channel_id=1, source_target_pairs={{0,64},{1,65},{2,66},{3,67},{4,68},{5,69},{6,70},{7,71},{8,72},{9,... | collective-permute-start | bytes 589832 | tf_op jit(solution)/shard_map/ppermute | solution.py:27
  56.2 0.8 collective-permute-start.10
  57.0 2.3 %collective-permute-done.11 = bf16[384,256]{1,0:T(8,128)(2,1)S(1)} collective-permute-done((bf16[384,256]{1,0:T(8,128)(2,1)S(1)}, bf16[384,256]{1,0:T(8,128)(2,1)S(1)}, u32[]{:S(2)}, u32[]{:S(2)}) %collective-permute-start.11) | collective-permute-done | bytes 196640 | tf_op jit(solution)/shard_map/ppermute | solution.py:27
  59.3 6.1 %collective-permute-done.10 = bf16[384,256]{1,0:T(8,128)(2,1)S(1)} collective-permute-done((bf16[384,256]{1,0:T(8,128)(2,1)S(1)}, bf16[384,256]{1,0:T(8,128)(2,1)S(1)}, u32[]{:S(2)}, u32[]{:S(2)}) %collective-permute-start.10) | collective-permute-done | bytes 196640 | tf_op jit(solution)/shard_map/ppermute | solution.py:27
  65.4 0.1 multiply_convert_fusion
  65.4 0.2 collective-permute-start.14
  65.6 2.8 %collective-permute-start.13 = (bf16[384,256]{1,0:T(8,128)(2,1)S(1)}, bf16[384,256]{1,0:T(8,128)(2,1)S(1)}, u32[]{:S(2)}, u32[]{:S(2)}) collective-permute-start(bf16[384,256]{1,0:T(8,128)(2,1)S(1)} %multiply_convert_fusion), channel_id=1, source_target_pairs={{0,16},{1,5},{2,18},{3,7},{4,20},{5,1},{6,22},{7,3},{8,24},{9,13},... | collective-permute-start | bytes 589832 | tf_op jit(solution)/shard_map/ppermute | solution.py:27
  68.4 2.0 %collective-permute-start.12 = (bf16[384,256]{1,0:T(8,128)(2,1)S(1)}, bf16[384,256]{1,0:T(8,128)(2,1)S(1)}, u32[]{:S(2)}, u32[]{:S(2)}) collective-permute-start(bf16[384,256]{1,0:T(8,128)(2,1)S(1)} %multiply_convert_fusion), channel_id=1, source_target_pairs={{0,24},{1,7},{2,26},{3,1},{4,28},{5,3},{6,30},{7,5},{8,0},{9,15},{... | collective-permute-start | bytes 589832 | tf_op jit(solution)/shard_map/ppermute | solution.py:27
  70.4 1.1 collective-permute-done.14
  71.5 2.0 %collective-permute-done.13 = bf16[384,256]{1,0:T(8,128)(2,1)S(1)} collective-permute-done((bf16[384,256]{1,0:T(8,128)(2,1)S(1)}, bf16[384,256]{1,0:T(8,128)(2,1)S(1)}, u32[]{:S(2)}, u32[]{:S(2)}) %collective-permute-start.13) | collective-permute-done | bytes 196640 | tf_op jit(solution)/shard_map/ppermute | solution.py:27
  73.5 0.7 collective-permute-done.12
  74.2 0.1 pad_maximum_fusion.refs_4_
  74.3 1.1 collective-permute-start.20
  75.4 2.7 %collective-permute-start.18 = (bf16[4,384,256]{2,1,0:T(8,128)(2,1)S(1)}, bf16[4,384,256]{2,1,0:T(8,128)(2,1)S(1)}, u32[]{:S(2)}, u32[]{:S(2)}) collective-permute-start(bf16[4,384,256]{2,1,0:T(8,128)(2,1)S(1)} %pad_maximum_fusion.refs_4_), channel_id=1, source_target_pairs={{0,4},{1,17},{2,6},{3,19},{4,0},{5,21},{6,2},{7,23},{8,12},{9,25},... | collective-permute-start | bytes 2359304 | tf_op jit(solution)/shard_map/ppermute | solution.py:27
  78.1 0.0 collective-permute-start.16
  78.1 3.7 %collective-permute-start.15 = (bf16[4,384,256]{2,1,0:T(8,128)(2,1)S(1)}, bf16[4,384,256]{2,1,0:T(8,128)(2,1)S(1)}, u32[]{:S(2)}, u32[]{:S(2)}) collective-permute-start(bf16[4,384,256]{2,1,0:T(8,128)(2,1)S(1)} %pad_maximum_fusion.refs_4_), channel_id=1, source_target_pairs={{0,1},{1,0},{2,3},{3,2},{4,5},{5,4},{6,7},{7,6},{8,9},{9,8},{10,11... | collective-permute-start | bytes 2359304 | tf_op jit(solution)/shard_map/ppermute | solution.py:27
  81.8 4.9 %collective-permute-done.20.refs_7_ = bf16[4,384,256]{2,1,0:T(8,128)(2,1)S(1)} collective-permute-done((bf16[4,384,256]{2,1,0:T(8,128)(2,1)S(1)}, bf16[4,384,256]{2,1,0:T(8,128)(2,1)S(1)}, u32[]{:S(2)}, u32[]{:S(2)}) %collective-permute-start.20) | collective-permute-done | bytes 786464 | tf_op jit(solution)/shard_map/ppermute | solution.py:27
  86.7 0.0 copy-start.2
  86.7 3.5 %collective-permute-start.21 = (bf16[4,384,256]{2,1,0:T(8,128)(2,1)S(1)}, bf16[4,384,256]{2,1,0:T(8,128)(2,1)S(1)}, u32[]{:S(2)}, u32[]{:S(2)}) collective-permute-start(bf16[4,384,256]{2,1,0:T(8,128)(2,1)S(1)} %collective-permute-done.20.refs_7_), channel_id=1, source_target_pairs={{0,1},{1,0},{2,3},{3,2},{4,5},{5,4},{6,7},{7,6},{8,9},{9,8},{10,11... | collective-permute-start | bytes 2359304 | tf_op jit(solution)/shard_map/ppermute | solution.py:27
  90.2 6.0 %collective-permute-done.18.refs_6_ = bf16[4,384,256]{2,1,0:T(8,128)(2,1)S(1)} collective-permute-done((bf16[4,384,256]{2,1,0:T(8,128)(2,1)S(1)}, bf16[4,384,256]{2,1,0:T(8,128)(2,1)S(1)}, u32[]{:S(2)}, u32[]{:S(2)}) %collective-permute-start.18) | collective-permute-done | bytes 786464 | tf_op jit(solution)/shard_map/ppermute | solution.py:27
  96.2 0.0 copy-start.3
  96.2 3.3 %collective-permute-start.19 = (bf16[4,384,256]{2,1,0:T(8,128)(2,1)S(1)}, bf16[4,384,256]{2,1,0:T(8,128)(2,1)S(1)}, u32[]{:S(2)}, u32[]{:S(2)}) collective-permute-start(bf16[4,384,256]{2,1,0:T(8,128)(2,1)S(1)} %collective-permute-done.18.refs_6_), channel_id=1, source_target_pairs={{0,1},{1,0},{2,3},{3,2},{4,5},{5,4},{6,7},{7,6},{8,9},{9,8},{10,11... | collective-permute-start | bytes 2359304 | tf_op jit(solution)/shard_map/ppermute | solution.py:27
  99.5 0.0 collective-permute-done.16.refs_5_
  99.5 0.1 collective-permute-start.17
  99.6 0.0 collective-permute-done.15.refs_0_
  99.6 0.0 collective-permute-done.21.refs_3_
  99.6 1.8 %collective-permute-done.19.refs_2_ = bf16[4,384,256]{2,1,0:T(8,128)(2,1)S(1)} collective-permute-done((bf16[4,384,256]{2,1,0:T(8,128)(2,1)S(1)}, bf16[4,384,256]{2,1,0:T(8,128)(2,1)S(1)}, u32[]{:S(2)}, u32[]{:S(2)}) %collective-permute-start.19) | collective-permute-done | bytes 786464 | tf_op jit(solution)/shard_map/ppermute | solution.py:27
  101.4 1.1 collective-permute-done.17.refs_1_
  102.5 0.0 copy-done.2
  102.5 0.0 copy-done.3
  102.5 0.0 copy-done
  102.5 14.6 %shard_map.47 = bf16[1536,512]{1,0:T(8,128)(2,1)} custom-call(s32[1]{0:T(128)} %bitcast.here_ref, f32[1536,128]{1,0:T(8,128)S(1)} %copy-done, bf16[1536,6144]{1,0:T(8,128)(2,1)} %bitcast.24, bf16[4,384,256]{2,1,0:T(8,128)(2,1)S(1)} %collective-permute-done.15.refs_0_, bf16[4,384,256]{2,1,0:T(8,128)(2,1)S(1)} %collective-permute-done.17.refs_1_, ...), custom_call_target="tpu_custom_call" | custom-call | tf_op jit(solution)/shard_map/pallas_call | solution.py:175
  (1 shorter events, 0.0 us)
Async XLA Ops:
  1.3 0.7 copy-start.1
  16.8 5.4 %copy-start.4 = (bf16[4,384,256]{2,1,0:T(8,128)(2,1)S(1)}, bf16[4,384,256]{2,1,0:T(8,128)(2,1)}, u32[]{:S(2)}) copy-start(bf16[4,384,256]{2,1,0:T(8,128)(2,1)} %get-tuple-element.19) | copy-start | bytes 2359300
  16.8 3.4 %collective-permute-start.1 = (bf16[4,384,256]{2,1,0:T(8,128)(2,1)S(1)}, bf16[4,384,256]{2,1,0:T(8,128)(2,1)S(1)}, u32[]{:S(2)}, u32[]{:S(2)}) collective-permute-start(bf16[4,384,256]{2,1,0:T(8,128)(2,1)S(1)} %get-tuple-element.18), channel_id=1, source_target_pairs={{0,1},{1,0},{2,3},{3,2},{4,5},{5,4},{6,7},{7,6},{8,9},{9,8},{10,11... | collective-permute-start | bytes 2359304 | tf_op jit(solution)/shard_map/ppermute | solution.py:27
  18.3 3.9 %collective-permute-start.3 = (bf16[4,384,256]{2,1,0:T(8,128)(2,1)S(1)}, bf16[4,384,256]{2,1,0:T(8,128)(2,1)S(1)}, u32[]{:S(2)}, u32[]{:S(2)}) collective-permute-start(bf16[4,384,256]{2,1,0:T(8,128)(2,1)S(1)} %get-tuple-element.20), channel_id=1, source_target_pairs={{0,1},{1,0},{2,3},{3,2},{4,5},{5,4},{6,7},{7,6},{8,9},{9,8},{10,11... | collective-permute-start | bytes 2359304 | tf_op jit(solution)/shard_map/ppermute | solution.py:27
  18.4 7.1 %collective-permute-start.5 = (bf16[4,384,256]{2,1,0:T(8,128)(2,1)S(1)}, bf16[4,384,256]{2,1,0:T(8,128)(2,1)S(1)}, u32[]{:S(2)}, u32[]{:S(2)}) collective-permute-start(bf16[4,384,256]{2,1,0:T(8,128)(2,1)S(1)} %get-tuple-element.22), channel_id=1, source_target_pairs={{0,1},{1,0},{2,3},{3,2},{4,5},{5,4},{6,7},{7,6},{8,9},{9,8},{10,11... | collective-permute-start | bytes 2359304 | tf_op jit(solution)/shard_map/ppermute | solution.py:27
  18.8 7.8 %collective-permute-start = (bf16[4,384,256]{2,1,0:T(8,128)(2,1)S(1)}, bf16[4,384,256]{2,1,0:T(8,128)(2,1)S(1)}, u32[]{:S(2)}, u32[]{:S(2)}) collective-permute-start(bf16[4,384,256]{2,1,0:T(8,128)(2,1)S(1)} %get-tuple-element.16), channel_id=1, source_target_pairs={{0,1},{1,0},{2,3},{3,2},{4,5},{5,4},{6,7},{7,6},{8,9},{9,8},{10,11... | collective-permute-start | bytes 2359304 | tf_op jit(solution)/shard_map/ppermute | solution.py:27
  20.4 13.3 %collective-permute-start.2 = (bf16[4,384,256]{2,1,0:T(8,128)(2,1)S(1)}, bf16[4,384,256]{2,1,0:T(8,128)(2,1)S(1)}, u32[]{:S(2)}, u32[]{:S(2)}) collective-permute-start(bf16[4,384,256]{2,1,0:T(8,128)(2,1)S(1)} %add_convert_fusion.2), channel_id=1, source_target_pairs={{0,2},{1,9},{2,4},{3,11},{4,6},{5,13},{6,0},{7,15},{8,10},{9,17},{... | collective-permute-start | bytes 2359304 | tf_op jit(solution)/shard_map/ppermute | solution.py:27
  22.4 20.4 %collective-permute-start.4 = (bf16[4,384,256]{2,1,0:T(8,128)(2,1)S(1)}, bf16[4,384,256]{2,1,0:T(8,128)(2,1)S(1)}, u32[]{:S(2)}, u32[]{:S(2)}) collective-permute-start(bf16[4,384,256]{2,1,0:T(8,128)(2,1)S(1)} %add_convert_fusion.1), channel_id=1, source_target_pairs={{0,6},{1,25},{2,0},{3,27},{4,2},{5,29},{6,4},{7,31},{8,14},{9,1},{... | collective-permute-start | bytes 2359304 | tf_op jit(solution)/shard_map/ppermute | solution.py:27
  25.6 17.7 %collective-permute-start.6 = (bf16[4,384,256]{2,1,0:T(8,128)(2,1)S(1)}, bf16[4,384,256]{2,1,0:T(8,128)(2,1)S(1)}, u32[]{:S(2)}, u32[]{:S(2)}) collective-permute-start(bf16[4,384,256]{2,1,0:T(8,128)(2,1)S(1)} %add_convert_fusion), channel_id=1, source_target_pairs={{0,4},{1,17},{2,6},{3,19},{4,0},{5,21},{6,2},{7,23},{8,12},{9,25},... | collective-permute-start | bytes 2359304 | tf_op jit(solution)/shard_map/ppermute | solution.py:27
  43.9 6.1 %collective-permute-start.7 = (bf16[384,256]{1,0:T(8,128)(2,1)S(1)}, bf16[384,256]{1,0:T(8,128)(2,1)S(1)}, u32[]{:S(2)}, u32[]{:S(2)}) collective-permute-start(bf16[384,256]{1,0:T(8,128)(2,1)S(1)} %get-tuple-element.25), channel_id=1, source_target_pairs={{0,8},{1,3},{2,10},{3,5},{4,12},{5,7},{6,14},{7,1},{8,16},{9,11},{... | collective-permute-start | bytes 589832 | tf_op jit(solution)/shard_map/ppermute | solution.py:27
  45.2 7.9 %collective-permute-start.9 = (bf16[384,256]{1,0:T(8,128)(2,1)S(1)}, bf16[384,256]{1,0:T(8,128)(2,1)S(1)}, u32[]{:S(2)}, u32[]{:S(2)}) collective-permute-start(bf16[384,256]{1,0:T(8,128)(2,1)S(1)} %get-tuple-element.26), channel_id=1, source_target_pairs={{0,16},{1,5},{2,18},{3,7},{4,20},{5,1},{6,22},{7,3},{8,24},{9,13},... | collective-permute-start | bytes 589832 | tf_op jit(solution)/shard_map/ppermute | solution.py:27
  47.6 5.5 %collective-permute-start.8 = (bf16[384,256]{1,0:T(8,128)(2,1)S(1)}, bf16[384,256]{1,0:T(8,128)(2,1)S(1)}, u32[]{:S(2)}, u32[]{:S(2)}) collective-permute-start(bf16[384,256]{1,0:T(8,128)(2,1)S(1)} %get-tuple-element.27), channel_id=1, source_target_pairs={{0,24},{1,7},{2,26},{3,1},{4,28},{5,3},{6,30},{7,5},{8,0},{9,15},{... | collective-permute-start | bytes 589832 | tf_op jit(solution)/shard_map/ppermute | solution.py:27
  53.1 49.4 %copy-start = (f32[1536,128]{1,0:T(8,128)S(1)}, f32[1536,128]{1,0:T(8,128)}, u32[]{:S(2)}) copy-start(f32[1536,128]{1,0:T(8,128)} %get-tuple-element.14.f_ref) | copy-start | bytes 2359300
  53.2 6.1 %collective-permute-start.11 = (bf16[384,256]{1,0:T(8,128)(2,1)S(1)}, bf16[384,256]{1,0:T(8,128)(2,1)S(1)}, u32[]{:S(2)}, u32[]{:S(2)}) collective-permute-start(bf16[384,256]{1,0:T(8,128)(2,1)S(1)} %fusion.3), channel_id=1, source_target_pairs={{0,64},{1,65},{2,66},{3,67},{4,68},{5,69},{6,70},{7,71},{8,72},{9,... | collective-permute-start | bytes 589832 | tf_op jit(solution)/shard_map/ppermute | solution.py:27
  56.2 9.2 %collective-permute-start.10 = (bf16[384,256]{1,0:T(8,128)(2,1)S(1)}, bf16[384,256]{1,0:T(8,128)(2,1)S(1)}, u32[]{:S(2)}, u32[]{:S(2)}) collective-permute-start(bf16[384,256]{1,0:T(8,128)(2,1)S(1)} %fusion.3), channel_id=1, source_target_pairs={{0,96},{1,97},{2,98},{3,99},{4,100},{5,101},{6,102},{7,103},{8,104... | collective-permute-start | bytes 589832 | tf_op jit(solution)/shard_map/ppermute | solution.py:27
  65.4 6.1 %collective-permute-start.14 = (bf16[384,256]{1,0:T(8,128)(2,1)S(1)}, bf16[384,256]{1,0:T(8,128)(2,1)S(1)}, u32[]{:S(2)}, u32[]{:S(2)}) collective-permute-start(bf16[384,256]{1,0:T(8,128)(2,1)S(1)} %multiply_convert_fusion), channel_id=1, source_target_pairs={{0,8},{1,3},{2,10},{3,5},{4,12},{5,7},{6,14},{7,1},{8,16},{9,11},{... | collective-permute-start | bytes 589832 | tf_op jit(solution)/shard_map/ppermute | solution.py:27
  65.6 7.9 %collective-permute-start.13 = (bf16[384,256]{1,0:T(8,128)(2,1)S(1)}, bf16[384,256]{1,0:T(8,128)(2,1)S(1)}, u32[]{:S(2)}, u32[]{:S(2)}) collective-permute-start(bf16[384,256]{1,0:T(8,128)(2,1)S(1)} %multiply_convert_fusion), channel_id=1, source_target_pairs={{0,16},{1,5},{2,18},{3,7},{4,20},{5,1},{6,22},{7,3},{8,24},{9,13},... | collective-permute-start | bytes 589832 | tf_op jit(solution)/shard_map/ppermute | solution.py:27
  68.4 5.8 %collective-permute-start.12 = (bf16[384,256]{1,0:T(8,128)(2,1)S(1)}, bf16[384,256]{1,0:T(8,128)(2,1)S(1)}, u32[]{:S(2)}, u32[]{:S(2)}) collective-permute-start(bf16[384,256]{1,0:T(8,128)(2,1)S(1)} %multiply_convert_fusion), channel_id=1, source_target_pairs={{0,24},{1,7},{2,26},{3,1},{4,28},{5,3},{6,30},{7,5},{8,0},{9,15},{... | collective-permute-start | bytes 589832 | tf_op jit(solution)/shard_map/ppermute | solution.py:27
  74.3 12.4 %collective-permute-start.20 = (bf16[4,384,256]{2,1,0:T(8,128)(2,1)S(1)}, bf16[4,384,256]{2,1,0:T(8,128)(2,1)S(1)}, u32[]{:S(2)}, u32[]{:S(2)}) collective-permute-start(bf16[4,384,256]{2,1,0:T(8,128)(2,1)S(1)} %pad_maximum_fusion.refs_4_), channel_id=1, source_target_pairs={{0,2},{1,9},{2,4},{3,11},{4,6},{5,13},{6,0},{7,15},{8,10},{9,17},{... | collective-permute-start | bytes 2359304 | tf_op jit(solution)/shard_map/ppermute | solution.py:27
  75.4 20.8 %collective-permute-start.18 = (bf16[4,384,256]{2,1,0:T(8,128)(2,1)S(1)}, bf16[4,384,256]{2,1,0:T(8,128)(2,1)S(1)}, u32[]{:S(2)}, u32[]{:S(2)}) collective-permute-start(bf16[4,384,256]{2,1,0:T(8,128)(2,1)S(1)} %pad_maximum_fusion.refs_4_), channel_id=1, source_target_pairs={{0,4},{1,17},{2,6},{3,19},{4,0},{5,21},{6,2},{7,23},{8,12},{9,25},... | collective-permute-start | bytes 2359304 | tf_op jit(solution)/shard_map/ppermute | solution.py:27
  78.1 21.4 %collective-permute-start.16 = (bf16[4,384,256]{2,1,0:T(8,128)(2,1)S(1)}, bf16[4,384,256]{2,1,0:T(8,128)(2,1)S(1)}, u32[]{:S(2)}, u32[]{:S(2)}) collective-permute-start(bf16[4,384,256]{2,1,0:T(8,128)(2,1)S(1)} %pad_maximum_fusion.refs_4_), channel_id=1, source_target_pairs={{0,6},{1,25},{2,0},{3,27},{4,2},{5,29},{6,4},{7,31},{8,14},{9,1},{... | collective-permute-start | bytes 2359304 | tf_op jit(solution)/shard_map/ppermute | solution.py:27
  78.1 21.5 %collective-permute-start.15 = (bf16[4,384,256]{2,1,0:T(8,128)(2,1)S(1)}, bf16[4,384,256]{2,1,0:T(8,128)(2,1)S(1)}, u32[]{:S(2)}, u32[]{:S(2)}) collective-permute-start(bf16[4,384,256]{2,1,0:T(8,128)(2,1)S(1)} %pad_maximum_fusion.refs_4_), channel_id=1, source_target_pairs={{0,1},{1,0},{2,3},{3,2},{4,5},{5,4},{6,7},{7,6},{8,9},{9,8},{10,11... | collective-permute-start | bytes 2359304 | tf_op jit(solution)/shard_map/ppermute | solution.py:27
  86.7 15.8 %copy-start.2 = (bf16[4,384,256]{2,1,0:T(8,128)(2,1)}, bf16[4,384,256]{2,1,0:T(8,128)(2,1)S(1)}, u32[]{:S(2)}) copy-start(bf16[4,384,256]{2,1,0:T(8,128)(2,1)S(1)} %collective-permute-done.20.refs_7_) | copy-start | bytes 2359300
  86.7 12.8 %collective-permute-start.21 = (bf16[4,384,256]{2,1,0:T(8,128)(2,1)S(1)}, bf16[4,384,256]{2,1,0:T(8,128)(2,1)S(1)}, u32[]{:S(2)}, u32[]{:S(2)}) collective-permute-start(bf16[4,384,256]{2,1,0:T(8,128)(2,1)S(1)} %collective-permute-done.20.refs_7_), channel_id=1, source_target_pairs={{0,1},{1,0},{2,3},{3,2},{4,5},{5,4},{6,7},{7,6},{8,9},{9,8},{10,11... | collective-permute-start | bytes 2359304 | tf_op jit(solution)/shard_map/ppermute | solution.py:27
  96.2 6.3 %copy-start.3 = (bf16[4,384,256]{2,1,0:T(8,128)(2,1)}, bf16[4,384,256]{2,1,0:T(8,128)(2,1)S(1)}, u32[]{:S(2)}) copy-start(bf16[4,384,256]{2,1,0:T(8,128)(2,1)S(1)} %collective-permute-done.18.refs_6_) | copy-start | bytes 2359300
  96.2 5.2 %collective-permute-start.19 = (bf16[4,384,256]{2,1,0:T(8,128)(2,1)S(1)}, bf16[4,384,256]{2,1,0:T(8,128)(2,1)S(1)}, u32[]{:S(2)}, u32[]{:S(2)}) collective-permute-start(bf16[4,384,256]{2,1,0:T(8,128)(2,1)S(1)} %collective-permute-done.18.refs_6_), channel_id=1, source_target_pairs={{0,1},{1,0},{2,3},{3,2},{4,5},{5,4},{6,7},{7,6},{8,9},{9,8},{10,11... | collective-permute-start | bytes 2359304 | tf_op jit(solution)/shard_map/ppermute | solution.py:27
  99.5 3.0 %collective-permute-start.17 = (bf16[4,384,256]{2,1,0:T(8,128)(2,1)S(1)}, bf16[4,384,256]{2,1,0:T(8,128)(2,1)S(1)}, u32[]{:S(2)}, u32[]{:S(2)}) collective-permute-start(bf16[4,384,256]{2,1,0:T(8,128)(2,1)S(1)} %collective-permute-done.16.refs_5_), channel_id=1, source_target_pairs={{0,1},{1,0},{2,3},{3,2},{4,5},{5,4},{6,7},{7,6},{8,9},{9,8},{10,11... | collective-permute-start | bytes 2359304 | tf_op jit(solution)/shard_map/ppermute | solution.py:27

commit v4 on v3

--- a/solution.py
+++ b/solution.py
@@ -1,3 +1,5 @@
+import functools
+
 import jax
 import jax.numpy as jnp
 import numpy as np
@@ -37,6 +39,10 @@
 
 def to_pair(array):
     return shifted(array, ({"core": 1}, {"core": 1}))
+
+
+def pair_in_two(array):
+    return jnp.concatenate([to_pair(array[:2]), to_pair(array[2:])])
 
 
 def across(array, step):
@@ -137,55 +143,81 @@
 BLOCKS = ((0, 128), (128, 384), (384, 768), (768, 1280), (1280, 1536))
 
 
-def panel_body(here_ref, f_ref, b_ref, *refs):
-    parts, (out_ref, gram, result, sems, out_sems, *buffers) = refs[: 4 * SPOTS // 2], refs[4 * SPOTS // 2 :]
+def panel_body(steps, here_ref, b_ref, *refs):
+    count = 2 * len(steps)
+    parts, refs = refs[:count], refs[count:]
+    is_last = len(steps) > 1
+    if is_last:
+        before_ref, f_ref, out_ref, before, result, before_sems, out_sems = refs
+        held = b_ref
+    else:
+        out_ref, zero_ref, held, result, sems, out_sems = refs
+        zero_ref[...] = jnp.zeros_like(zero_ref)
 
     def copy(block):
         start, end = BLOCKS[block]
-        return pltpu.make_async_copy(b_ref.at[pl.ds(start, end - start)], buffers[block], sems.at[block])
+        part = pl.ds(start, end - start)
+        return pltpu.make_async_copy(b_ref.at[part], held.at[part], sems.at[block])
+
+    def copy_before(block):
+        start, end = BLOCKS[block]
+        part = pl.ds(start, end - start)
+        return pltpu.make_async_copy(before_ref.at[part], before.at[part], before_sems.at[block])
 
     def copy_out(block):
         start, end = BLOCKS[block]
         part = pl.ds(start, end - start)
         return pltpu.make_async_copy(result.at[part], out_ref.at[part], out_sems.at[block])
 
+    def begin(block):
+        (copy_before if is_last else copy)(block).start()
+
     for block in range(2):
-        copy(block).start()
+        begin(block)
     core, x, z = place_of(here_ref[0])
-    for whose, owner in enumerate((1 - core, core)):
-        for k in range(SPOTS):
-            for m in range(SPOTS):
-                row = pl.multiple_of(group_of(owner, x, z, k, m) * GROUP, GROUP)
-                column = pl.multiple_of(owner * HALF, HALF)
-                gram[pl.ds(row, GROUP), pl.ds(column, HALF)] = parts[whose * SPOTS + k][m]
     for block, (start, end) in enumerate(BLOCKS):
-        copy(block).wait()
+        (copy_before if is_last else copy)(block).wait()
         if block + 2 < len(BLOCKS):
-            copy(block + 2).start()
-        total = jnp.dot(buffers[block][...], gram[...], preferred_element_type=F32)
-        for c in range(0, PANEL, LANES):
-            result[start:end, c : c + LANES] = (total[:, c : c + LANES] * f_ref[start:end]).astype(BF16)
+            begin(block + 2)
+        for whose, owner in enumerate((1 - core, core)):
+            total = before[start:end, whose * HALF : (whose + 1) * HALF] if is_last else None
+            for n, k in enumerate(steps):
+                columns = [
+                    held[start:end, pl.ds(pl.multiple_of(group_of(owner, x, z, k, m) * GROUP, GROUP), GROUP)]
+                    for m in range(SPOTS)
+                ]
+                right = parts[whose * len(steps) + n][...].reshape(SPOTS * GROUP, HALF)
+                product = jnp.dot(jnp.concatenate(columns, axis=1), right, preferred_element_type=F32)
+                total = product if total is None else total + product
+            if is_last:
+                for c in range(0, HALF, LANES):
+                    column = pl.multiple_of(owner * HALF + c, LANES)
+                    piece = total[:, c : c + LANES] * f_ref[start:end]
+                    result[start:end, pl.ds(column, LANES)] = piece.astype(BF16)
+            else:
+                result[start:end, whose * HALF : (whose + 1) * HALF] = total
         copy_out(block).start()
     for block in range(len(BLOCKS)):
         copy_out(block).wait()
 
 
-def panel_rows(here, bvals, factor, parts):
+def panel_part(steps, here, bvals, parts, before=None, factor=None):
     rows, aux = bvals.shape
+    is_last = before is not None
+    blocks = pltpu.SemaphoreType.DMA((len(BLOCKS),))
+    kind = BF16 if is_last else F32
+    shape = jax.ShapeDtypeStruct((rows, PANEL), kind) if is_last else pltpu.HBM((rows, PANEL), kind)
+    zeros = jax.ShapeDtypeStruct((SPOTS, GROUP, HALF), BF16)
     return pl.pallas_call(
-        panel_body,
-        in_specs=[TABLE, WHOLE, FAR] + [WHOLE] * len(parts),
-        out_specs=FAR,
-        out_shape=jax.ShapeDtypeStruct((rows, PANEL), BF16),
-        scratch_shapes=[
-            pltpu.VMEM((aux, PANEL), BF16),
-            pltpu.VMEM((rows, PANEL), BF16),
-            pltpu.SemaphoreType.DMA((len(BLOCKS),)),
-            pltpu.SemaphoreType.DMA((len(BLOCKS),)),
-        ]
-        + [pltpu.VMEM((end - start, aux), BF16) for start, end in BLOCKS],
-        compiler_params=LARGE,
-    )(here, factor, bvals, *parts)
+        functools.partial(panel_body, steps),
+        in_specs=[TABLE, WHOLE if is_last else FAR] + [WHOLE] * len(parts) + [FAR, WHOLE] * is_last,
+        out_specs=FAR if is_last else [FAR, WHOLE, WHOLE],
+        out_shape=shape if is_last else [shape, zeros, pltpu.VMEM((rows, aux), BF16)],
+        scratch_shapes=[pltpu.VMEM((rows, PANEL), F32)] * is_last
+        + [pltpu.VMEM((rows, PANEL), kind), blocks, blocks],
+        compiler_params=pltpu.CompilerParams(vmem_limit_bytes=16 << 20),
+        cost_estimate=pl.CostEstimate(flops=0, bytes_accessed=0, transcendentals=0),
+    )(here, bvals, *parts, *([before, factor] if is_last else []))
 
 
 def total_of(arrays):
@@ -208,10 +240,15 @@
     whole = (total_of([across(share, 1), across(share, 0)]) / total_rows).astype(BF16)
     rows = {k: along_second(whole, SPOTS - k) for k in (1, 3, 2)}
     row = jnp.stack([whole] + [rows[k] for k in range(1, SPOTS)])
-    own = {0: row, **{k: along_first(row, SPOTS - k) for k in (1, 3, 2)}}
-    other = {k: to_pair(own[k]) for k in (0, 1, 3, 2)}
-    parts = [other[k] for k in range(SPOTS)] + [own[k] for k in range(SPOTS)]
-    return panel_rows(here, bvals, factor, parts)[None]
+    own = {k: along_first(row, SPOTS - k) for k in (3, 1, 2)}
+    result, zeros, bvals = panel_part((0,), here, bvals, [to_pair(row), row])
+    own[3] = own[3] + zeros
+    other = {3: to_pair(own[3])}
+    for k in (1, 2):
+        own[k] = own[k] + BF16(0.0) * other[3]
+        other[k] = pair_in_two(own[k])
+    parts = [other[k] for k in (3, 1, 2)] + [own[k] for k in (3, 1, 2)]
+    return panel_part((3, 1, 2), here, bvals, parts, result, factor)[None]
 
 
 def solution(mesh):

time: 117 us -> 113 us (0.966)
  starting transfers between devices: 35.8 us -> 31.1 us
  waiting for transfers between devices: 48.4 us -> 44.3 us
  Pallas kernels: 29.4 us -> 33.1 us
    ppermute x22 -> x24, starting transfers between devices: 35.8 us -> 31.1 us  [shifted(): return lax.ppermute(array, ('grp', 'rows'), pairs)]
    ppermute x22 -> x24, waiting for transfers between devices: 48.4 us -> 44.3 us  [shifted(): return lax.ppermute(array, ('grp', 'rows'), pairs)]
    pallas_call x1 -> x2, Pallas kernels: 14.6 us -> 18.4 us  [panel_part(): pl.pallas_call(functools.partial(panel_body, steps), in_specs=[TABLE, WHO...]
  transfers between devices with their start and end apart: 22 -> 24, of which waited for: 15 -> 16; matrix products, arithmetic and copies ran while one was open for 1% -> 1% of each run, Pallas kernels for 0% -> 8%
where the time goes in v4:
time: 113 us
  waiting for transfers between devices  44.3 us (39%)
  Pallas kernels  33.1 us (29%)
  starting transfers between devices  31.1 us (28%)
  other arithmetic  1.91 us (2%)
  between operations  1.61 us (1%)
    ppermute x24, waiting for transfers between devices, shifted(): return lax.ppermute(array, ('grp', 'rows'), pairs)  44.3 us
    ppermute x24, starting transfers between devices, shifted(): return lax.ppermute(array, ('grp', 'rows'), pairs)  31.1 us
    pallas_call x2, Pallas kernels, panel_part(): pl.pallas_call(functools.partial(panel_body, steps), in_specs=[TABLE, WHO...  18.4 us
    pallas_call x1, Pallas kernels, gram_parts(): pl.pallas_call(gram_body, in_specs=[TABLE, TABLE, TABLE, FAR, FAR], out_s...  14.8 us
  transfers between devices with their start and end apart: 24, of which 16 were waited for; matrix products, arithmetic and copies ran while one was open for 1% of the time, Pallas kernels for 8%

profile of v4, /device:TPU:1, one launch (start us, length us, event | category | flops | bytes accessed | tf_op | source)
XLA Modules:
  0.0 112.9 jit_solution(16784004767446853941)
XLA Ops:
  1.3 0.7 copy-done.2
  2.0 14.8 %shard_map.46 = (bf16[4,384,256]{2,1,0:T(8,128)(2,1)S(1)}, bf16[4,384,256]{2,1,0:T(8,128)(2,1)S(1)}, bf16[4,384,256]{2,1,0:T(8,128)(2,1)S(1)}, bf16[4,384,256]{2...) custom-call(s32[1]{0:T(128)} %bitcast.here_ref, ...), custom_call_target="tpu_custom_call" | custom-call | tf_op jit(solution)/shard_map/pallas_call | solution.py:125
  16.8 0.0 copy-start.3
  16.8 1.5 %collective-permute-start.1 = (bf16[4,384,256]{2,1,0:T(8,128)(2,1)S(1)}, bf16[4,384,256]{2,1,0:T(8,128)(2,1)S(1)}, u32[]{:S(2)}, u32[]{:S(2)}) collective-permute-start(bf16[4,384,256]{2,1,0:T(8,128)(2,1)S(1)} %get-tuple-element.20), channel_id=1, source_target_pairs={{0,1},{1,0},{2,3},{3,2},{4,5},{5,4},{6,7},{7,6},{8,9},{9,8},{10,11... | collective-permute-start | bytes 2359304 | tf_op jit(solution)/shard_map/ppermute | solution.py:29
  18.3 0.1 collective-permute-start.3
  18.4 0.4 collective-permute-start.5
  18.8 0.1 collective-permute-start
  18.9 1.3 %collective-permute-done.1 = bf16[4,384,256]{2,1,0:T(8,128)(2,1)S(1)} collective-permute-done((bf16[4,384,256]{2,1,0:T(8,128)(2,1)S(1)}, bf16[4,384,256]{2,1,0:T(8,128)(2,1)S(1)}, u32[]{:S(2)}, u32[]{:S(2)}) %collective-permute-start.1) | collective-permute-done | bytes 786464 | tf_op jit(solution)/shard_map/ppermute | solution.py:29
  20.2 0.2 add_convert_fusion.2
  20.4 1.8 %collective-permute-start.2 = (bf16[4,384,256]{2,1,0:T(8,128)(2,1)S(1)}, bf16[4,384,256]{2,1,0:T(8,128)(2,1)S(1)}, u32[]{:S(2)}, u32[]{:S(2)}) collective-permute-start(bf16[4,384,256]{2,1,0:T(8,128)(2,1)S(1)} %add_convert_fusion.2), channel_id=1, source_target_pairs={{0,2},{1,9},{2,4},{3,11},{4,6},{5,13},{6,0},{7,15},{8,10},{9,17},{... | collective-permute-start | bytes 2359304 | tf_op jit(solution)/shard_map/ppermute | solution.py:29
  22.2 0.0 collective-permute-done.3
  22.2 0.2 add_convert_fusion.1
  22.4 3.0 %collective-permute-start.4 = (bf16[4,384,256]{2,1,0:T(8,128)(2,1)S(1)}, bf16[4,384,256]{2,1,0:T(8,128)(2,1)S(1)}, u32[]{:S(2)}, u32[]{:S(2)}) collective-permute-start(bf16[4,384,256]{2,1,0:T(8,128)(2,1)S(1)} %add_convert_fusion.1), channel_id=1, source_target_pairs={{0,6},{1,25},{2,0},{3,27},{4,2},{5,29},{6,4},{7,31},{8,14},{9,1},{... | collective-permute-start | bytes 2359304 | tf_op jit(solution)/shard_map/ppermute | solution.py:29
  25.4 0.0 collective-permute-done.5
  25.4 0.2 add_convert_fusion
  25.6 1.0 collective-permute-start.6
  26.6 0.0 collective-permute-done
  26.6 7.1 %collective-permute-done.2 = bf16[4,384,256]{2,1,0:T(8,128)(2,1)S(1)} collective-permute-done((bf16[4,384,256]{2,1,0:T(8,128)(2,1)S(1)}, bf16[4,384,256]{2,1,0:T(8,128)(2,1)S(1)}, u32[]{:S(2)}, u32[]{:S(2)}) %collective-permute-start.2) | collective-permute-done | bytes 786464 | tf_op jit(solution)/shard_map/ppermute | solution.py:29
  33.7 9.1 %collective-permute-done.4 = bf16[4,384,256]{2,1,0:T(8,128)(2,1)S(1)} collective-permute-done((bf16[4,384,256]{2,1,0:T(8,128)(2,1)S(1)}, bf16[4,384,256]{2,1,0:T(8,128)(2,1)S(1)}, u32[]{:S(2)}, u32[]{:S(2)}) %collective-permute-start.4) | collective-permute-done | bytes 786464 | tf_op jit(solution)/shard_map/ppermute | solution.py:29
  42.8 0.5 collective-permute-done.6
  43.3 0.6 fusion.4
  43.9 1.3 %collective-permute-start.7 = (bf16[384,256]{1,0:T(8,128)(2,1)S(1)}, bf16[384,256]{1,0:T(8,128)(2,1)S(1)}, u32[]{:S(2)}, u32[]{:S(2)}) collective-permute-start(bf16[384,256]{1,0:T(8,128)(2,1)S(1)} %get-tuple-element.37), channel_id=1, source_target_pairs={{0,8},{1,3},{2,10},{3,5},{4,12},{5,7},{6,14},{7,1},{8,16},{9,11},{... | collective-permute-start | bytes 589832 | tf_op jit(solution)/shard_map/ppermute | solution.py:29
  45.2 2.4 %collective-permute-start.9 = (bf16[384,256]{1,0:T(8,128)(2,1)S(1)}, bf16[384,256]{1,0:T(8,128)(2,1)S(1)}, u32[]{:S(2)}, u32[]{:S(2)}) collective-permute-start(bf16[384,256]{1,0:T(8,128)(2,1)S(1)} %get-tuple-element.38), channel_id=1, source_target_pairs={{0,16},{1,5},{2,18},{3,7},{4,20},{5,1},{6,22},{7,3},{8,24},{9,13},... | collective-permute-start | bytes 589832 | tf_op jit(solution)/shard_map/ppermute | solution.py:29
  47.6 1.2 %collective-permute-start.8 = (bf16[384,256]{1,0:T(8,128)(2,1)S(1)}, bf16[384,256]{1,0:T(8,128)(2,1)S(1)}, u32[]{:S(2)}, u32[]{:S(2)}) collective-permute-start(bf16[384,256]{1,0:T(8,128)(2,1)S(1)} %get-tuple-element.39), channel_id=1, source_target_pairs={{0,24},{1,7},{2,26},{3,1},{4,28},{5,3},{6,30},{7,5},{8,0},{9,15},{... | collective-permute-start | bytes 589832 | tf_op jit(solution)/shard_map/ppermute | solution.py:29
  48.8 1.2 %collective-permute-done.7 = bf16[384,256]{1,0:T(8,128)(2,1)S(1)} collective-permute-done((bf16[384,256]{1,0:T(8,128)(2,1)S(1)}, bf16[384,256]{1,0:T(8,128)(2,1)S(1)}, u32[]{:S(2)}, u32[]{:S(2)}) %collective-permute-start.7) | collective-permute-done | bytes 196640 | tf_op jit(solution)/shard_map/ppermute | solution.py:29
  50.0 3.1 %collective-permute-done.9 = bf16[384,256]{1,0:T(8,128)(2,1)S(1)} collective-permute-done((bf16[384,256]{1,0:T(8,128)(2,1)S(1)}, bf16[384,256]{1,0:T(8,128)(2,1)S(1)}, u32[]{:S(2)}, u32[]{:S(2)}) %collective-permute-start.9) | collective-permute-done | bytes 196640 | tf_op jit(solution)/shard_map/ppermute | solution.py:29
  53.1 0.0 collective-permute-done.8
  53.1 0.1 fusion.3
  53.2 3.0 %collective-permute-start.11 = (bf16[384,256]{1,0:T(8,128)(2,1)S(1)}, bf16[384,256]{1,0:T(8,128)(2,1)S(1)}, u32[]{:S(2)}, u32[]{:S(2)}) collective-permute-start(bf16[384,256]{1,0:T(8,128)(2,1)S(1)} %fusion.3), channel_id=1, source_target_pairs={{0,64},{1,65},{2,66},{3,67},{4,68},{5,69},{6,70},{7,71},{8,72},{9,... | collective-permute-start | bytes 589832 | tf_op jit(solution)/shard_map/ppermute | solution.py:29
  56.2 0.8 collective-permute-start.10
  57.0 2.3 %collective-permute-done.11 = bf16[384,256]{1,0:T(8,128)(2,1)S(1)} collective-permute-done((bf16[384,256]{1,0:T(8,128)(2,1)S(1)}, bf16[384,256]{1,0:T(8,128)(2,1)S(1)}, u32[]{:S(2)}, u32[]{:S(2)}) %collective-permute-start.11) | collective-permute-done | bytes 196640 | tf_op jit(solution)/shard_map/ppermute | solution.py:29
  59.3 6.1 %collective-permute-done.10 = bf16[384,256]{1,0:T(8,128)(2,1)S(1)} collective-permute-done((bf16[384,256]{1,0:T(8,128)(2,1)S(1)}, bf16[384,256]{1,0:T(8,128)(2,1)S(1)}, u32[]{:S(2)}, u32[]{:S(2)}) %collective-permute-start.10) | collective-permute-done | bytes 196640 | tf_op jit(solution)/shard_map/ppermute | solution.py:29
  65.4 0.1 multiply_convert_fusion
  65.4 0.2 collective-permute-start.14
  65.6 2.8 %collective-permute-start.13 = (bf16[384,256]{1,0:T(8,128)(2,1)S(1)}, bf16[384,256]{1,0:T(8,128)(2,1)S(1)}, u32[]{:S(2)}, u32[]{:S(2)}) collective-permute-start(bf16[384,256]{1,0:T(8,128)(2,1)S(1)} %multiply_convert_fusion), channel_id=1, source_target_pairs={{0,16},{1,5},{2,18},{3,7},{4,20},{5,1},{6,22},{7,3},{8,24},{9,13},... | collective-permute-start | bytes 589832 | tf_op jit(solution)/shard_map/ppermute | solution.py:29
  68.5 2.0 %collective-permute-start.12 = (bf16[384,256]{1,0:T(8,128)(2,1)S(1)}, bf16[384,256]{1,0:T(8,128)(2,1)S(1)}, u32[]{:S(2)}, u32[]{:S(2)}) collective-permute-start(bf16[384,256]{1,0:T(8,128)(2,1)S(1)} %multiply_convert_fusion), channel_id=1, source_target_pairs={{0,24},{1,7},{2,26},{3,1},{4,28},{5,3},{6,30},{7,5},{8,0},{9,15},{... | collective-permute-start | bytes 589832 | tf_op jit(solution)/shard_map/ppermute | solution.py:29
  70.4 1.1 collective-permute-done.14
  71.5 2.0 %collective-permute-done.13 = bf16[384,256]{1,0:T(8,128)(2,1)S(1)} collective-permute-done((bf16[384,256]{1,0:T(8,128)(2,1)S(1)}, bf16[384,256]{1,0:T(8,128)(2,1)S(1)}, u32[]{:S(2)}, u32[]{:S(2)}) %collective-permute-start.13) | collective-permute-done | bytes 196640 | tf_op jit(solution)/shard_map/ppermute | solution.py:29
  73.5 0.7 collective-permute-done.12
  74.2 0.1 pad_maximum_fusion.refs_1_
  74.3 2.7 %collective-permute-start.15 = (bf16[4,384,256]{2,1,0:T(8,128)(2,1)S(1)}, bf16[4,384,256]{2,1,0:T(8,128)(2,1)S(1)}, u32[]{:S(2)}, u32[]{:S(2)}) collective-permute-start(bf16[4,384,256]{2,1,0:T(8,128)(2,1)S(1)} %pad_maximum_fusion.refs_1_), channel_id=1, source_target_pairs={{0,1},{1,0},{2,3},{3,2},{4,5},{5,4},{6,7},{7,6},{8,9},{9,8},{10,11... | collective-permute-start | bytes 2359304 | tf_op jit(solution)/shard_map/ppermute | solution.py:29
  77.0 0.7 collective-permute-start.16
  77.7 2.9 %collective-permute-start.21 = (bf16[4,384,256]{2,1,0:T(8,128)(2,1)S(1)}, bf16[4,384,256]{2,1,0:T(8,128)(2,1)S(1)}, u32[]{:S(2)}, u32[]{:S(2)}) collective-permute-start(bf16[4,384,256]{2,1,0:T(8,128)(2,1)S(1)} %pad_maximum_fusion.refs_1_), channel_id=1, source_target_pairs={{0,4},{1,17},{2,6},{3,19},{4,0},{5,21},{6,2},{7,23},{8,12},{9,25},... | collective-permute-start | bytes 2359304 | tf_op jit(solution)/shard_map/ppermute | solution.py:29
  80.6 0.0 collective-permute-start.18
  80.6 0.0 collective-permute-done.15.refs_0_
  80.6 8.7 %shard_map.47 = (f32[1536,512]{1,0:T(8,128)}, bf16[4,384,256]{2,1,0:T(8,128)(2,1)S(1)}, bf16[1536,6144]{1,0:T(8,128)(2,1)S(1)}) custom-call(s32[1]{0:T(128)} %bitcast.here_ref, bf16[1536,6144]{1,0:T(8,128)(2,1)} %bitcast.24, bf16[4,384,256]{2,1,0:T(8,128)(2,1)S(1)} %collective-permute-done.15.refs_0_, bf16[4,384,256]{2,1,0:T(8,128)(2,1)S(1)} %pad_maximum_fusion.refs_1_), custom_call_target="tpu_custom_call" | custom-call | tf_op jit(solution)/shard_map/pallas_call | solution.py:211
  89.3 0.0 collective-permute-done.16
  89.4 0.2 add.53.refs_3_
  89.6 1.3 %collective-permute-start.17 = (bf16[4,384,256]{2,1,0:T(8,128)(2,1)S(1)}, bf16[4,384,256]{2,1,0:T(8,128)(2,1)S(1)}, u32[]{:S(2)}, u32[]{:S(2)}) collective-permute-start(bf16[4,384,256]{2,1,0:T(8,128)(2,1)S(1)} %add.53.refs_3_), channel_id=1, source_target_pairs={{0,1},{1,0},{2,3},{3,2},{4,5},{5,4},{6,7},{7,6},{8,9},{9,8},{10,11... | collective-permute-start | bytes 2359304 | tf_op jit(solution)/shard_map/ppermute | solution.py:29
  90.9 7.8 %collective-permute-done.21 = bf16[4,384,256]{2,1,0:T(8,128)(2,1)S(1)} collective-permute-done((bf16[4,384,256]{2,1,0:T(8,128)(2,1)S(1)}, bf16[4,384,256]{2,1,0:T(8,128)(2,1)S(1)}, u32[]{:S(2)}, u32[]{:S(2)}) %collective-permute-start.21) | collective-permute-done | bytes 786464 | tf_op jit(solution)/shard_map/ppermute | solution.py:29
  98.7 0.1 multiply_add_fusion
  98.8 0.1 fusion.5
  98.9 1.0 collective-permute-start.22
  99.9 0.1 collective-permute-start.23
  100.0 0.1 fusion.6
  100.1 0.5 collective-permute-start.19
  100.6 0.3 collective-permute-start.20
  100.9 0.4 collective-permute-done.22
  101.3 0.6 collective-permute-done.23
  101.8 0.1 pad_maximum_fusion.2.refs_2_
  101.9 0.5 collective-permute-done.19
  102.4 0.6 collective-permute-done.20
  102.9 0.1 pad_maximum_fusion.1.refs_1_
  103.0 9.6 %shard_map.48 = bf16[1536,512]{1,0:T(8,128)(2,1)} custom-call(s32[1]{0:T(128)} %bitcast.here_ref, bf16[1536,6144]{1,0:T(8,128)(2,1)S(1)} %get-tuple-element.25.b_ref, bf16[4,384,256]{2,1,0:T(8,128)(2,1)S(1)} %collective-permute-done.17.refs_0_, bf16[4,384,256]{2,1,0:T(8,128)(2,1)S(1)} %pad_maximum_fusion.1.refs_1_, ...), custom_call_target="tpu_custom_call" | custom-call | tf_op jit(solution)/shard_map/pallas_call | solution.py:211
  (9 shorter events, 0.1 us)
Async XLA Ops:
  1.3 0.7 copy-start.2
  16.8 5.4 %copy-start.3 = (bf16[4,384,256]{2,1,0:T(8,128)(2,1)S(1)}, bf16[4,384,256]{2,1,0:T(8,128)(2,1)}, u32[]{:S(2)}) copy-start(bf16[4,384,256]{2,1,0:T(8,128)(2,1)} %get-tuple-element.21) | copy-start | bytes 2359300
  16.8 3.4 %collective-permute-start.1 = (bf16[4,384,256]{2,1,0:T(8,128)(2,1)S(1)}, bf16[4,384,256]{2,1,0:T(8,128)(2,1)S(1)}, u32[]{:S(2)}, u32[]{:S(2)}) collective-permute-start(bf16[4,384,256]{2,1,0:T(8,128)(2,1)S(1)} %get-tuple-element.20), channel_id=1, source_target_pairs={{0,1},{1,0},{2,3},{3,2},{4,5},{5,4},{6,7},{7,6},{8,9},{9,8},{10,11... | collective-permute-start | bytes 2359304 | tf_op jit(solution)/shard_map/ppermute | solution.py:29
  18.3 3.9 %collective-permute-start.3 = (bf16[4,384,256]{2,1,0:T(8,128)(2,1)S(1)}, bf16[4,384,256]{2,1,0:T(8,128)(2,1)S(1)}, u32[]{:S(2)}, u32[]{:S(2)}) collective-permute-start(bf16[4,384,256]{2,1,0:T(8,128)(2,1)S(1)} %get-tuple-element.22), channel_id=1, source_target_pairs={{0,1},{1,0},{2,3},{3,2},{4,5},{5,4},{6,7},{7,6},{8,9},{9,8},{10,11... | collective-permute-start | bytes 2359304 | tf_op jit(solution)/shard_map/ppermute | solution.py:29
  18.4 7.1 %collective-permute-start.5 = (bf16[4,384,256]{2,1,0:T(8,128)(2,1)S(1)}, bf16[4,384,256]{2,1,0:T(8,128)(2,1)S(1)}, u32[]{:S(2)}, u32[]{:S(2)}) collective-permute-start(bf16[4,384,256]{2,1,0:T(8,128)(2,1)S(1)} %get-tuple-element.24), channel_id=1, source_target_pairs={{0,1},{1,0},{2,3},{3,2},{4,5},{5,4},{6,7},{7,6},{8,9},{9,8},{10,11... | collective-permute-start | bytes 2359304 | tf_op jit(solution)/shard_map/ppermute | solution.py:29
  18.8 7.8 %collective-permute-start = (bf16[4,384,256]{2,1,0:T(8,128)(2,1)S(1)}, bf16[4,384,256]{2,1,0:T(8,128)(2,1)S(1)}, u32[]{:S(2)}, u32[]{:S(2)}) collective-permute-start(bf16[4,384,256]{2,1,0:T(8,128)(2,1)S(1)} %get-tuple-element.18), channel_id=1, source_target_pairs={{0,1},{1,0},{2,3},{3,2},{4,5},{5,4},{6,7},{7,6},{8,9},{9,8},{10,11... | collective-permute-start | bytes 2359304 | tf_op jit(solution)/shard_map/ppermute | solution.py:29
  20.4 13.3 %collective-permute-start.2 = (bf16[4,384,256]{2,1,0:T(8,128)(2,1)S(1)}, bf16[4,384,256]{2,1,0:T(8,128)(2,1)S(1)}, u32[]{:S(2)}, u32[]{:S(2)}) collective-permute-start(bf16[4,384,256]{2,1,0:T(8,128)(2,1)S(1)} %add_convert_fusion.2), channel_id=1, source_target_pairs={{0,2},{1,9},{2,4},{3,11},{4,6},{5,13},{6,0},{7,15},{8,10},{9,17},{... | collective-permute-start | bytes 2359304 | tf_op jit(solution)/shard_map/ppermute | solution.py:29
  22.4 20.4 %collective-permute-start.4 = (bf16[4,384,256]{2,1,0:T(8,128)(2,1)S(1)}, bf16[4,384,256]{2,1,0:T(8,128)(2,1)S(1)}, u32[]{:S(2)}, u32[]{:S(2)}) collective-permute-start(bf16[4,384,256]{2,1,0:T(8,128)(2,1)S(1)} %add_convert_fusion.1), channel_id=1, source_target_pairs={{0,6},{1,25},{2,0},{3,27},{4,2},{5,29},{6,4},{7,31},{8,14},{9,1},{... | collective-permute-start | bytes 2359304 | tf_op jit(solution)/shard_map/ppermute | solution.py:29
  25.6 17.7 %collective-permute-start.6 = (bf16[4,384,256]{2,1,0:T(8,128)(2,1)S(1)}, bf16[4,384,256]{2,1,0:T(8,128)(2,1)S(1)}, u32[]{:S(2)}, u32[]{:S(2)}) collective-permute-start(bf16[4,384,256]{2,1,0:T(8,128)(2,1)S(1)} %add_convert_fusion), channel_id=1, source_target_pairs={{0,4},{1,17},{2,6},{3,19},{4,0},{5,21},{6,2},{7,23},{8,12},{9,25},... | collective-permute-start | bytes 2359304 | tf_op jit(solution)/shard_map/ppermute | solution.py:29
  43.9 6.1 %collective-permute-start.7 = (bf16[384,256]{1,0:T(8,128)(2,1)S(1)}, bf16[384,256]{1,0:T(8,128)(2,1)S(1)}, u32[]{:S(2)}, u32[]{:S(2)}) collective-permute-start(bf16[384,256]{1,0:T(8,128)(2,1)S(1)} %get-tuple-element.37), channel_id=1, source_target_pairs={{0,8},{1,3},{2,10},{3,5},{4,12},{5,7},{6,14},{7,1},{8,16},{9,11},{... | collective-permute-start | bytes 589832 | tf_op jit(solution)/shard_map/ppermute | solution.py:29
  45.2 7.9 %collective-permute-start.9 = (bf16[384,256]{1,0:T(8,128)(2,1)S(1)}, bf16[384,256]{1,0:T(8,128)(2,1)S(1)}, u32[]{:S(2)}, u32[]{:S(2)}) collective-permute-start(bf16[384,256]{1,0:T(8,128)(2,1)S(1)} %get-tuple-element.38), channel_id=1, source_target_pairs={{0,16},{1,5},{2,18},{3,7},{4,20},{5,1},{6,22},{7,3},{8,24},{9,13},... | collective-permute-start | bytes 589832 | tf_op jit(solution)/shard_map/ppermute | solution.py:29
  47.6 5.5 %collective-permute-start.8 = (bf16[384,256]{1,0:T(8,128)(2,1)S(1)}, bf16[384,256]{1,0:T(8,128)(2,1)S(1)}, u32[]{:S(2)}, u32[]{:S(2)}) collective-permute-start(bf16[384,256]{1,0:T(8,128)(2,1)S(1)} %get-tuple-element.39), channel_id=1, source_target_pairs={{0,24},{1,7},{2,26},{3,1},{4,28},{5,3},{6,30},{7,5},{8,0},{9,15},{... | collective-permute-start | bytes 589832 | tf_op jit(solution)/shard_map/ppermute | solution.py:29
  53.2 6.1 %collective-permute-start.11 = (bf16[384,256]{1,0:T(8,128)(2,1)S(1)}, bf16[384,256]{1,0:T(8,128)(2,1)S(1)}, u32[]{:S(2)}, u32[]{:S(2)}) collective-permute-start(bf16[384,256]{1,0:T(8,128)(2,1)S(1)} %fusion.3), channel_id=1, source_target_pairs={{0,64},{1,65},{2,66},{3,67},{4,68},{5,69},{6,70},{7,71},{8,72},{9,... | collective-permute-start | bytes 589832 | tf_op jit(solution)/shard_map/ppermute | solution.py:29
  56.2 9.2 %collective-permute-start.10 = (bf16[384,256]{1,0:T(8,128)(2,1)S(1)}, bf16[384,256]{1,0:T(8,128)(2,1)S(1)}, u32[]{:S(2)}, u32[]{:S(2)}) collective-permute-start(bf16[384,256]{1,0:T(8,128)(2,1)S(1)} %fusion.3), channel_id=1, source_target_pairs={{0,96},{1,97},{2,98},{3,99},{4,100},{5,101},{6,102},{7,103},{8,104... | collective-permute-start | bytes 589832 | tf_op jit(solution)/shard_map/ppermute | solution.py:29
  65.4 6.1 %collective-permute-start.14 = (bf16[384,256]{1,0:T(8,128)(2,1)S(1)}, bf16[384,256]{1,0:T(8,128)(2,1)S(1)}, u32[]{:S(2)}, u32[]{:S(2)}) collective-permute-start(bf16[384,256]{1,0:T(8,128)(2,1)S(1)} %multiply_convert_fusion), channel_id=1, source_target_pairs={{0,8},{1,3},{2,10},{3,5},{4,12},{5,7},{6,14},{7,1},{8,16},{9,11},{... | collective-permute-start | bytes 589832 | tf_op jit(solution)/shard_map/ppermute | solution.py:29
  65.6 7.9 %collective-permute-start.13 = (bf16[384,256]{1,0:T(8,128)(2,1)S(1)}, bf16[384,256]{1,0:T(8,128)(2,1)S(1)}, u32[]{:S(2)}, u32[]{:S(2)}) collective-permute-start(bf16[384,256]{1,0:T(8,128)(2,1)S(1)} %multiply_convert_fusion), channel_id=1, source_target_pairs={{0,16},{1,5},{2,18},{3,7},{4,20},{5,1},{6,22},{7,3},{8,24},{9,13},... | collective-permute-start | bytes 589832 | tf_op jit(solution)/shard_map/ppermute | solution.py:29
  68.5 5.8 %collective-permute-start.12 = (bf16[384,256]{1,0:T(8,128)(2,1)S(1)}, bf16[384,256]{1,0:T(8,128)(2,1)S(1)}, u32[]{:S(2)}, u32[]{:S(2)}) collective-permute-start(bf16[384,256]{1,0:T(8,128)(2,1)S(1)} %multiply_convert_fusion), channel_id=1, source_target_pairs={{0,24},{1,7},{2,26},{3,1},{4,28},{5,3},{6,30},{7,5},{8,0},{9,15},{... | collective-permute-start | bytes 589832 | tf_op jit(solution)/shard_map/ppermute | solution.py:29
  74.3 6.3 %collective-permute-start.15 = (bf16[4,384,256]{2,1,0:T(8,128)(2,1)S(1)}, bf16[4,384,256]{2,1,0:T(8,128)(2,1)S(1)}, u32[]{:S(2)}, u32[]{:S(2)}) collective-permute-start(bf16[4,384,256]{2,1,0:T(8,128)(2,1)S(1)} %pad_maximum_fusion.refs_1_), channel_id=1, source_target_pairs={{0,1},{1,0},{2,3},{3,2},{4,5},{5,4},{6,7},{7,6},{8,9},{9,8},{10,11... | collective-permute-start | bytes 2359304 | tf_op jit(solution)/shard_map/ppermute | solution.py:29
  77.0 12.3 %collective-permute-start.16 = (bf16[4,384,256]{2,1,0:T(8,128)(2,1)S(1)}, bf16[4,384,256]{2,1,0:T(8,128)(2,1)S(1)}, u32[]{:S(2)}, u32[]{:S(2)}) collective-permute-start(bf16[4,384,256]{2,1,0:T(8,128)(2,1)S(1)} %pad_maximum_fusion.refs_1_), channel_id=1, source_target_pairs={{0,2},{1,9},{2,4},{3,11},{4,6},{5,13},{6,0},{7,15},{8,10},{9,17},{... | collective-permute-start | bytes 2359304 | tf_op jit(solution)/shard_map/ppermute | solution.py:29
  77.7 21.0 %collective-permute-start.21 = (bf16[4,384,256]{2,1,0:T(8,128)(2,1)S(1)}, bf16[4,384,256]{2,1,0:T(8,128)(2,1)S(1)}, u32[]{:S(2)}, u32[]{:S(2)}) collective-permute-start(bf16[4,384,256]{2,1,0:T(8,128)(2,1)S(1)} %pad_maximum_fusion.refs_1_), channel_id=1, source_target_pairs={{0,4},{1,17},{2,6},{3,19},{4,0},{5,21},{6,2},{7,23},{8,12},{9,25},... | collective-permute-start | bytes 2359304 | tf_op jit(solution)/shard_map/ppermute | solution.py:29
  80.6 18.1 %collective-permute-start.18 = (bf16[4,384,256]{2,1,0:T(8,128)(2,1)S(1)}, bf16[4,384,256]{2,1,0:T(8,128)(2,1)S(1)}, u32[]{:S(2)}, u32[]{:S(2)}) collective-permute-start(bf16[4,384,256]{2,1,0:T(8,128)(2,1)S(1)} %pad_maximum_fusion.refs_1_), channel_id=1, source_target_pairs={{0,6},{1,25},{2,0},{3,27},{4,2},{5,29},{6,4},{7,31},{8,14},{9,1},{... | collective-permute-start | bytes 2359304 | tf_op jit(solution)/shard_map/ppermute | solution.py:29
  89.6 9.1 %collective-permute-start.17 = (bf16[4,384,256]{2,1,0:T(8,128)(2,1)S(1)}, bf16[4,384,256]{2,1,0:T(8,128)(2,1)S(1)}, u32[]{:S(2)}, u32[]{:S(2)}) collective-permute-start(bf16[4,384,256]{2,1,0:T(8,128)(2,1)S(1)} %add.53.refs_3_), channel_id=1, source_target_pairs={{0,1},{1,0},{2,3},{3,2},{4,5},{5,4},{6,7},{7,6},{8,9},{9,8},{10,11... | collective-permute-start | bytes 2359304 | tf_op jit(solution)/shard_map/ppermute | solution.py:29
  98.9 2.4 %collective-permute-start.22 = (bf16[2,384,256]{2,1,0:T(8,128)(2,1)S(1)}, bf16[2,384,256]{2,1,0:T(8,128)(2,1)S(1)}, u32[]{:S(2)}, u32[]{:S(2)}) collective-permute-start(bf16[2,384,256]{2,1,0:T(8,128)(2,1)S(1)} %get-tuple-element.31), channel_id=1, source_target_pairs={{0,1},{1,0},{2,3},{3,2},{4,5},{5,4},{6,7},{7,6},{8,9},{9,8},{10,11... | collective-permute-start | bytes 1179656 | tf_op jit(solution)/shard_map/ppermute | solution.py:29
  99.9 1.9 %collective-permute-start.23 = (bf16[2,384,256]{2,1,0:T(8,128)(2,1)S(1)}, bf16[2,384,256]{2,1,0:T(8,128)(2,1)S(1)}, u32[]{:S(2)}, u32[]{:S(2)}) collective-permute-start(bf16[2,384,256]{2,1,0:T(8,128)(2,1)S(1)} %get-tuple-element.32), channel_id=1, source_target_pairs={{0,1},{1,0},{2,3},{3,2},{4,5},{5,4},{6,7},{7,6},{8,9},{9,8},{10,11... | collective-permute-start | bytes 1179656 | tf_op jit(solution)/shard_map/ppermute | solution.py:29
  100.0 3.0 %copy-start.1 = (f32[1536,128]{1,0:T(8,128)S(1)}, f32[1536,128]{1,0:T(8,128)}, u32[]{:S(2)}) copy-start(f32[1536,128]{1,0:T(8,128)} %get-tuple-element.28.refs_7_) | copy-start | bytes 2359300
  100.1 2.3 %collective-permute-start.19 = (bf16[2,384,256]{2,1,0:T(8,128)(2,1)S(1)}, bf16[2,384,256]{2,1,0:T(8,128)(2,1)S(1)}, u32[]{:S(2)}, u32[]{:S(2)}) collective-permute-start(bf16[2,384,256]{2,1,0:T(8,128)(2,1)S(1)} %get-tuple-element.35), channel_id=1, source_target_pairs={{0,1},{1,0},{2,3},{3,2},{4,5},{5,4},{6,7},{7,6},{8,9},{9,8},{10,11... | collective-permute-start | bytes 1179656 | tf_op jit(solution)/shard_map/ppermute | solution.py:29
  100.6 2.5 %copy-start = (f32[1536,512]{1,0:T(8,128)S(1)}, f32[1536,512]{1,0:T(8,128)}, u32[]{:S(2)}) copy-start(f32[1536,512]{1,0:T(8,128)} %get-tuple-element.27.refs_6_) | copy-start | bytes 9437188
  100.6 2.4 %collective-permute-start.20 = (bf16[2,384,256]{2,1,0:T(8,128)(2,1)S(1)}, bf16[2,384,256]{2,1,0:T(8,128)(2,1)S(1)}, u32[]{:S(2)}, u32[]{:S(2)}) collective-permute-start(bf16[2,384,256]{2,1,0:T(8,128)(2,1)S(1)} %get-tuple-element.36), channel_id=1, source_target_pairs={{0,1},{1,0},{2,3},{3,2},{4,5},{5,4},{6,7},{7,6},{8,9},{9,8},{10,11... | collective-permute-start | bytes 1179656 | tf_op jit(solution)/shard_map/ppermute | solution.py:29

commit v5 on v3

--- a/solution.py
+++ b/solution.py
@@ -1,3 +1,5 @@
+import functools
+
 import jax
 import jax.numpy as jnp
 import numpy as np
@@ -135,14 +137,16 @@
 
 
 BLOCKS = ((0, 128), (128, 384), (384, 768), (768, 1280), (1280, 1536))
-
-
-def panel_body(here_ref, f_ref, b_ref, *refs):
-    parts, (out_ref, gram, result, sems, out_sems, *buffers) = refs[: 4 * SPOTS // 2], refs[4 * SPOTS // 2 :]
+HALVES = ((0, 1024), (1024, 1536))
+
+
+def early_body(here_ref, b_ref, other_ref, own_ref, out_ref, zero_ref, held, result, sems, out_sems):
+    zero_ref[...] = jnp.zeros_like(zero_ref)
 
     def copy(block):
         start, end = BLOCKS[block]
-        return pltpu.make_async_copy(b_ref.at[pl.ds(start, end - start)], buffers[block], sems.at[block])
+        part = pl.ds(start, end - start)
+        return pltpu.make_async_copy(b_ref.at[part], held.at[part], sems.at[block])
 
     def copy_out(block):
         start, end = BLOCKS[block]
@@ -152,40 +156,102 @@
     for block in range(2):
         copy(block).start()
     core, x, z = place_of(here_ref[0])
-    for whose, owner in enumerate((1 - core, core)):
-        for k in range(SPOTS):
-            for m in range(SPOTS):
-                row = pl.multiple_of(group_of(owner, x, z, k, m) * GROUP, GROUP)
-                column = pl.multiple_of(owner * HALF, HALF)
-                gram[pl.ds(row, GROUP), pl.ds(column, HALF)] = parts[whose * SPOTS + k][m]
     for block, (start, end) in enumerate(BLOCKS):
         copy(block).wait()
         if block + 2 < len(BLOCKS):
             copy(block + 2).start()
-        total = jnp.dot(buffers[block][...], gram[...], preferred_element_type=F32)
-        for c in range(0, PANEL, LANES):
-            result[start:end, c : c + LANES] = (total[:, c : c + LANES] * f_ref[start:end]).astype(BF16)
+        for whose, (owner, part) in enumerate(((1 - core, other_ref), (core, own_ref))):
+            left = columns_of(held, start, end, owner, x, z, 0)
+            product = jnp.dot(left, part[...].reshape(SPOTS * GROUP, HALF), preferred_element_type=F32)
+            result[start:end, whose * HALF : (whose + 1) * HALF] = product
         copy_out(block).start()
     for block in range(len(BLOCKS)):
         copy_out(block).wait()
 
 
-def panel_rows(here, bvals, factor, parts):
+def columns_of(held, start, end, owner, x, z, k):
+    columns = []
+    for m in range(SPOTS):
+        column = pl.multiple_of(group_of(owner, x, z, k, m) * GROUP, GROUP)
+        columns.append(held[start:end, pl.ds(column, GROUP)])
+    return jnp.concatenate(columns, axis=1)
+
+
+def early_panel(here, bvals, other, own):
     rows, aux = bvals.shape
+    blocks = pltpu.SemaphoreType.DMA((len(BLOCKS),))
     return pl.pallas_call(
-        panel_body,
-        in_specs=[TABLE, WHOLE, FAR] + [WHOLE] * len(parts),
+        early_body,
+        in_specs=[TABLE, FAR, WHOLE, WHOLE],
+        out_specs=[FAR, WHOLE, WHOLE],
+        out_shape=[
+            pltpu.HBM((rows, PANEL), F32),
+            jax.ShapeDtypeStruct((SPOTS, GROUP, HALF), BF16),
+            pltpu.VMEM((rows, aux), BF16),
+        ],
+        scratch_shapes=[pltpu.VMEM((rows, PANEL), F32), blocks, blocks],
+        compiler_params=MODEST,
+        cost_estimate=SMALL,
+    )(here, bvals, other, own)
+
+
+MODEST = pltpu.CompilerParams(vmem_limit_bytes=16 << 20)
+SMALL = pl.CostEstimate(flops=0, bytes_accessed=0, transcendentals=0)
+
+
+def late_body(steps, whose, here_ref, held, before_ref, f_ref, *refs):
+    parts, (out_ref, before, result, sems, out_sems) = refs[: len(steps)], refs[-5:]
+    core, x, z = place_of(here_ref[0])
+    owner = core if whose else 1 - core
+
+    def copy(block):
+        start, end = HALVES[block]
+        part = pl.ds(start, end - start)
+        source = before_ref.at[part, pl.ds(whose * HALF, HALF)]
+        return pltpu.make_async_copy(source, before.at[part], sems.at[block])
+
+    def copy_out(block):
+        start, end = HALVES[block]
+        part = pl.ds(start, end - start)
+        target = out_ref.at[part, pl.ds(pl.multiple_of(owner * HALF, HALF), HALF)]
+        return pltpu.make_async_copy(result.at[part], target, out_sems.at[block])
+
+    for block in range(len(HALVES)):
+        copy(block).start()
+    for block, (start, end) in enumerate(HALVES):
+        middle = (start + end) // 2
+        spans = ((start, middle), (middle, end))
+        totals = [None, None]
+        for part, k in zip(parts, steps):
+            right = part[...].reshape(SPOTS * GROUP, HALF)
+            for n, (low, high) in enumerate(spans):
+                left = columns_of(held, low, high, owner, x, z, k)
+                product = jnp.dot(left, right, preferred_element_type=F32)
+                totals[n] = product if totals[n] is None else totals[n] + product
+        copy(block).wait()
+        for total, (low, high) in zip(totals, spans):
+            for c in range(0, HALF, LANES):
+                piece = total[:, c : c + LANES] + before[low:high, c : c + LANES]
+                result[low:high, c : c + LANES] = (piece * f_ref[low:high]).astype(BF16)
+        copy_out(block).start()
+    for block in range(len(HALVES)):
+        copy_out(block).wait()
+
+
+def late_panel(steps, whose, here, held, before, factor, parts, out):
+    rows = held.shape[0]
+    blocks = pltpu.SemaphoreType.DMA((len(HALVES),))
+    extra = [] if out is None else [out]
+    return pl.pallas_call(
+        functools.partial(late_body, steps, whose),
+        in_specs=[TABLE, WHOLE, FAR, WHOLE] + [WHOLE] * len(parts) + [FAR] * len(extra),
         out_specs=FAR,
         out_shape=jax.ShapeDtypeStruct((rows, PANEL), BF16),
-        scratch_shapes=[
-            pltpu.VMEM((aux, PANEL), BF16),
-            pltpu.VMEM((rows, PANEL), BF16),
-            pltpu.SemaphoreType.DMA((len(BLOCKS),)),
-            pltpu.SemaphoreType.DMA((len(BLOCKS),)),
-        ]
-        + [pltpu.VMEM((end - start, aux), BF16) for start, end in BLOCKS],
-        compiler_params=LARGE,
-    )(here, factor, bvals, *parts)
+        scratch_shapes=[pltpu.VMEM((rows, HALF), F32), pltpu.VMEM((rows, HALF), BF16), blocks, blocks],
+        input_output_aliases={4 + len(parts): 0} if extra else {},
+        compiler_params=MODEST,
+        cost_estimate=SMALL,
+    )(here, held, before, factor, *parts, *extra)
 
 
 def total_of(arrays):
@@ -208,10 +274,17 @@
     whole = (total_of([across(share, 1), across(share, 0)]) / total_rows).astype(BF16)
     rows = {k: along_second(whole, SPOTS - k) for k in (1, 3, 2)}
     row = jnp.stack([whole] + [rows[k] for k in range(1, SPOTS)])
-    own = {0: row, **{k: along_first(row, SPOTS - k) for k in (1, 3, 2)}}
-    other = {k: to_pair(own[k]) for k in (0, 1, 3, 2)}
-    parts = [other[k] for k in range(SPOTS)] + [own[k] for k in range(SPOTS)]
-    return panel_rows(here, bvals, factor, parts)[None]
+    own = {k: along_first(row, SPOTS - k) for k in (3, 1, 2)}
+    early, zeros, held = early_panel(here, bvals, to_pair(row), row)
+    own[3] = own[3] + zeros
+    other = {3: to_pair(own[3])}
+    for k in (1, 2):
+        own[k] = own[k] + BF16(0.0) * other[3]
+        other[k] = to_pair(own[k])
+    result, steps = None, (3, 1, 2)
+    for whose, parts in ((1, own), (0, other)):
+        result = late_panel(steps, whose, here, held, early, factor, [parts[k] for k in steps], result)
+    return result[None]
 
 
 def solution(mesh):

time: 117 us -> 111 us (0.949)
  waiting for transfers between devices: 48.4 us -> 42.3 us
  starting transfers between devices: 35.8 us -> 30.5 us
  Pallas kernels: 29.4 us -> 34.3 us
    ppermute x22, waiting for transfers between devices: 48.4 us -> 42.3 us  [shifted(): return lax.ppermute(array, ('grp', 'rows'), pairs)]
    ppermute x22, starting transfers between devices: 35.8 us -> 30.5 us  [shifted(): return lax.ppermute(array, ('grp', 'rows'), pairs)]
    pallas_call x1 -> x3, Pallas kernels: 14.6 us -> 19.5 us  [the longest x2 10.8 us: late_panel(): pl.pallas_call(functools.partial(late_body, steps, whose), in_specs=[TABL...]
  transfers between devices with their start and end apart: 22 -> 22, of which waited for: 15 -> 12; matrix products, arithmetic and copies ran while one was open for 1% -> 1% of each run, Pallas kernels for 0% -> 13%
where the time goes in v5:
time: 111 us
  waiting for transfers between devices  42.3 us (38%)
  Pallas kernels  34.3 us (31%)
  starting transfers between devices  30.5 us (27%)
  other arithmetic  1.77 us (2%)
  between operations  1.62 us (1%)
    ppermute x22, waiting for transfers between devices, shifted(): return lax.ppermute(array, ('grp', 'rows'), pairs)  42.3 us
    ppermute x22, starting transfers between devices, shifted(): return lax.ppermute(array, ('grp', 'rows'), pairs)  30.5 us
    pallas_call x1, Pallas kernels, gram_parts(): pl.pallas_call(gram_body, in_specs=[TABLE, TABLE, TABLE, FAR, FAR], out_s...  14.8 us
    pallas_call x2, Pallas kernels, late_panel(): pl.pallas_call(functools.partial(late_body, steps, whose), in_specs=[TABL...  10.8 us
    pallas_call x1, Pallas kernels, early_panel(): pl.pallas_call(early_body, in_specs=[TABLE, FAR, WHOLE, WHOLE], out_specs...  8.72 us
  transfers between devices with their start and end apart: 22, of which 12 were waited for; matrix products, arithmetic and copies ran while one was open for 1% of the time, Pallas kernels for 13%

profile of v5, /device:TPU:1, one launch (start us, length us, event | category | flops | bytes accessed | tf_op | source)
XLA Modules:
  0.0 111.2 jit_solution(13142150119884471067)
XLA Ops:
  1.3 0.0 copy-start.2
  1.3 0.7 copy-done.2
  2.0 14.8 %shard_map.46 = (bf16[4,384,256]{2,1,0:T(8,128)(2,1)S(1)}, bf16[4,384,256]{2,1,0:T(8,128)(2,1)S(1)}, bf16[4,384,256]{2,1,0:T(8,128)(2,1)S(1)}, bf16[4,384,256]{2...) custom-call(s32[1]{0:T(128)} %bitcast.here_ref, ...), custom_call_target="tpu_custom_call" | custom-call | tf_op jit(solution)/shard_map/pallas_call | solution.py:121
  16.8 0.0 copy-start.3
  16.8 1.5 %collective-permute-start.1 = (bf16[4,384,256]{2,1,0:T(8,128)(2,1)S(1)}, bf16[4,384,256]{2,1,0:T(8,128)(2,1)S(1)}, u32[]{:S(2)}, u32[]{:S(2)}) collective-permute-start(bf16[4,384,256]{2,1,0:T(8,128)(2,1)S(1)} %get-tuple-element.20), channel_id=1, source_target_pairs={{0,1},{1,0},{2,3},{3,2},{4,5},{5,4},{6,7},{7,6},{8,9},{9,8},{10,11... | collective-permute-start | bytes 2359304 | tf_op jit(solution)/shard_map/ppermute | solution.py:29
  18.3 0.1 collective-permute-start.3
  18.4 0.4 collective-permute-start.5
  18.8 0.1 collective-permute-start
  18.9 1.3 %collective-permute-done.1 = bf16[4,384,256]{2,1,0:T(8,128)(2,1)S(1)} collective-permute-done((bf16[4,384,256]{2,1,0:T(8,128)(2,1)S(1)}, bf16[4,384,256]{2,1,0:T(8,128)(2,1)S(1)}, u32[]{:S(2)}, u32[]{:S(2)}) %collective-permute-start.1) | collective-permute-done | bytes 786464 | tf_op jit(solution)/shard_map/ppermute | solution.py:29
  20.2 0.2 add_convert_fusion.2
  20.4 1.8 %collective-permute-start.2 = (bf16[4,384,256]{2,1,0:T(8,128)(2,1)S(1)}, bf16[4,384,256]{2,1,0:T(8,128)(2,1)S(1)}, u32[]{:S(2)}, u32[]{:S(2)}) collective-permute-start(bf16[4,384,256]{2,1,0:T(8,128)(2,1)S(1)} %add_convert_fusion.2), channel_id=1, source_target_pairs={{0,2},{1,9},{2,4},{3,11},{4,6},{5,13},{6,0},{7,15},{8,10},{9,17},{... | collective-permute-start | bytes 2359304 | tf_op jit(solution)/shard_map/ppermute | solution.py:29
  22.2 0.0 collective-permute-done.3
  22.2 0.0 copy-done.3
  22.2 0.2 add_convert_fusion.1
  22.4 3.0 %collective-permute-start.4 = (bf16[4,384,256]{2,1,0:T(8,128)(2,1)S(1)}, bf16[4,384,256]{2,1,0:T(8,128)(2,1)S(1)}, u32[]{:S(2)}, u32[]{:S(2)}) collective-permute-start(bf16[4,384,256]{2,1,0:T(8,128)(2,1)S(1)} %add_convert_fusion.1), channel_id=1, source_target_pairs={{0,6},{1,25},{2,0},{3,27},{4,2},{5,29},{6,4},{7,31},{8,14},{9,1},{... | collective-permute-start | bytes 2359304 | tf_op jit(solution)/shard_map/ppermute | solution.py:29
  25.4 0.0 collective-permute-done.5
  25.4 0.2 add_convert_fusion
  25.6 1.0 collective-permute-start.6
  26.6 0.0 collective-permute-done
  26.6 7.1 %collective-permute-done.2 = bf16[4,384,256]{2,1,0:T(8,128)(2,1)S(1)} collective-permute-done((bf16[4,384,256]{2,1,0:T(8,128)(2,1)S(1)}, bf16[4,384,256]{2,1,0:T(8,128)(2,1)S(1)}, u32[]{:S(2)}, u32[]{:S(2)}) %collective-permute-start.2) | collective-permute-done | bytes 786464 | tf_op jit(solution)/shard_map/ppermute | solution.py:29
  33.7 9.1 %collective-permute-done.4 = bf16[4,384,256]{2,1,0:T(8,128)(2,1)S(1)} collective-permute-done((bf16[4,384,256]{2,1,0:T(8,128)(2,1)S(1)}, bf16[4,384,256]{2,1,0:T(8,128)(2,1)S(1)}, u32[]{:S(2)}, u32[]{:S(2)}) %collective-permute-start.4) | collective-permute-done | bytes 786464 | tf_op jit(solution)/shard_map/ppermute | solution.py:29
  42.8 0.5 collective-permute-done.6
  43.3 0.6 fusion.4
  43.9 1.3 %collective-permute-start.7 = (bf16[384,256]{1,0:T(8,128)(2,1)S(1)}, bf16[384,256]{1,0:T(8,128)(2,1)S(1)}, u32[]{:S(2)}, u32[]{:S(2)}) collective-permute-start(bf16[384,256]{1,0:T(8,128)(2,1)S(1)} %get-tuple-element.33), channel_id=1, source_target_pairs={{0,8},{1,3},{2,10},{3,5},{4,12},{5,7},{6,14},{7,1},{8,16},{9,11},{... | collective-permute-start | bytes 589832 | tf_op jit(solution)/shard_map/ppermute | solution.py:29
  45.2 2.4 %collective-permute-start.9 = (bf16[384,256]{1,0:T(8,128)(2,1)S(1)}, bf16[384,256]{1,0:T(8,128)(2,1)S(1)}, u32[]{:S(2)}, u32[]{:S(2)}) collective-permute-start(bf16[384,256]{1,0:T(8,128)(2,1)S(1)} %get-tuple-element.34), channel_id=1, source_target_pairs={{0,16},{1,5},{2,18},{3,7},{4,20},{5,1},{6,22},{7,3},{8,24},{9,13},... | collective-permute-start | bytes 589832 | tf_op jit(solution)/shard_map/ppermute | solution.py:29
  47.6 1.2 %collective-permute-start.8 = (bf16[384,256]{1,0:T(8,128)(2,1)S(1)}, bf16[384,256]{1,0:T(8,128)(2,1)S(1)}, u32[]{:S(2)}, u32[]{:S(2)}) collective-permute-start(bf16[384,256]{1,0:T(8,128)(2,1)S(1)} %get-tuple-element.35), channel_id=1, source_target_pairs={{0,24},{1,7},{2,26},{3,1},{4,28},{5,3},{6,30},{7,5},{8,0},{9,15},{... | collective-permute-start | bytes 589832 | tf_op jit(solution)/shard_map/ppermute | solution.py:29
  48.8 1.2 %collective-permute-done.7 = bf16[384,256]{1,0:T(8,128)(2,1)S(1)} collective-permute-done((bf16[384,256]{1,0:T(8,128)(2,1)S(1)}, bf16[384,256]{1,0:T(8,128)(2,1)S(1)}, u32[]{:S(2)}, u32[]{:S(2)}) %collective-permute-start.7) | collective-permute-done | bytes 196640 | tf_op jit(solution)/shard_map/ppermute | solution.py:29
  50.0 3.1 %collective-permute-done.9 = bf16[384,256]{1,0:T(8,128)(2,1)S(1)} collective-permute-done((bf16[384,256]{1,0:T(8,128)(2,1)S(1)}, bf16[384,256]{1,0:T(8,128)(2,1)S(1)}, u32[]{:S(2)}, u32[]{:S(2)}) %collective-permute-start.9) | collective-permute-done | bytes 196640 | tf_op jit(solution)/shard_map/ppermute | solution.py:29
  53.1 0.0 collective-permute-done.8
  53.1 0.1 fusion.3
  53.2 3.0 %collective-permute-start.11 = (bf16[384,256]{1,0:T(8,128)(2,1)S(1)}, bf16[384,256]{1,0:T(8,128)(2,1)S(1)}, u32[]{:S(2)}, u32[]{:S(2)}) collective-permute-start(bf16[384,256]{1,0:T(8,128)(2,1)S(1)} %fusion.3), channel_id=1, source_target_pairs={{0,64},{1,65},{2,66},{3,67},{4,68},{5,69},{6,70},{7,71},{8,72},{9,... | collective-permute-start | bytes 589832 | tf_op jit(solution)/shard_map/ppermute | solution.py:29
  56.2 0.8 collective-permute-start.10
  57.0 2.3 %collective-permute-done.11 = bf16[384,256]{1,0:T(8,128)(2,1)S(1)} collective-permute-done((bf16[384,256]{1,0:T(8,128)(2,1)S(1)}, bf16[384,256]{1,0:T(8,128)(2,1)S(1)}, u32[]{:S(2)}, u32[]{:S(2)}) %collective-permute-start.11) | collective-permute-done | bytes 196640 | tf_op jit(solution)/shard_map/ppermute | solution.py:29
  59.3 6.1 %collective-permute-done.10 = bf16[384,256]{1,0:T(8,128)(2,1)S(1)} collective-permute-done((bf16[384,256]{1,0:T(8,128)(2,1)S(1)}, bf16[384,256]{1,0:T(8,128)(2,1)S(1)}, u32[]{:S(2)}, u32[]{:S(2)}) %collective-permute-start.10) | collective-permute-done | bytes 196640 | tf_op jit(solution)/shard_map/ppermute | solution.py:29
  65.4 0.1 multiply_convert_fusion
  65.4 0.2 collective-permute-start.14
  65.6 2.8 %collective-permute-start.13 = (bf16[384,256]{1,0:T(8,128)(2,1)S(1)}, bf16[384,256]{1,0:T(8,128)(2,1)S(1)}, u32[]{:S(2)}, u32[]{:S(2)}) collective-permute-start(bf16[384,256]{1,0:T(8,128)(2,1)S(1)} %multiply_convert_fusion), channel_id=1, source_target_pairs={{0,16},{1,5},{2,18},{3,7},{4,20},{5,1},{6,22},{7,3},{8,24},{9,13},... | collective-permute-start | bytes 589832 | tf_op jit(solution)/shard_map/ppermute | solution.py:29
  68.5 2.0 %collective-permute-start.12 = (bf16[384,256]{1,0:T(8,128)(2,1)S(1)}, bf16[384,256]{1,0:T(8,128)(2,1)S(1)}, u32[]{:S(2)}, u32[]{:S(2)}) collective-permute-start(bf16[384,256]{1,0:T(8,128)(2,1)S(1)} %multiply_convert_fusion), channel_id=1, source_target_pairs={{0,24},{1,7},{2,26},{3,1},{4,28},{5,3},{6,30},{7,5},{8,0},{9,15},{... | collective-permute-start | bytes 589832 | tf_op jit(solution)/shard_map/ppermute | solution.py:29
  70.4 1.1 collective-permute-done.14
  71.5 2.0 %collective-permute-done.13 = bf16[384,256]{1,0:T(8,128)(2,1)S(1)} collective-permute-done((bf16[384,256]{1,0:T(8,128)(2,1)S(1)}, bf16[384,256]{1,0:T(8,128)(2,1)S(1)}, u32[]{:S(2)}, u32[]{:S(2)}) %collective-permute-start.13) | collective-permute-done | bytes 196640 | tf_op jit(solution)/shard_map/ppermute | solution.py:29
  73.5 0.7 collective-permute-done.12
  74.2 0.1 pad_maximum_fusion.own_ref
  74.3 2.7 %collective-permute-start.15 = (bf16[4,384,256]{2,1,0:T(8,128)(2,1)S(1)}, bf16[4,384,256]{2,1,0:T(8,128)(2,1)S(1)}, u32[]{:S(2)}, u32[]{:S(2)}) collective-permute-start(bf16[4,384,256]{2,1,0:T(8,128)(2,1)S(1)} %pad_maximum_fusion.own_ref), channel_id=1, source_target_pairs={{0,1},{1,0},{2,3},{3,2},{4,5},{5,4},{6,7},{7,6},{8,9},{9,8},{10,11... | collective-permute-start | bytes 2359304 | tf_op jit(solution)/shard_map/ppermute | solution.py:29
  77.0 0.7 collective-permute-start.16
  77.7 2.9 %collective-permute-start.20 = (bf16[4,384,256]{2,1,0:T(8,128)(2,1)S(1)}, bf16[4,384,256]{2,1,0:T(8,128)(2,1)S(1)}, u32[]{:S(2)}, u32[]{:S(2)}) collective-permute-start(bf16[4,384,256]{2,1,0:T(8,128)(2,1)S(1)} %pad_maximum_fusion.own_ref), channel_id=1, source_target_pairs={{0,4},{1,17},{2,6},{3,19},{4,0},{5,21},{6,2},{7,23},{8,12},{9,25},... | collective-permute-start | bytes 2359304 | tf_op jit(solution)/shard_map/ppermute | solution.py:29
  80.6 0.0 collective-permute-start.18
  80.6 0.0 collective-permute-done.15.other_ref
  80.6 8.7 %shard_map.47 = (f32[1536,512]{1,0:T(8,128)}, bf16[4,384,256]{2,1,0:T(8,128)(2,1)S(1)}, bf16[1536,6144]{1,0:T(8,128)(2,1)S(1)}) custom-call(s32[1]{0:T(128)} %bitcast.here_ref, bf16[1536,6144]{1,0:T(8,128)(2,1)} %bitcast.24, bf16[4,384,256]{2,1,0:T(8,128)(2,1)S(1)} %collective-permute-done.15.other_ref, bf16[4,384,256]{2,1,0:T(8,128)(2,1)S(1)} %pad_maximum_fusion.own_ref), custom_call_target="tpu_custom_call" | custom-call | tf_op jit(solution)/shard_map/pallas_call | solution.py:183
  89.3 0.0 collective-permute-done.16
  89.4 0.2 add.53.refs_0_
  89.6 0.0 copy-start
  89.6 0.0 copy-start.1
  89.6 1.3 %collective-permute-start.17 = (bf16[4,384,256]{2,1,0:T(8,128)(2,1)S(1)}, bf16[4,384,256]{2,1,0:T(8,128)(2,1)S(1)}, u32[]{:S(2)}, u32[]{:S(2)}) collective-permute-start(bf16[4,384,256]{2,1,0:T(8,128)(2,1)S(1)} %add.53.refs_0_), channel_id=1, source_target_pairs={{0,1},{1,0},{2,3},{3,2},{4,5},{5,4},{6,7},{7,6},{8,9},{9,8},{10,11... | collective-permute-start | bytes 2359304 | tf_op jit(solution)/shard_map/ppermute | solution.py:29
  90.9 7.8 %collective-permute-done.20 = bf16[4,384,256]{2,1,0:T(8,128)(2,1)S(1)} collective-permute-done((bf16[4,384,256]{2,1,0:T(8,128)(2,1)S(1)}, bf16[4,384,256]{2,1,0:T(8,128)(2,1)S(1)}, u32[]{:S(2)}, u32[]{:S(2)}) %collective-permute-start.20) | collective-permute-done | bytes 786464 | tf_op jit(solution)/shard_map/ppermute | solution.py:29
  98.7 0.0 collective-permute-done.18
  98.7 0.0 collective-permute-done.17.refs_0_
  98.7 0.1 multiply_add_fusion
  98.8 1.0 collective-permute-start.21
  99.8 0.3 collective-permute-start.19
  100.2 0.0 copy-done.1
  100.2 5.4 %shard_map.48.refs_3_ = bf16[1536,512]{1,0:T(8,128)(2,1)} custom-call(s32[1]{0:T(128)} %bitcast.here_ref, bf16[1536,6144]{1,0:T(8,128)(2,1)S(1)} %get-tuple-element.25.held, f32[1536,512]{1,0:T(8,128)S(1)} %copy-done, f32[1536,128]{1,0:T(8,128)S(1)} %copy-done.1, bf16[4,384,256]{2,1,0:T(8,128)(2,1)S(1)} %add.53.refs_0_, ...), custom_call_target="tpu_custom_call" | custom-call | tf_op jit(solution)/shard_map/pallas_call | solution.py:245
  105.6 0.0 collective-permute-done.21.refs_2_
  105.6 0.0 collective-permute-done.19.refs_1_
  105.6 5.4 %shard_map.49 = bf16[1536,512]{1,0:T(8,128)(2,1)} custom-call(s32[1]{0:T(128)} %bitcast.here_ref, bf16[1536,6144]{1,0:T(8,128)(2,1)S(1)} %get-tuple-element.25.held, f32[1536,512]{1,0:T(8,128)S(1)} %copy-done, f32[1536,128]{1,0:T(8,128)S(1)} %copy-done.1, bf16[4,384,256]{2,1,0:T(8,128)(2,1)S(1)} %collective-permute-done.17.refs_0_, ...), custom_call_target="tpu_custom_call", output_to_operand_aliasing={{}: (7, {})} | custom-call | tf_op jit(solution)/shard_map/pallas_call | solution.py:245
  (2 shorter events, 0.0 us)
Async XLA Ops:
  1.3 0.7 copy-start.2
  16.8 5.4 %copy-start.3 = (bf16[4,384,256]{2,1,0:T(8,128)(2,1)S(1)}, bf16[4,384,256]{2,1,0:T(8,128)(2,1)}, u32[]{:S(2)}) copy-start(bf16[4,384,256]{2,1,0:T(8,128)(2,1)} %get-tuple-element.21) | copy-start | bytes 2359300
  16.8 3.4 %collective-permute-start.1 = (bf16[4,384,256]{2,1,0:T(8,128)(2,1)S(1)}, bf16[4,384,256]{2,1,0:T(8,128)(2,1)S(1)}, u32[]{:S(2)}, u32[]{:S(2)}) collective-permute-start(bf16[4,384,256]{2,1,0:T(8,128)(2,1)S(1)} %get-tuple-element.20), channel_id=1, source_target_pairs={{0,1},{1,0},{2,3},{3,2},{4,5},{5,4},{6,7},{7,6},{8,9},{9,8},{10,11... | collective-permute-start | bytes 2359304 | tf_op jit(solution)/shard_map/ppermute | solution.py:29
  18.3 3.9 %collective-permute-start.3 = (bf16[4,384,256]{2,1,0:T(8,128)(2,1)S(1)}, bf16[4,384,256]{2,1,0:T(8,128)(2,1)S(1)}, u32[]{:S(2)}, u32[]{:S(2)}) collective-permute-start(bf16[4,384,256]{2,1,0:T(8,128)(2,1)S(1)} %get-tuple-element.22), channel_id=1, source_target_pairs={{0,1},{1,0},{2,3},{3,2},{4,5},{5,4},{6,7},{7,6},{8,9},{9,8},{10,11... | collective-permute-start | bytes 2359304 | tf_op jit(solution)/shard_map/ppermute | solution.py:29
  18.4 7.1 %collective-permute-start.5 = (bf16[4,384,256]{2,1,0:T(8,128)(2,1)S(1)}, bf16[4,384,256]{2,1,0:T(8,128)(2,1)S(1)}, u32[]{:S(2)}, u32[]{:S(2)}) collective-permute-start(bf16[4,384,256]{2,1,0:T(8,128)(2,1)S(1)} %get-tuple-element.24), channel_id=1, source_target_pairs={{0,1},{1,0},{2,3},{3,2},{4,5},{5,4},{6,7},{7,6},{8,9},{9,8},{10,11... | collective-permute-start | bytes 2359304 | tf_op jit(solution)/shard_map/ppermute | solution.py:29
  18.8 7.8 %collective-permute-start = (bf16[4,384,256]{2,1,0:T(8,128)(2,1)S(1)}, bf16[4,384,256]{2,1,0:T(8,128)(2,1)S(1)}, u32[]{:S(2)}, u32[]{:S(2)}) collective-permute-start(bf16[4,384,256]{2,1,0:T(8,128)(2,1)S(1)} %get-tuple-element.18), channel_id=1, source_target_pairs={{0,1},{1,0},{2,3},{3,2},{4,5},{5,4},{6,7},{7,6},{8,9},{9,8},{10,11... | collective-permute-start | bytes 2359304 | tf_op jit(solution)/shard_map/ppermute | solution.py:29
  20.4 13.3 %collective-permute-start.2 = (bf16[4,384,256]{2,1,0:T(8,128)(2,1)S(1)}, bf16[4,384,256]{2,1,0:T(8,128)(2,1)S(1)}, u32[]{:S(2)}, u32[]{:S(2)}) collective-permute-start(bf16[4,384,256]{2,1,0:T(8,128)(2,1)S(1)} %add_convert_fusion.2), channel_id=1, source_target_pairs={{0,2},{1,9},{2,4},{3,11},{4,6},{5,13},{6,0},{7,15},{8,10},{9,17},{... | collective-permute-start | bytes 2359304 | tf_op jit(solution)/shard_map/ppermute | solution.py:29
  22.4 20.4 %collective-permute-start.4 = (bf16[4,384,256]{2,1,0:T(8,128)(2,1)S(1)}, bf16[4,384,256]{2,1,0:T(8,128)(2,1)S(1)}, u32[]{:S(2)}, u32[]{:S(2)}) collective-permute-start(bf16[4,384,256]{2,1,0:T(8,128)(2,1)S(1)} %add_convert_fusion.1), channel_id=1, source_target_pairs={{0,6},{1,25},{2,0},{3,27},{4,2},{5,29},{6,4},{7,31},{8,14},{9,1},{... | collective-permute-start | bytes 2359304 | tf_op jit(solution)/shard_map/ppermute | solution.py:29
  25.6 17.7 %collective-permute-start.6 = (bf16[4,384,256]{2,1,0:T(8,128)(2,1)S(1)}, bf16[4,384,256]{2,1,0:T(8,128)(2,1)S(1)}, u32[]{:S(2)}, u32[]{:S(2)}) collective-permute-start(bf16[4,384,256]{2,1,0:T(8,128)(2,1)S(1)} %add_convert_fusion), channel_id=1, source_target_pairs={{0,4},{1,17},{2,6},{3,19},{4,0},{5,21},{6,2},{7,23},{8,12},{9,25},... | collective-permute-start | bytes 2359304 | tf_op jit(solution)/shard_map/ppermute | solution.py:29
  43.9 6.1 %collective-permute-start.7 = (bf16[384,256]{1,0:T(8,128)(2,1)S(1)}, bf16[384,256]{1,0:T(8,128)(2,1)S(1)}, u32[]{:S(2)}, u32[]{:S(2)}) collective-permute-start(bf16[384,256]{1,0:T(8,128)(2,1)S(1)} %get-tuple-element.33), channel_id=1, source_target_pairs={{0,8},{1,3},{2,10},{3,5},{4,12},{5,7},{6,14},{7,1},{8,16},{9,11},{... | collective-permute-start | bytes 589832 | tf_op jit(solution)/shard_map/ppermute | solution.py:29
  45.2 7.9 %collective-permute-start.9 = (bf16[384,256]{1,0:T(8,128)(2,1)S(1)}, bf16[384,256]{1,0:T(8,128)(2,1)S(1)}, u32[]{:S(2)}, u32[]{:S(2)}) collective-permute-start(bf16[384,256]{1,0:T(8,128)(2,1)S(1)} %get-tuple-element.34), channel_id=1, source_target_pairs={{0,16},{1,5},{2,18},{3,7},{4,20},{5,1},{6,22},{7,3},{8,24},{9,13},... | collective-permute-start | bytes 589832 | tf_op jit(solution)/shard_map/ppermute | solution.py:29
  47.6 5.5 %collective-permute-start.8 = (bf16[384,256]{1,0:T(8,128)(2,1)S(1)}, bf16[384,256]{1,0:T(8,128)(2,1)S(1)}, u32[]{:S(2)}, u32[]{:S(2)}) collective-permute-start(bf16[384,256]{1,0:T(8,128)(2,1)S(1)} %get-tuple-element.35), channel_id=1, source_target_pairs={{0,24},{1,7},{2,26},{3,1},{4,28},{5,3},{6,30},{7,5},{8,0},{9,15},{... | collective-permute-start | bytes 589832 | tf_op jit(solution)/shard_map/ppermute | solution.py:29
  53.2 6.1 %collective-permute-start.11 = (bf16[384,256]{1,0:T(8,128)(2,1)S(1)}, bf16[384,256]{1,0:T(8,128)(2,1)S(1)}, u32[]{:S(2)}, u32[]{:S(2)}) collective-permute-start(bf16[384,256]{1,0:T(8,128)(2,1)S(1)} %fusion.3), channel_id=1, source_target_pairs={{0,64},{1,65},{2,66},{3,67},{4,68},{5,69},{6,70},{7,71},{8,72},{9,... | collective-permute-start | bytes 589832 | tf_op jit(solution)/shard_map/ppermute | solution.py:29
  56.2 9.2 %collective-permute-start.10 = (bf16[384,256]{1,0:T(8,128)(2,1)S(1)}, bf16[384,256]{1,0:T(8,128)(2,1)S(1)}, u32[]{:S(2)}, u32[]{:S(2)}) collective-permute-start(bf16[384,256]{1,0:T(8,128)(2,1)S(1)} %fusion.3), channel_id=1, source_target_pairs={{0,96},{1,97},{2,98},{3,99},{4,100},{5,101},{6,102},{7,103},{8,104... | collective-permute-start | bytes 589832 | tf_op jit(solution)/shard_map/ppermute | solution.py:29
  65.4 6.1 %collective-permute-start.14 = (bf16[384,256]{1,0:T(8,128)(2,1)S(1)}, bf16[384,256]{1,0:T(8,128)(2,1)S(1)}, u32[]{:S(2)}, u32[]{:S(2)}) collective-permute-start(bf16[384,256]{1,0:T(8,128)(2,1)S(1)} %multiply_convert_fusion), channel_id=1, source_target_pairs={{0,8},{1,3},{2,10},{3,5},{4,12},{5,7},{6,14},{7,1},{8,16},{9,11},{... | collective-permute-start | bytes 589832 | tf_op jit(solution)/shard_map/ppermute | solution.py:29
  65.6 7.9 %collective-permute-start.13 = (bf16[384,256]{1,0:T(8,128)(2,1)S(1)}, bf16[384,256]{1,0:T(8,128)(2,1)S(1)}, u32[]{:S(2)}, u32[]{:S(2)}) collective-permute-start(bf16[384,256]{1,0:T(8,128)(2,1)S(1)} %multiply_convert_fusion), channel_id=1, source_target_pairs={{0,16},{1,5},{2,18},{3,7},{4,20},{5,1},{6,22},{7,3},{8,24},{9,13},... | collective-permute-start | bytes 589832 | tf_op jit(solution)/shard_map/ppermute | solution.py:29
  68.5 5.8 %collective-permute-start.12 = (bf16[384,256]{1,0:T(8,128)(2,1)S(1)}, bf16[384,256]{1,0:T(8,128)(2,1)S(1)}, u32[]{:S(2)}, u32[]{:S(2)}) collective-permute-start(bf16[384,256]{1,0:T(8,128)(2,1)S(1)} %multiply_convert_fusion), channel_id=1, source_target_pairs={{0,24},{1,7},{2,26},{3,1},{4,28},{5,3},{6,30},{7,5},{8,0},{9,15},{... | collective-permute-start | bytes 589832 | tf_op jit(solution)/shard_map/ppermute | solution.py:29
  74.3 6.3 %collective-permute-start.15 = (bf16[4,384,256]{2,1,0:T(8,128)(2,1)S(1)}, bf16[4,384,256]{2,1,0:T(8,128)(2,1)S(1)}, u32[]{:S(2)}, u32[]{:S(2)}) collective-permute-start(bf16[4,384,256]{2,1,0:T(8,128)(2,1)S(1)} %pad_maximum_fusion.own_ref), channel_id=1, source_target_pairs={{0,1},{1,0},{2,3},{3,2},{4,5},{5,4},{6,7},{7,6},{8,9},{9,8},{10,11... | collective-permute-start | bytes 2359304 | tf_op jit(solution)/shard_map/ppermute | solution.py:29
  77.0 12.3 %collective-permute-start.16 = (bf16[4,384,256]{2,1,0:T(8,128)(2,1)S(1)}, bf16[4,384,256]{2,1,0:T(8,128)(2,1)S(1)}, u32[]{:S(2)}, u32[]{:S(2)}) collective-permute-start(bf16[4,384,256]{2,1,0:T(8,128)(2,1)S(1)} %pad_maximum_fusion.own_ref), channel_id=1, source_target_pairs={{0,2},{1,9},{2,4},{3,11},{4,6},{5,13},{6,0},{7,15},{8,10},{9,17},{... | collective-permute-start | bytes 2359304 | tf_op jit(solution)/shard_map/ppermute | solution.py:29
  77.7 21.0 %collective-permute-start.20 = (bf16[4,384,256]{2,1,0:T(8,128)(2,1)S(1)}, bf16[4,384,256]{2,1,0:T(8,128)(2,1)S(1)}, u32[]{:S(2)}, u32[]{:S(2)}) collective-permute-start(bf16[4,384,256]{2,1,0:T(8,128)(2,1)S(1)} %pad_maximum_fusion.own_ref), channel_id=1, source_target_pairs={{0,4},{1,17},{2,6},{3,19},{4,0},{5,21},{6,2},{7,23},{8,12},{9,25},... | collective-permute-start | bytes 2359304 | tf_op jit(solution)/shard_map/ppermute | solution.py:29
  80.6 18.1 %collective-permute-start.18 = (bf16[4,384,256]{2,1,0:T(8,128)(2,1)S(1)}, bf16[4,384,256]{2,1,0:T(8,128)(2,1)S(1)}, u32[]{:S(2)}, u32[]{:S(2)}) collective-permute-start(bf16[4,384,256]{2,1,0:T(8,128)(2,1)S(1)} %pad_maximum_fusion.own_ref), channel_id=1, source_target_pairs={{0,6},{1,25},{2,0},{3,27},{4,2},{5,29},{6,4},{7,31},{8,14},{9,1},{... | collective-permute-start | bytes 2359304 | tf_op jit(solution)/shard_map/ppermute | solution.py:29
  89.6 10.6 %copy-start = (f32[1536,512]{1,0:T(8,128)S(1)}, f32[1536,512]{1,0:T(8,128)}, u32[]{:S(2)}) copy-start(f32[1536,512]{1,0:T(8,128)} %get-tuple-element.26.before_ref) | copy-start | bytes 9437188
  89.6 10.6 %copy-start.1 = (f32[1536,128]{1,0:T(8,128)S(1)}, f32[1536,128]{1,0:T(8,128)}, u32[]{:S(2)}) copy-start(f32[1536,128]{1,0:T(8,128)} %get-tuple-element.27.f_ref) | copy-start | bytes 2359300
  89.6 9.1 %collective-permute-start.17 = (bf16[4,384,256]{2,1,0:T(8,128)(2,1)S(1)}, bf16[4,384,256]{2,1,0:T(8,128)(2,1)S(1)}, u32[]{:S(2)}, u32[]{:S(2)}) collective-permute-start(bf16[4,384,256]{2,1,0:T(8,128)(2,1)S(1)} %add.53.refs_0_), channel_id=1, source_target_pairs={{0,1},{1,0},{2,3},{3,2},{4,5},{5,4},{6,7},{7,6},{8,9},{9,8},{10,11... | collective-permute-start | bytes 2359304 | tf_op jit(solution)/shard_map/ppermute | solution.py:29
  98.8 6.7 %collective-permute-start.21 = (bf16[4,384,256]{2,1,0:T(8,128)(2,1)S(1)}, bf16[4,384,256]{2,1,0:T(8,128)(2,1)S(1)}, u32[]{:S(2)}, u32[]{:S(2)}) collective-permute-start(bf16[4,384,256]{2,1,0:T(8,128)(2,1)S(1)} %get-tuple-element.31.refs_2_), channel_id=1, source_target_pairs={{0,1},{1,0},{2,3},{3,2},{4,5},{5,4},{6,7},{7,6},{8,9},{9,8},{10,11... | collective-permute-start | bytes 2359304 | tf_op jit(solution)/shard_map/ppermute | solution.py:29
  99.8 5.7 %collective-permute-start.19 = (bf16[4,384,256]{2,1,0:T(8,128)(2,1)S(1)}, bf16[4,384,256]{2,1,0:T(8,128)(2,1)S(1)}, u32[]{:S(2)}, u32[]{:S(2)}) collective-permute-start(bf16[4,384,256]{2,1,0:T(8,128)(2,1)S(1)} %get-tuple-element.32.refs_1_), channel_id=1, source_target_pairs={{0,1},{1,0},{2,3},{3,2},{4,5},{5,4},{6,7},{7,6},{8,9},{9,8},{10,11... | collective-permute-start | bytes 2359304 | tf_op jit(solution)/shard_map/ppermute | solution.py:29

commit v6 on v5

--- a/solution.py
+++ b/solution.py
@@ -199,21 +199,26 @@
 SMALL = pl.CostEstimate(flops=0, bytes_accessed=0, transcendentals=0)
 
 
-def late_body(steps, whose, here_ref, held, before_ref, f_ref, *refs):
+def late_body(steps, whose, is_last, here_ref, held, before_ref, f_ref, *refs):
     parts, (out_ref, before, result, sems, out_sems) = refs[: len(steps)], refs[-5:]
+    if not is_last:
+        out_ref, zero_ref = refs[len(steps) : len(steps) + 2]
+        zero_ref[...] = jnp.zeros_like(zero_ref)
     core, x, z = place_of(here_ref[0])
     owner = core if whose else 1 - core
 
     def copy(block):
         start, end = HALVES[block]
         part = pl.ds(start, end - start)
-        source = before_ref.at[part, pl.ds(whose * HALF, HALF)]
+        source = before_ref.at[part, pl.ds(whose * HALF if before_ref.shape[1] == PANEL else 0, HALF)]
         return pltpu.make_async_copy(source, before.at[part], sems.at[block])
 
     def copy_out(block):
         start, end = HALVES[block]
         part = pl.ds(start, end - start)
-        target = out_ref.at[part, pl.ds(pl.multiple_of(owner * HALF, HALF), HALF)]
+        target = out_ref.at[part]
+        if is_last:
+            target = out_ref.at[part, pl.ds(pl.multiple_of(owner * HALF, HALF), HALF)]
         return pltpu.make_async_copy(result.at[part], target, out_sems.at[block])
 
     for block in range(len(HALVES)):
@@ -232,22 +237,25 @@
         for total, (low, high) in zip(totals, spans):
             for c in range(0, HALF, LANES):
                 piece = total[:, c : c + LANES] + before[low:high, c : c + LANES]
-                result[low:high, c : c + LANES] = (piece * f_ref[low:high]).astype(BF16)
+                result[low:high, c : c + LANES] = (piece * f_ref[low:high]).astype(BF16) if is_last else piece
         copy_out(block).start()
     for block in range(len(HALVES)):
         copy_out(block).wait()
 
 
-def late_panel(steps, whose, here, held, before, factor, parts, out):
+def late_panel(steps, whose, here, held, before, factor, parts, out, is_last=True):
     rows = held.shape[0]
+    kind = BF16 if is_last else F32
     blocks = pltpu.SemaphoreType.DMA((len(HALVES),))
     extra = [] if out is None else [out]
     return pl.pallas_call(
-        functools.partial(late_body, steps, whose),
+        functools.partial(late_body, steps, whose, is_last),
         in_specs=[TABLE, WHOLE, FAR, WHOLE] + [WHOLE] * len(parts) + [FAR] * len(extra),
-        out_specs=FAR,
-        out_shape=jax.ShapeDtypeStruct((rows, PANEL), BF16),
-        scratch_shapes=[pltpu.VMEM((rows, HALF), F32), pltpu.VMEM((rows, HALF), BF16), blocks, blocks],
+        out_specs=[FAR] + [WHOLE] * (not is_last),
+        out_shape=[jax.ShapeDtypeStruct((rows, PANEL), BF16)]
+        if is_last
+        else [pltpu.HBM((rows, HALF), F32), jax.ShapeDtypeStruct(parts[0].shape, BF16)],
+        scratch_shapes=[pltpu.VMEM((rows, HALF), F32), pltpu.VMEM((rows, HALF), kind), blocks, blocks],
         input_output_aliases={4 + len(parts): 0} if extra else {},
         compiler_params=MODEST,
         cost_estimate=SMALL,
@@ -278,12 +286,12 @@
     early, zeros, held = early_panel(here, bvals, to_pair(row), row)
     own[3] = own[3] + zeros
     other = {3: to_pair(own[3])}
+    middle, zeros = late_panel((3,), 1, here, held, early, factor, [own[3]], None, False)
     for k in (1, 2):
-        own[k] = own[k] + BF16(0.0) * other[3]
+        own[k] = own[k] + (zeros + BF16(0.0) * other[3])
         other[k] = to_pair(own[k])
-    result, steps = None, (3, 1, 2)
-    for whose, parts in ((1, own), (0, other)):
-        result = late_panel(steps, whose, here, held, early, factor, [parts[k] for k in steps], result)
+    (result,) = late_panel((1, 2), 1, here, held, middle, factor, [own[k] for k in (1, 2)], None)
+    (result,) = late_panel((3, 1, 2), 0, here, held, early, factor, [other[k] for k in (3, 1, 2)], result)
     return result[None]
 
 

time: 111 us -> 110 us (level)
  waiting for transfers between devices: 42.3 us -> 37.3 us
  local copies, waits for them, and re-layouts: 0.74 us -> 2.63 us
  Pallas kernels: 34.3 us -> 36 us
    ppermute x22, waiting for transfers between devices: 42.3 us -> 37.3 us  [shifted(): return lax.ppermute(array, ('grp', 'rows'), pairs)]
    unnamed x8 -> x12, local copies, waits for them, and re-layouts: 0.7 us -> 2.59 us
    pallas_call x2 -> x3, Pallas kernels: 10.8 us -> 12.5 us  [late_panel(): pl.pallas_call(functools.partial(late_body, steps, whose, is_last), in_sp...]
  transfers between devices with their start and end apart: 22 -> 22, of which waited for: 12 -> 12; matrix products, arithmetic and copies ran while one was open for 1% -> 1% of each run, Pallas kernels for 13% -> 14%
where the time goes in v6:
time: 110 us
  waiting for transfers between devices  37.3 us (34%)
  Pallas kernels  36 us (33%)
  starting transfers between devices  30.5 us (28%)
  local copies, waits for them, and re-layouts  2.63 us (2%)
  other arithmetic  1.81 us (2%)
  between operations  1.63 us (1%)
    ppermute x22, waiting for transfers between devices, shifted(): return lax.ppermute(array, ('grp', 'rows'), pairs)  37.3 us
    ppermute x22, starting transfers between devices, shifted(): return lax.ppermute(array, ('grp', 'rows'), pairs)  30.5 us
    pallas_call x1, Pallas kernels, gram_parts(): pl.pallas_call(gram_body, in_specs=[TABLE, TABLE, TABLE, FAR, FAR], out_s...  14.8 us
    pallas_call x3, Pallas kernels, late_panel(): pl.pallas_call(functools.partial(late_body, steps, whose, is_last), in_sp...  12.5 us
    pallas_call x1, Pallas kernels, early_panel(): pl.pallas_call(early_body, in_specs=[TABLE, FAR, WHOLE, WHOLE], out_specs...  8.71 us
    unnamed x12, local copies, waits for them, and re-layouts  2.59 us
  transfers between devices with their start and end apart: 22, of which 12 were waited for; matrix products, arithmetic and copies ran while one was open for 1% of the time, Pallas kernels for 14%

profile of v6, /device:TPU:1, one launch (start us, length us, event | category | flops | bytes accessed | tf_op | source)
XLA Modules:
  0.0 109.9 jit_solution(5132192474133340064)
XLA Ops:
  1.3 0.0 copy-start.4
  1.3 0.7 copy-done.4
  2.0 14.8 %shard_map.46 = (bf16[4,384,256]{2,1,0:T(8,128)(2,1)S(1)}, bf16[4,384,256]{2,1,0:T(8,128)(2,1)S(1)}, bf16[4,384,256]{2,1,0:T(8,128)(2,1)S(1)}, bf16[4,384,256]{2...) custom-call(s32[1]{0:T(128)} %bitcast.here_ref, ...), custom_call_target="tpu_custom_call" | custom-call | tf_op jit(solution)/shard_map/pallas_call | solution.py:121
  16.8 0.0 copy-start.5
  16.8 1.5 %collective-permute-start.1 = (bf16[4,384,256]{2,1,0:T(8,128)(2,1)S(1)}, bf16[4,384,256]{2,1,0:T(8,128)(2,1)S(1)}, u32[]{:S(2)}, u32[]{:S(2)}) collective-permute-start(bf16[4,384,256]{2,1,0:T(8,128)(2,1)S(1)} %get-tuple-element.22), channel_id=1, source_target_pairs={{0,1},{1,0},{2,3},{3,2},{4,5},{5,4},{6,7},{7,6},{8,9},{9,8},{10,11... | collective-permute-start | bytes 2359304 | tf_op jit(solution)/shard_map/ppermute | solution.py:29
  18.3 0.1 collective-permute-start.3
  18.4 0.4 collective-permute-start.5
  18.8 0.1 collective-permute-start
  18.9 1.3 %collective-permute-done.1 = bf16[4,384,256]{2,1,0:T(8,128)(2,1)S(1)} collective-permute-done((bf16[4,384,256]{2,1,0:T(8,128)(2,1)S(1)}, bf16[4,384,256]{2,1,0:T(8,128)(2,1)S(1)}, u32[]{:S(2)}, u32[]{:S(2)}) %collective-permute-start.1) | collective-permute-done | bytes 786464 | tf_op jit(solution)/shard_map/ppermute | solution.py:29
  20.2 0.2 add_convert_fusion.2
  20.4 1.8 %collective-permute-start.2 = (bf16[4,384,256]{2,1,0:T(8,128)(2,1)S(1)}, bf16[4,384,256]{2,1,0:T(8,128)(2,1)S(1)}, u32[]{:S(2)}, u32[]{:S(2)}) collective-permute-start(bf16[4,384,256]{2,1,0:T(8,128)(2,1)S(1)} %add_convert_fusion.2), channel_id=1, source_target_pairs={{0,2},{1,9},{2,4},{3,11},{4,6},{5,13},{6,0},{7,15},{8,10},{9,17},{... | collective-permute-start | bytes 2359304 | tf_op jit(solution)/shard_map/ppermute | solution.py:29
  22.2 0.0 collective-permute-done.3
  22.2 0.0 copy-done.5
  22.2 0.2 add_convert_fusion.1
  22.4 3.0 %collective-permute-start.4 = (bf16[4,384,256]{2,1,0:T(8,128)(2,1)S(1)}, bf16[4,384,256]{2,1,0:T(8,128)(2,1)S(1)}, u32[]{:S(2)}, u32[]{:S(2)}) collective-permute-start(bf16[4,384,256]{2,1,0:T(8,128)(2,1)S(1)} %add_convert_fusion.1), channel_id=1, source_target_pairs={{0,6},{1,25},{2,0},{3,27},{4,2},{5,29},{6,4},{7,31},{8,14},{9,1},{... | collective-permute-start | bytes 2359304 | tf_op jit(solution)/shard_map/ppermute | solution.py:29
  25.4 0.0 collective-permute-done.5
  25.4 0.2 add_convert_fusion
  25.6 1.0 collective-permute-start.6
  26.6 0.0 collective-permute-done
  26.6 7.1 %collective-permute-done.2 = bf16[4,384,256]{2,1,0:T(8,128)(2,1)S(1)} collective-permute-done((bf16[4,384,256]{2,1,0:T(8,128)(2,1)S(1)}, bf16[4,384,256]{2,1,0:T(8,128)(2,1)S(1)}, u32[]{:S(2)}, u32[]{:S(2)}) %collective-permute-start.2) | collective-permute-done | bytes 786464 | tf_op jit(solution)/shard_map/ppermute | solution.py:29
  33.7 9.1 %collective-permute-done.4 = bf16[4,384,256]{2,1,0:T(8,128)(2,1)S(1)} collective-permute-done((bf16[4,384,256]{2,1,0:T(8,128)(2,1)S(1)}, bf16[4,384,256]{2,1,0:T(8,128)(2,1)S(1)}, u32[]{:S(2)}, u32[]{:S(2)}) %collective-permute-start.4) | collective-permute-done | bytes 786464 | tf_op jit(solution)/shard_map/ppermute | solution.py:29
  42.8 0.5 collective-permute-done.6
  43.3 0.6 fusion.6
  43.9 1.3 %collective-permute-start.7 = (bf16[384,256]{1,0:T(8,128)(2,1)S(1)}, bf16[384,256]{1,0:T(8,128)(2,1)S(1)}, u32[]{:S(2)}, u32[]{:S(2)}) collective-permute-start(bf16[384,256]{1,0:T(8,128)(2,1)S(1)} %get-tuple-element.37), channel_id=1, source_target_pairs={{0,8},{1,3},{2,10},{3,5},{4,12},{5,7},{6,14},{7,1},{8,16},{9,11},{... | collective-permute-start | bytes 589832 | tf_op jit(solution)/shard_map/ppermute | solution.py:29
  45.2 2.4 %collective-permute-start.9 = (bf16[384,256]{1,0:T(8,128)(2,1)S(1)}, bf16[384,256]{1,0:T(8,128)(2,1)S(1)}, u32[]{:S(2)}, u32[]{:S(2)}) collective-permute-start(bf16[384,256]{1,0:T(8,128)(2,1)S(1)} %get-tuple-element.38), channel_id=1, source_target_pairs={{0,16},{1,5},{2,18},{3,7},{4,20},{5,1},{6,22},{7,3},{8,24},{9,13},... | collective-permute-start | bytes 589832 | tf_op jit(solution)/shard_map/ppermute | solution.py:29
  47.6 1.2 %collective-permute-start.8 = (bf16[384,256]{1,0:T(8,128)(2,1)S(1)}, bf16[384,256]{1,0:T(8,128)(2,1)S(1)}, u32[]{:S(2)}, u32[]{:S(2)}) collective-permute-start(bf16[384,256]{1,0:T(8,128)(2,1)S(1)} %get-tuple-element.39), channel_id=1, source_target_pairs={{0,24},{1,7},{2,26},{3,1},{4,28},{5,3},{6,30},{7,5},{8,0},{9,15},{... | collective-permute-start | bytes 589832 | tf_op jit(solution)/shard_map/ppermute | solution.py:29
  48.8 1.2 %collective-permute-done.7 = bf16[384,256]{1,0:T(8,128)(2,1)S(1)} collective-permute-done((bf16[384,256]{1,0:T(8,128)(2,1)S(1)}, bf16[384,256]{1,0:T(8,128)(2,1)S(1)}, u32[]{:S(2)}, u32[]{:S(2)}) %collective-permute-start.7) | collective-permute-done | bytes 196640 | tf_op jit(solution)/shard_map/ppermute | solution.py:29
  50.0 3.1 %collective-permute-done.9 = bf16[384,256]{1,0:T(8,128)(2,1)S(1)} collective-permute-done((bf16[384,256]{1,0:T(8,128)(2,1)S(1)}, bf16[384,256]{1,0:T(8,128)(2,1)S(1)}, u32[]{:S(2)}, u32[]{:S(2)}) %collective-permute-start.9) | collective-permute-done | bytes 196640 | tf_op jit(solution)/shard_map/ppermute | solution.py:29
  53.1 0.0 collective-permute-done.8
  53.1 0.1 fusion.3
  53.2 3.0 %collective-permute-start.11 = (bf16[384,256]{1,0:T(8,128)(2,1)S(1)}, bf16[384,256]{1,0:T(8,128)(2,1)S(1)}, u32[]{:S(2)}, u32[]{:S(2)}) collective-permute-start(bf16[384,256]{1,0:T(8,128)(2,1)S(1)} %fusion.3), channel_id=1, source_target_pairs={{0,64},{1,65},{2,66},{3,67},{4,68},{5,69},{6,70},{7,71},{8,72},{9,... | collective-permute-start | bytes 589832 | tf_op jit(solution)/shard_map/ppermute | solution.py:29
  56.2 0.8 collective-permute-start.10
  57.0 2.3 %collective-permute-done.11 = bf16[384,256]{1,0:T(8,128)(2,1)S(1)} collective-permute-done((bf16[384,256]{1,0:T(8,128)(2,1)S(1)}, bf16[384,256]{1,0:T(8,128)(2,1)S(1)}, u32[]{:S(2)}, u32[]{:S(2)}) %collective-permute-start.11) | collective-permute-done | bytes 196640 | tf_op jit(solution)/shard_map/ppermute | solution.py:29
  59.3 6.1 %collective-permute-done.10 = bf16[384,256]{1,0:T(8,128)(2,1)S(1)} collective-permute-done((bf16[384,256]{1,0:T(8,128)(2,1)S(1)}, bf16[384,256]{1,0:T(8,128)(2,1)S(1)}, u32[]{:S(2)}, u32[]{:S(2)}) %collective-permute-start.10) | collective-permute-done | bytes 196640 | tf_op jit(solution)/shard_map/ppermute | solution.py:29
  65.4 0.1 multiply_convert_fusion
  65.4 0.2 collective-permute-start.14
  65.6 2.8 %collective-permute-start.13 = (bf16[384,256]{1,0:T(8,128)(2,1)S(1)}, bf16[384,256]{1,0:T(8,128)(2,1)S(1)}, u32[]{:S(2)}, u32[]{:S(2)}) collective-permute-start(bf16[384,256]{1,0:T(8,128)(2,1)S(1)} %multiply_convert_fusion), channel_id=1, source_target_pairs={{0,16},{1,5},{2,18},{3,7},{4,20},{5,1},{6,22},{7,3},{8,24},{9,13},... | collective-permute-start | bytes 589832 | tf_op jit(solution)/shard_map/ppermute | solution.py:29
  68.5 2.0 %collective-permute-start.12 = (bf16[384,256]{1,0:T(8,128)(2,1)S(1)}, bf16[384,256]{1,0:T(8,128)(2,1)S(1)}, u32[]{:S(2)}, u32[]{:S(2)}) collective-permute-start(bf16[384,256]{1,0:T(8,128)(2,1)S(1)} %multiply_convert_fusion), channel_id=1, source_target_pairs={{0,24},{1,7},{2,26},{3,1},{4,28},{5,3},{6,30},{7,5},{8,0},{9,15},{... | collective-permute-start | bytes 589832 | tf_op jit(solution)/shard_map/ppermute | solution.py:29
  70.4 1.1 collective-permute-done.14
  71.5 2.0 %collective-permute-done.13 = bf16[384,256]{1,0:T(8,128)(2,1)S(1)} collective-permute-done((bf16[384,256]{1,0:T(8,128)(2,1)S(1)}, bf16[384,256]{1,0:T(8,128)(2,1)S(1)}, u32[]{:S(2)}, u32[]{:S(2)}) %collective-permute-start.13) | collective-permute-done | bytes 196640 | tf_op jit(solution)/shard_map/ppermute | solution.py:29
  73.5 0.7 collective-permute-done.12
  74.2 0.1 pad_maximum_fusion.own_ref
  74.3 2.7 %collective-permute-start.15 = (bf16[4,384,256]{2,1,0:T(8,128)(2,1)S(1)}, bf16[4,384,256]{2,1,0:T(8,128)(2,1)S(1)}, u32[]{:S(2)}, u32[]{:S(2)}) collective-permute-start(bf16[4,384,256]{2,1,0:T(8,128)(2,1)S(1)} %pad_maximum_fusion.own_ref), channel_id=1, source_target_pairs={{0,1},{1,0},{2,3},{3,2},{4,5},{5,4},{6,7},{7,6},{8,9},{9,8},{10,11... | collective-permute-start | bytes 2359304 | tf_op jit(solution)/shard_map/ppermute | solution.py:29
  77.0 0.7 collective-permute-start.16
  77.7 2.9 %collective-permute-start.20 = (bf16[4,384,256]{2,1,0:T(8,128)(2,1)S(1)}, bf16[4,384,256]{2,1,0:T(8,128)(2,1)S(1)}, u32[]{:S(2)}, u32[]{:S(2)}) collective-permute-start(bf16[4,384,256]{2,1,0:T(8,128)(2,1)S(1)} %pad_maximum_fusion.own_ref), channel_id=1, source_target_pairs={{0,4},{1,17},{2,6},{3,19},{4,0},{5,21},{6,2},{7,23},{8,12},{9,25},... | collective-permute-start | bytes 2359304 | tf_op jit(solution)/shard_map/ppermute | solution.py:29
  80.6 0.0 collective-permute-start.18
  80.6 0.0 collective-permute-done.15.other_ref
  80.6 8.7 %shard_map.47 = (f32[1536,512]{1,0:T(8,128)}, bf16[4,384,256]{2,1,0:T(8,128)(2,1)S(1)}, bf16[1536,6144]{1,0:T(8,128)(2,1)S(1)}) custom-call(s32[1]{0:T(128)} %bitcast.here_ref, bf16[1536,6144]{1,0:T(8,128)(2,1)} %bitcast.24, bf16[4,384,256]{2,1,0:T(8,128)(2,1)S(1)} %collective-permute-done.15.other_ref, bf16[4,384,256]{2,1,0:T(8,128)(2,1)S(1)} %pad_maximum_fusion.own_ref), custom_call_target="tpu_custom_call" | custom-call | tf_op jit(solution)/shard_map/pallas_call | solution.py:183
  89.3 0.0 collective-permute-done.16
  89.4 0.2 add.57.refs_0_
  89.6 1.3 %collective-permute-start.17 = (bf16[4,384,256]{2,1,0:T(8,128)(2,1)S(1)}, bf16[4,384,256]{2,1,0:T(8,128)(2,1)S(1)}, u32[]{:S(2)}, u32[]{:S(2)}) collective-permute-start(bf16[4,384,256]{2,1,0:T(8,128)(2,1)S(1)} %add.57.refs_0_), channel_id=1, source_target_pairs={{0,1},{1,0},{2,3},{3,2},{4,5},{5,4},{6,7},{7,6},{8,9},{9,8},{10,11... | collective-permute-start | bytes 2359304 | tf_op jit(solution)/shard_map/ppermute | solution.py:29
  90.9 1.9 %copy-done = f32[1536,512]{1,0:T(8,128)S(1)} copy-done((f32[1536,512]{1,0:T(8,128)S(1)}, f32[1536,512]{1,0:T(8,128)}, u32[]{:S(2)}) %copy-start) | copy-done | bytes 3145752
  92.8 3.0 %shard_map.48 = (f32[1536,256]{1,0:T(8,128)}, bf16[4,384,256]{2,1,0:T(8,128)(2,1)S(1)}) custom-call(s32[1]{0:T(128)} %bitcast.here_ref, bf16[1536,6144]{1,0:T(8,128)(2,1)S(1)} %get-tuple-element.27.held, f32[1536,512]{1,0:T(8,128)S(1)} %copy-done, f32[1536,128]{1,0:T(8,128)S(1)} %copy-done.2, bf16[4,384,256]{2,1,0:T(8,128)(2,1)S(1)} %add.57.refs_0_), custom_call_target="tpu_custom_call" | custom-call | tf_op jit(solution)/shard_map/pallas_call | solution.py:251
  95.8 2.8 %collective-permute-done.20 = bf16[4,384,256]{2,1,0:T(8,128)(2,1)S(1)} collective-permute-done((bf16[4,384,256]{2,1,0:T(8,128)(2,1)S(1)}, bf16[4,384,256]{2,1,0:T(8,128)(2,1)S(1)}, u32[]{:S(2)}, u32[]{:S(2)}) %collective-permute-start.20) | collective-permute-done | bytes 786464 | tf_op jit(solution)/shard_map/ppermute | solution.py:29
  98.7 0.0 collective-permute-done.18
  98.7 0.0 collective-permute-done.17.refs_0_
  98.7 0.2 fusion.4
  98.9 1.0 collective-permute-start.21
  99.9 0.3 collective-permute-start.19
  100.2 4.0 %shard_map.49.refs_3_ = bf16[1536,512]{1,0:T(8,128)(2,1)} custom-call(s32[1]{0:T(128)} %bitcast.here_ref, bf16[1536,6144]{1,0:T(8,128)(2,1)S(1)} %get-tuple-element.27.held, f32[1536,256]{1,0:T(8,128)S(1)} %copy-done.3, f32[1536,128]{1,0:T(8,128)S(1)} %copy-done.2, bf16[4,384,256]{2,1,0:T(8,128)(2,1)S(1)} %get-tuple-element.36.refs_0_, ...), custom_call_target="tpu_custom_call" | custom-call | tf_op jit(solution)/shard_map/pallas_call | solution.py:251
  104.3 0.0 collective-permute-done.21.refs_2_
  104.3 0.0 collective-permute-done.19.refs_1_
  104.3 0.0 copy-done.1
  104.3 5.4 %shard_map.50 = bf16[1536,512]{1,0:T(8,128)(2,1)} custom-call(s32[1]{0:T(128)} %bitcast.here_ref, bf16[1536,6144]{1,0:T(8,128)(2,1)S(1)} %get-tuple-element.27.held, f32[1536,512]{1,0:T(8,128)S(1)} %copy-done.1, f32[1536,128]{1,0:T(8,128)S(1)} %copy-done.2, bf16[4,384,256]{2,1,0:T(8,128)(2,1)S(1)} %collective-permute-done.17.refs_0_, ...), custom_call_target="tpu_custom_call", output_to_operand_aliasing={{}: (7, {})} | custom-call | tf_op jit(solution)/shard_map/pallas_call | solution.py:251
  (7 shorter events, 0.1 us)
Async XLA Ops:
  1.3 0.7 copy-start.4
  16.8 5.4 %copy-start.5 = (bf16[4,384,256]{2,1,0:T(8,128)(2,1)S(1)}, bf16[4,384,256]{2,1,0:T(8,128)(2,1)}, u32[]{:S(2)}) copy-start(bf16[4,384,256]{2,1,0:T(8,128)(2,1)} %get-tuple-element.23) | copy-start | bytes 2359300
  16.8 3.4 %collective-permute-start.1 = (bf16[4,384,256]{2,1,0:T(8,128)(2,1)S(1)}, bf16[4,384,256]{2,1,0:T(8,128)(2,1)S(1)}, u32[]{:S(2)}, u32[]{:S(2)}) collective-permute-start(bf16[4,384,256]{2,1,0:T(8,128)(2,1)S(1)} %get-tuple-element.22), channel_id=1, source_target_pairs={{0,1},{1,0},{2,3},{3,2},{4,5},{5,4},{6,7},{7,6},{8,9},{9,8},{10,11... | collective-permute-start | bytes 2359304 | tf_op jit(solution)/shard_map/ppermute | solution.py:29
  18.3 3.9 %collective-permute-start.3 = (bf16[4,384,256]{2,1,0:T(8,128)(2,1)S(1)}, bf16[4,384,256]{2,1,0:T(8,128)(2,1)S(1)}, u32[]{:S(2)}, u32[]{:S(2)}) collective-permute-start(bf16[4,384,256]{2,1,0:T(8,128)(2,1)S(1)} %get-tuple-element.24), channel_id=1, source_target_pairs={{0,1},{1,0},{2,3},{3,2},{4,5},{5,4},{6,7},{7,6},{8,9},{9,8},{10,11... | collective-permute-start | bytes 2359304 | tf_op jit(solution)/shard_map/ppermute | solution.py:29
  18.4 7.1 %collective-permute-start.5 = (bf16[4,384,256]{2,1,0:T(8,128)(2,1)S(1)}, bf16[4,384,256]{2,1,0:T(8,128)(2,1)S(1)}, u32[]{:S(2)}, u32[]{:S(2)}) collective-permute-start(bf16[4,384,256]{2,1,0:T(8,128)(2,1)S(1)} %get-tuple-element.26), channel_id=1, source_target_pairs={{0,1},{1,0},{2,3},{3,2},{4,5},{5,4},{6,7},{7,6},{8,9},{9,8},{10,11... | collective-permute-start | bytes 2359304 | tf_op jit(solution)/shard_map/ppermute | solution.py:29
  18.8 7.8 %collective-permute-start = (bf16[4,384,256]{2,1,0:T(8,128)(2,1)S(1)}, bf16[4,384,256]{2,1,0:T(8,128)(2,1)S(1)}, u32[]{:S(2)}, u32[]{:S(2)}) collective-permute-start(bf16[4,384,256]{2,1,0:T(8,128)(2,1)S(1)} %get-tuple-element.20), channel_id=1, source_target_pairs={{0,1},{1,0},{2,3},{3,2},{4,5},{5,4},{6,7},{7,6},{8,9},{9,8},{10,11... | collective-permute-start | bytes 2359304 | tf_op jit(solution)/shard_map/ppermute | solution.py:29
  20.4 13.3 %collective-permute-start.2 = (bf16[4,384,256]{2,1,0:T(8,128)(2,1)S(1)}, bf16[4,384,256]{2,1,0:T(8,128)(2,1)S(1)}, u32[]{:S(2)}, u32[]{:S(2)}) collective-permute-start(bf16[4,384,256]{2,1,0:T(8,128)(2,1)S(1)} %add_convert_fusion.2), channel_id=1, source_target_pairs={{0,2},{1,9},{2,4},{3,11},{4,6},{5,13},{6,0},{7,15},{8,10},{9,17},{... | collective-permute-start | bytes 2359304 | tf_op jit(solution)/shard_map/ppermute | solution.py:29
  22.4 20.4 %collective-permute-start.4 = (bf16[4,384,256]{2,1,0:T(8,128)(2,1)S(1)}, bf16[4,384,256]{2,1,0:T(8,128)(2,1)S(1)}, u32[]{:S(2)}, u32[]{:S(2)}) collective-permute-start(bf16[4,384,256]{2,1,0:T(8,128)(2,1)S(1)} %add_convert_fusion.1), channel_id=1, source_target_pairs={{0,6},{1,25},{2,0},{3,27},{4,2},{5,29},{6,4},{7,31},{8,14},{9,1},{... | collective-permute-start | bytes 2359304 | tf_op jit(solution)/shard_map/ppermute | solution.py:29
  25.6 17.7 %collective-permute-start.6 = (bf16[4,384,256]{2,1,0:T(8,128)(2,1)S(1)}, bf16[4,384,256]{2,1,0:T(8,128)(2,1)S(1)}, u32[]{:S(2)}, u32[]{:S(2)}) collective-permute-start(bf16[4,384,256]{2,1,0:T(8,128)(2,1)S(1)} %add_convert_fusion), channel_id=1, source_target_pairs={{0,4},{1,17},{2,6},{3,19},{4,0},{5,21},{6,2},{7,23},{8,12},{9,25},... | collective-permute-start | bytes 2359304 | tf_op jit(solution)/shard_map/ppermute | solution.py:29
  43.9 6.1 %collective-permute-start.7 = (bf16[384,256]{1,0:T(8,128)(2,1)S(1)}, bf16[384,256]{1,0:T(8,128)(2,1)S(1)}, u32[]{:S(2)}, u32[]{:S(2)}) collective-permute-start(bf16[384,256]{1,0:T(8,128)(2,1)S(1)} %get-tuple-element.37), channel_id=1, source_target_pairs={{0,8},{1,3},{2,10},{3,5},{4,12},{5,7},{6,14},{7,1},{8,16},{9,11},{... | collective-permute-start | bytes 589832 | tf_op jit(solution)/shard_map/ppermute | solution.py:29
  45.2 7.9 %collective-permute-start.9 = (bf16[384,256]{1,0:T(8,128)(2,1)S(1)}, bf16[384,256]{1,0:T(8,128)(2,1)S(1)}, u32[]{:S(2)}, u32[]{:S(2)}) collective-permute-start(bf16[384,256]{1,0:T(8,128)(2,1)S(1)} %get-tuple-element.38), channel_id=1, source_target_pairs={{0,16},{1,5},{2,18},{3,7},{4,20},{5,1},{6,22},{7,3},{8,24},{9,13},... | collective-permute-start | bytes 589832 | tf_op jit(solution)/shard_map/ppermute | solution.py:29
  47.6 5.5 %collective-permute-start.8 = (bf16[384,256]{1,0:T(8,128)(2,1)S(1)}, bf16[384,256]{1,0:T(8,128)(2,1)S(1)}, u32[]{:S(2)}, u32[]{:S(2)}) collective-permute-start(bf16[384,256]{1,0:T(8,128)(2,1)S(1)} %get-tuple-element.39), channel_id=1, source_target_pairs={{0,24},{1,7},{2,26},{3,1},{4,28},{5,3},{6,30},{7,5},{8,0},{9,15},{... | collective-permute-start | bytes 589832 | tf_op jit(solution)/shard_map/ppermute | solution.py:29
  53.2 6.1 %collective-permute-start.11 = (bf16[384,256]{1,0:T(8,128)(2,1)S(1)}, bf16[384,256]{1,0:T(8,128)(2,1)S(1)}, u32[]{:S(2)}, u32[]{:S(2)}) collective-permute-start(bf16[384,256]{1,0:T(8,128)(2,1)S(1)} %fusion.3), channel_id=1, source_target_pairs={{0,64},{1,65},{2,66},{3,67},{4,68},{5,69},{6,70},{7,71},{8,72},{9,... | collective-permute-start | bytes 589832 | tf_op jit(solution)/shard_map/ppermute | solution.py:29
  56.2 9.2 %collective-permute-start.10 = (bf16[384,256]{1,0:T(8,128)(2,1)S(1)}, bf16[384,256]{1,0:T(8,128)(2,1)S(1)}, u32[]{:S(2)}, u32[]{:S(2)}) collective-permute-start(bf16[384,256]{1,0:T(8,128)(2,1)S(1)} %fusion.3), channel_id=1, source_target_pairs={{0,96},{1,97},{2,98},{3,99},{4,100},{5,101},{6,102},{7,103},{8,104... | collective-permute-start | bytes 589832 | tf_op jit(solution)/shard_map/ppermute | solution.py:29
  65.4 6.1 %collective-permute-start.14 = (bf16[384,256]{1,0:T(8,128)(2,1)S(1)}, bf16[384,256]{1,0:T(8,128)(2,1)S(1)}, u32[]{:S(2)}, u32[]{:S(2)}) collective-permute-start(bf16[384,256]{1,0:T(8,128)(2,1)S(1)} %multiply_convert_fusion), channel_id=1, source_target_pairs={{0,8},{1,3},{2,10},{3,5},{4,12},{5,7},{6,14},{7,1},{8,16},{9,11},{... | collective-permute-start | bytes 589832 | tf_op jit(solution)/shard_map/ppermute | solution.py:29
  65.6 7.9 %collective-permute-start.13 = (bf16[384,256]{1,0:T(8,128)(2,1)S(1)}, bf16[384,256]{1,0:T(8,128)(2,1)S(1)}, u32[]{:S(2)}, u32[]{:S(2)}) collective-permute-start(bf16[384,256]{1,0:T(8,128)(2,1)S(1)} %multiply_convert_fusion), channel_id=1, source_target_pairs={{0,16},{1,5},{2,18},{3,7},{4,20},{5,1},{6,22},{7,3},{8,24},{9,13},... | collective-permute-start | bytes 589832 | tf_op jit(solution)/shard_map/ppermute | solution.py:29
  68.5 5.8 %collective-permute-start.12 = (bf16[384,256]{1,0:T(8,128)(2,1)S(1)}, bf16[384,256]{1,0:T(8,128)(2,1)S(1)}, u32[]{:S(2)}, u32[]{:S(2)}) collective-permute-start(bf16[384,256]{1,0:T(8,128)(2,1)S(1)} %multiply_convert_fusion), channel_id=1, source_target_pairs={{0,24},{1,7},{2,26},{3,1},{4,28},{5,3},{6,30},{7,5},{8,0},{9,15},{... | collective-permute-start | bytes 589832 | tf_op jit(solution)/shard_map/ppermute | solution.py:29
  74.3 6.3 %collective-permute-start.15 = (bf16[4,384,256]{2,1,0:T(8,128)(2,1)S(1)}, bf16[4,384,256]{2,1,0:T(8,128)(2,1)S(1)}, u32[]{:S(2)}, u32[]{:S(2)}) collective-permute-start(bf16[4,384,256]{2,1,0:T(8,128)(2,1)S(1)} %pad_maximum_fusion.own_ref), channel_id=1, source_target_pairs={{0,1},{1,0},{2,3},{3,2},{4,5},{5,4},{6,7},{7,6},{8,9},{9,8},{10,11... | collective-permute-start | bytes 2359304 | tf_op jit(solution)/shard_map/ppermute | solution.py:29
  77.0 12.3 %collective-permute-start.16 = (bf16[4,384,256]{2,1,0:T(8,128)(2,1)S(1)}, bf16[4,384,256]{2,1,0:T(8,128)(2,1)S(1)}, u32[]{:S(2)}, u32[]{:S(2)}) collective-permute-start(bf16[4,384,256]{2,1,0:T(8,128)(2,1)S(1)} %pad_maximum_fusion.own_ref), channel_id=1, source_target_pairs={{0,2},{1,9},{2,4},{3,11},{4,6},{5,13},{6,0},{7,15},{8,10},{9,17},{... | collective-permute-start | bytes 2359304 | tf_op jit(solution)/shard_map/ppermute | solution.py:29
  77.7 21.0 %collective-permute-start.20 = (bf16[4,384,256]{2,1,0:T(8,128)(2,1)S(1)}, bf16[4,384,256]{2,1,0:T(8,128)(2,1)S(1)}, u32[]{:S(2)}, u32[]{:S(2)}) collective-permute-start(bf16[4,384,256]{2,1,0:T(8,128)(2,1)S(1)} %pad_maximum_fusion.own_ref), channel_id=1, source_target_pairs={{0,4},{1,17},{2,6},{3,19},{4,0},{5,21},{6,2},{7,23},{8,12},{9,25},... | collective-permute-start | bytes 2359304 | tf_op jit(solution)/shard_map/ppermute | solution.py:29
  80.6 18.1 %collective-permute-start.18 = (bf16[4,384,256]{2,1,0:T(8,128)(2,1)S(1)}, bf16[4,384,256]{2,1,0:T(8,128)(2,1)S(1)}, u32[]{:S(2)}, u32[]{:S(2)}) collective-permute-start(bf16[4,384,256]{2,1,0:T(8,128)(2,1)S(1)} %pad_maximum_fusion.own_ref), channel_id=1, source_target_pairs={{0,6},{1,25},{2,0},{3,27},{4,2},{5,29},{6,4},{7,31},{8,14},{9,1},{... | collective-permute-start | bytes 2359304 | tf_op jit(solution)/shard_map/ppermute | solution.py:29
  89.3 1.6 %copy-start.2 = (f32[1536,128]{1,0:T(8,128)S(1)}, f32[1536,128]{1,0:T(8,128)}, u32[]{:S(2)}) copy-start(f32[1536,128]{1,0:T(8,128)} %get-tuple-element.29.f_ref) | copy-start | bytes 2359300
  89.6 9.1 %collective-permute-start.17 = (bf16[4,384,256]{2,1,0:T(8,128)(2,1)S(1)}, bf16[4,384,256]{2,1,0:T(8,128)(2,1)S(1)}, u32[]{:S(2)}, u32[]{:S(2)}) collective-permute-start(bf16[4,384,256]{2,1,0:T(8,128)(2,1)S(1)} %add.57.refs_0_), channel_id=1, source_target_pairs={{0,1},{1,0},{2,3},{3,2},{4,5},{5,4},{6,7},{7,6},{8,9},{9,8},{10,11... | collective-permute-start | bytes 2359304 | tf_op jit(solution)/shard_map/ppermute | solution.py:29
  90.9 1.9 %copy-start = (f32[1536,512]{1,0:T(8,128)S(1)}, f32[1536,512]{1,0:T(8,128)}, u32[]{:S(2)}) copy-start(f32[1536,512]{1,0:T(8,128)} %get-tuple-element.28.before_ref) | copy-start | bytes 9437188
  98.7 1.5 %copy-start.3 = (f32[1536,256]{1,0:T(8,128)S(1)}, f32[1536,256]{1,0:T(8,128)}, u32[]{:S(2)}) copy-start(f32[1536,256]{1,0:T(8,128)} %get-tuple-element.32.before_ref) | copy-start | bytes 4718596
  98.9 5.4 %collective-permute-start.21 = (bf16[4,384,256]{2,1,0:T(8,128)(2,1)S(1)}, bf16[4,384,256]{2,1,0:T(8,128)(2,1)S(1)}, u32[]{:S(2)}, u32[]{:S(2)}) collective-permute-start(bf16[4,384,256]{2,1,0:T(8,128)(2,1)S(1)} %get-tuple-element.35.refs_1_), channel_id=1, source_target_pairs={{0,1},{1,0},{2,3},{3,2},{4,5},{5,4},{6,7},{7,6},{8,9},{9,8},{10,11... | collective-permute-start | bytes 2359304 | tf_op jit(solution)/shard_map/ppermute | solution.py:29
  99.9 4.4 %collective-permute-start.19 = (bf16[4,384,256]{2,1,0:T(8,128)(2,1)S(1)}, bf16[4,384,256]{2,1,0:T(8,128)(2,1)S(1)}, u32[]{:S(2)}, u32[]{:S(2)}) collective-permute-start(bf16[4,384,256]{2,1,0:T(8,128)(2,1)S(1)} %get-tuple-element.36.refs_0_), channel_id=1, source_target_pairs={{0,1},{1,0},{2,3},{3,2},{4,5},{5,4},{6,7},{7,6},{8,9},{9,8},{10,11... | collective-permute-start | bytes 2359304 | tf_op jit(solution)/shard_map/ppermute | solution.py:29
  100.2 4.1 %copy-start.1 = (f32[1536,512]{1,0:T(8,128)S(1)}, f32[1536,512]{1,0:T(8,128)}, u32[]{:S(2)}) copy-start(f32[1536,512]{1,0:T(8,128)} %get-tuple-element.28.before_ref) | copy-start | bytes 9437188

commit v7 on v6

--- a/solution.py
+++ b/solution.py
@@ -276,8 +276,8 @@
     parts = gram_parts(here, live, laplace, gap, bvals)
     theirs, mine, factor = parts[:SPOTS], parts[SPOTS : 2 * SPOTS], parts[-1]
 
-    pairs = {k: total_of([mine[k], to_pair(theirs[k])]) for k in (1, 3, 2, 0)}
-    held = total_of([pairs[0]] + [along_first(pairs[k].astype(BF16), k) for k in (1, 3, 2)])
+    pairs = {k: total_of([mine[k], to_pair(theirs[k])]) for k in (2, 1, 3, 0)}
+    held = total_of([pairs[0]] + [along_first(pairs[k].astype(BF16), k) for k in (2, 1, 3)])
     share = total_of([held[0]] + [along_second(held[k].astype(BF16), k) for k in (1, 3, 2)]).astype(BF16)
     whole = (total_of([across(share, 1), across(share, 0)]) / total_rows).astype(BF16)
     rows = {k: along_second(whole, SPOTS - k) for k in (1, 3, 2)}

time: 110 us -> 110 us (level)
  waiting for transfers between devices: 37.3 us -> 35.6 us
  starting transfers between devices: 30.5 us -> 31.7 us
    ppermute x22, waiting for transfers between devices: 37.3 us -> 35.6 us  [shifted(): return lax.ppermute(array, ('grp', 'rows'), pairs)]
    ppermute x22, starting transfers between devices: 30.5 us -> 31.7 us  [shifted(): return lax.ppermute(array, ('grp', 'rows'), pairs)]
  transfers between devices with their start and end apart: 22 -> 22, of which waited for: 12 -> 11; matrix products, arithmetic and copies ran while one was open for 1% -> 1% of each run, Pallas kernels for 14% -> 14%
where the time goes in v7:
time: 110 us; the launch traced here: 109 us
  Pallas kernels  36 us (33%)
  waiting for transfers between devices  35.6 us (32%)
  starting transfers between devices  31.7 us (29%)
  local copies, waits for them, and re-layouts  2.63 us (2%)
  other arithmetic  1.81 us (2%)
  between operations  1.64 us (1%)
    ppermute x22, waiting for transfers between devices, shifted(): return lax.ppermute(array, ('grp', 'rows'), pairs)  35.6 us
    ppermute x22, starting transfers between devices, shifted(): return lax.ppermute(array, ('grp', 'rows'), pairs)  31.7 us
    pallas_call x1, Pallas kernels, gram_parts(): pl.pallas_call(gram_body, in_specs=[TABLE, TABLE, TABLE, FAR, FAR], out_s...  14.8 us
    pallas_call x3, Pallas kernels, late_panel(): pl.pallas_call(functools.partial(late_body, steps, whose, is_last), in_sp...  12.5 us
    pallas_call x1, Pallas kernels, early_panel(): pl.pallas_call(early_body, in_specs=[TABLE, FAR, WHOLE, WHOLE], out_specs...  8.71 us
    unnamed x12, local copies, waits for them, and re-layouts  2.59 us
  transfers between devices with their start and end apart: 22, of which 11 were waited for; matrix products, arithmetic and copies ran while one was open for 1% of the time, Pallas kernels for 14%

profile of v7, /device:TPU:1, one launch (start us, length us, event | category | flops | bytes accessed | tf_op | source)
XLA Modules:
  0.0 109.3 jit_solution(8259763490230140104)
XLA Ops:
  1.3 0.0 copy-start.4
  1.3 0.7 copy-done.4
  2.0 14.8 %shard_map.46 = (bf16[4,384,256]{2,1,0:T(8,128)(2,1)S(1)}, bf16[4,384,256]{2,1,0:T(8,128)(2,1)S(1)}, bf16[4,384,256]{2,1,0:T(8,128)(2,1)S(1)}, bf16[4,384,256]{2...) custom-call(s32[1]{0:T(128)} %bitcast.here_ref, ...), custom_call_target="tpu_custom_call" | custom-call | tf_op jit(solution)/shard_map/pallas_call | solution.py:121
  16.8 1.5 %collective-permute-start.1 = (bf16[4,384,256]{2,1,0:T(8,128)(2,1)S(1)}, bf16[4,384,256]{2,1,0:T(8,128)(2,1)S(1)}, u32[]{:S(2)}, u32[]{:S(2)}) collective-permute-start(bf16[4,384,256]{2,1,0:T(8,128)(2,1)S(1)} %get-tuple-element.22), channel_id=1, source_target_pairs={{0,1},{1,0},{2,3},{3,2},{4,5},{5,4},{6,7},{7,6},{8,9},{9,8},{10,11... | collective-permute-start | bytes 2359304 | tf_op jit(solution)/shard_map/ppermute | solution.py:29
  18.3 0.1 collective-permute-start.3
  18.4 0.4 collective-permute-start.5
  18.8 0.1 collective-permute-start
  18.9 1.3 %collective-permute-done.1 = bf16[4,384,256]{2,1,0:T(8,128)(2,1)S(1)} collective-permute-done((bf16[4,384,256]{2,1,0:T(8,128)(2,1)S(1)}, bf16[4,384,256]{2,1,0:T(8,128)(2,1)S(1)}, u32[]{:S(2)}, u32[]{:S(2)}) %collective-permute-start.1) | collective-permute-done | bytes 786464 | tf_op jit(solution)/shard_map/ppermute | solution.py:29
  20.2 0.2 add_convert_fusion.2
  20.4 0.0 copy-start.5
  20.4 3.8 %collective-permute-start.2 = (bf16[4,384,256]{2,1,0:T(8,128)(2,1)S(1)}, bf16[4,384,256]{2,1,0:T(8,128)(2,1)S(1)}, u32[]{:S(2)}, u32[]{:S(2)}) collective-permute-start(bf16[4,384,256]{2,1,0:T(8,128)(2,1)S(1)} %add_convert_fusion.2), channel_id=1, source_target_pairs={{0,4},{1,17},{2,6},{3,19},{4,0},{5,21},{6,2},{7,23},{8,12},{9,25},... | collective-permute-start | bytes 2359304 | tf_op jit(solution)/shard_map/ppermute | solution.py:29
  24.2 0.0 collective-permute-done.3
  24.2 0.2 add_convert_fusion.1
  24.4 0.8 collective-permute-start.4
  25.2 0.0 collective-permute-done.5
  25.2 0.0 copy-done.5
  25.2 0.2 add_convert_fusion
  25.4 2.2 %collective-permute-start.6 = (bf16[4,384,256]{2,1,0:T(8,128)(2,1)S(1)}, bf16[4,384,256]{2,1,0:T(8,128)(2,1)S(1)}, u32[]{:S(2)}, u32[]{:S(2)}) collective-permute-start(bf16[4,384,256]{2,1,0:T(8,128)(2,1)S(1)} %add_convert_fusion), channel_id=1, source_target_pairs={{0,6},{1,25},{2,0},{3,27},{4,2},{5,29},{6,4},{7,31},{8,14},{9,1},{... | collective-permute-start | bytes 2359304 | tf_op jit(solution)/shard_map/ppermute | solution.py:29
  27.6 0.0 collective-permute-done
  27.6 6.3 %collective-permute-done.2 = bf16[4,384,256]{2,1,0:T(8,128)(2,1)S(1)} collective-permute-done((bf16[4,384,256]{2,1,0:T(8,128)(2,1)S(1)}, bf16[4,384,256]{2,1,0:T(8,128)(2,1)S(1)}, u32[]{:S(2)}, u32[]{:S(2)}) %collective-permute-start.2) | collective-permute-done | bytes 786464 | tf_op jit(solution)/shard_map/ppermute | solution.py:29
  33.9 8.4 %collective-permute-done.4 = bf16[4,384,256]{2,1,0:T(8,128)(2,1)S(1)} collective-permute-done((bf16[4,384,256]{2,1,0:T(8,128)(2,1)S(1)}, bf16[4,384,256]{2,1,0:T(8,128)(2,1)S(1)}, u32[]{:S(2)}, u32[]{:S(2)}) %collective-permute-start.4) | collective-permute-done | bytes 786464 | tf_op jit(solution)/shard_map/ppermute | solution.py:29
  42.3 0.5 collective-permute-done.6
  42.8 0.6 fusion.6
  43.4 1.3 %collective-permute-start.7 = (bf16[384,256]{1,0:T(8,128)(2,1)S(1)}, bf16[384,256]{1,0:T(8,128)(2,1)S(1)}, u32[]{:S(2)}, u32[]{:S(2)}) collective-permute-start(bf16[384,256]{1,0:T(8,128)(2,1)S(1)} %get-tuple-element.37), channel_id=1, source_target_pairs={{0,8},{1,3},{2,10},{3,5},{4,12},{5,7},{6,14},{7,1},{8,16},{9,11},{... | collective-permute-start | bytes 589832 | tf_op jit(solution)/shard_map/ppermute | solution.py:29
  44.6 2.4 %collective-permute-start.9 = (bf16[384,256]{1,0:T(8,128)(2,1)S(1)}, bf16[384,256]{1,0:T(8,128)(2,1)S(1)}, u32[]{:S(2)}, u32[]{:S(2)}) collective-permute-start(bf16[384,256]{1,0:T(8,128)(2,1)S(1)} %get-tuple-element.38), channel_id=1, source_target_pairs={{0,16},{1,5},{2,18},{3,7},{4,20},{5,1},{6,22},{7,3},{8,24},{9,13},... | collective-permute-start | bytes 589832 | tf_op jit(solution)/shard_map/ppermute | solution.py:29
  47.1 1.2 %collective-permute-start.8 = (bf16[384,256]{1,0:T(8,128)(2,1)S(1)}, bf16[384,256]{1,0:T(8,128)(2,1)S(1)}, u32[]{:S(2)}, u32[]{:S(2)}) collective-permute-start(bf16[384,256]{1,0:T(8,128)(2,1)S(1)} %get-tuple-element.39), channel_id=1, source_target_pairs={{0,24},{1,7},{2,26},{3,1},{4,28},{5,3},{6,30},{7,5},{8,0},{9,15},{... | collective-permute-start | bytes 589832 | tf_op jit(solution)/shard_map/ppermute | solution.py:29
  48.3 1.2 %collective-permute-done.7 = bf16[384,256]{1,0:T(8,128)(2,1)S(1)} collective-permute-done((bf16[384,256]{1,0:T(8,128)(2,1)S(1)}, bf16[384,256]{1,0:T(8,128)(2,1)S(1)}, u32[]{:S(2)}, u32[]{:S(2)}) %collective-permute-start.7) | collective-permute-done | bytes 196640 | tf_op jit(solution)/shard_map/ppermute | solution.py:29
  49.5 3.1 %collective-permute-done.9 = bf16[384,256]{1,0:T(8,128)(2,1)S(1)} collective-permute-done((bf16[384,256]{1,0:T(8,128)(2,1)S(1)}, bf16[384,256]{1,0:T(8,128)(2,1)S(1)}, u32[]{:S(2)}, u32[]{:S(2)}) %collective-permute-start.9) | collective-permute-done | bytes 196640 | tf_op jit(solution)/shard_map/ppermute | solution.py:29
  52.6 0.0 collective-permute-done.8
  52.6 0.1 fusion.3
  52.7 3.0 %collective-permute-start.11 = (bf16[384,256]{1,0:T(8,128)(2,1)S(1)}, bf16[384,256]{1,0:T(8,128)(2,1)S(1)}, u32[]{:S(2)}, u32[]{:S(2)}) collective-permute-start(bf16[384,256]{1,0:T(8,128)(2,1)S(1)} %fusion.3), channel_id=1, source_target_pairs={{0,64},{1,65},{2,66},{3,67},{4,68},{5,69},{6,70},{7,71},{8,72},{9,... | collective-permute-start | bytes 589832 | tf_op jit(solution)/shard_map/ppermute | solution.py:29
  55.7 0.8 collective-permute-start.10
  56.4 2.3 %collective-permute-done.11 = bf16[384,256]{1,0:T(8,128)(2,1)S(1)} collective-permute-done((bf16[384,256]{1,0:T(8,128)(2,1)S(1)}, bf16[384,256]{1,0:T(8,128)(2,1)S(1)}, u32[]{:S(2)}, u32[]{:S(2)}) %collective-permute-start.11) | collective-permute-done | bytes 196640 | tf_op jit(solution)/shard_map/ppermute | solution.py:29
  58.8 6.1 %collective-permute-done.10 = bf16[384,256]{1,0:T(8,128)(2,1)S(1)} collective-permute-done((bf16[384,256]{1,0:T(8,128)(2,1)S(1)}, bf16[384,256]{1,0:T(8,128)(2,1)S(1)}, u32[]{:S(2)}, u32[]{:S(2)}) %collective-permute-start.10) | collective-permute-done | bytes 196640 | tf_op jit(solution)/shard_map/ppermute | solution.py:29
  64.8 0.1 multiply_convert_fusion
  64.9 1.0 collective-permute-start.14
  65.9 1.7 %collective-permute-start.13 = (bf16[384,256]{1,0:T(8,128)(2,1)S(1)}, bf16[384,256]{1,0:T(8,128)(2,1)S(1)}, u32[]{:S(2)}, u32[]{:S(2)}) collective-permute-start(bf16[384,256]{1,0:T(8,128)(2,1)S(1)} %multiply_convert_fusion), channel_id=1, source_target_pairs={{0,16},{1,5},{2,18},{3,7},{4,20},{5,1},{6,22},{7,3},{8,24},{9,13},... | collective-permute-start | bytes 589832 | tf_op jit(solution)/shard_map/ppermute | solution.py:29
  67.6 2.0 %collective-permute-start.12 = (bf16[384,256]{1,0:T(8,128)(2,1)S(1)}, bf16[384,256]{1,0:T(8,128)(2,1)S(1)}, u32[]{:S(2)}, u32[]{:S(2)}) collective-permute-start(bf16[384,256]{1,0:T(8,128)(2,1)S(1)} %multiply_convert_fusion), channel_id=1, source_target_pairs={{0,24},{1,7},{2,26},{3,1},{4,28},{5,3},{6,30},{7,5},{8,0},{9,15},{... | collective-permute-start | bytes 589832 | tf_op jit(solution)/shard_map/ppermute | solution.py:29
  69.6 3.3 %collective-permute-done.14 = bf16[384,256]{1,0:T(8,128)(2,1)S(1)} collective-permute-done((bf16[384,256]{1,0:T(8,128)(2,1)S(1)}, bf16[384,256]{1,0:T(8,128)(2,1)S(1)}, u32[]{:S(2)}, u32[]{:S(2)}) %collective-permute-start.14) | collective-permute-done | bytes 196640 | tf_op jit(solution)/shard_map/ppermute | solution.py:29
  72.9 0.0 collective-permute-done.13
  72.9 0.7 collective-permute-done.12
  73.7 0.1 pad_maximum_fusion.own_ref
  73.8 2.7 %collective-permute-start.15 = (bf16[4,384,256]{2,1,0:T(8,128)(2,1)S(1)}, bf16[4,384,256]{2,1,0:T(8,128)(2,1)S(1)}, u32[]{:S(2)}, u32[]{:S(2)}) collective-permute-start(bf16[4,384,256]{2,1,0:T(8,128)(2,1)S(1)} %pad_maximum_fusion.own_ref), channel_id=1, source_target_pairs={{0,1},{1,0},{2,3},{3,2},{4,5},{5,4},{6,7},{7,6},{8,9},{9,8},{10,11... | collective-permute-start | bytes 2359304 | tf_op jit(solution)/shard_map/ppermute | solution.py:29
  76.5 1.4 %collective-permute-start.16 = (bf16[4,384,256]{2,1,0:T(8,128)(2,1)S(1)}, bf16[4,384,256]{2,1,0:T(8,128)(2,1)S(1)}, u32[]{:S(2)}, u32[]{:S(2)}) collective-permute-start(bf16[4,384,256]{2,1,0:T(8,128)(2,1)S(1)} %pad_maximum_fusion.own_ref), channel_id=1, source_target_pairs={{0,2},{1,9},{2,4},{3,11},{4,6},{5,13},{6,0},{7,15},{8,10},{9,17},{... | collective-permute-start | bytes 2359304 | tf_op jit(solution)/shard_map/ppermute | solution.py:29
  77.9 2.1 %collective-permute-start.20 = (bf16[4,384,256]{2,1,0:T(8,128)(2,1)S(1)}, bf16[4,384,256]{2,1,0:T(8,128)(2,1)S(1)}, u32[]{:S(2)}, u32[]{:S(2)}) collective-permute-start(bf16[4,384,256]{2,1,0:T(8,128)(2,1)S(1)} %pad_maximum_fusion.own_ref), channel_id=1, source_target_pairs={{0,4},{1,17},{2,6},{3,19},{4,0},{5,21},{6,2},{7,23},{8,12},{9,25},... | collective-permute-start | bytes 2359304 | tf_op jit(solution)/shard_map/ppermute | solution.py:29
  80.0 0.6 collective-permute-start.18
  80.6 0.0 collective-permute-done.15.other_ref
  80.6 8.7 %shard_map.47 = (f32[1536,512]{1,0:T(8,128)}, bf16[4,384,256]{2,1,0:T(8,128)(2,1)S(1)}, bf16[1536,6144]{1,0:T(8,128)(2,1)S(1)}) custom-call(s32[1]{0:T(128)} %bitcast.here_ref, bf16[1536,6144]{1,0:T(8,128)(2,1)} %bitcast.24, bf16[4,384,256]{2,1,0:T(8,128)(2,1)S(1)} %collective-permute-done.15.other_ref, bf16[4,384,256]{2,1,0:T(8,128)(2,1)S(1)} %pad_maximum_fusion.own_ref), custom_call_target="tpu_custom_call" | custom-call | tf_op jit(solution)/shard_map/pallas_call | solution.py:183
  89.3 0.0 collective-permute-done.16
  89.3 0.2 add.57.refs_0_
  89.6 1.3 %collective-permute-start.17 = (bf16[4,384,256]{2,1,0:T(8,128)(2,1)S(1)}, bf16[4,384,256]{2,1,0:T(8,128)(2,1)S(1)}, u32[]{:S(2)}, u32[]{:S(2)}) collective-permute-start(bf16[4,384,256]{2,1,0:T(8,128)(2,1)S(1)} %add.57.refs_0_), channel_id=1, source_target_pairs={{0,1},{1,0},{2,3},{3,2},{4,5},{5,4},{6,7},{7,6},{8,9},{9,8},{10,11... | collective-permute-start | bytes 2359304 | tf_op jit(solution)/shard_map/ppermute | solution.py:29
  90.9 0.0 copy-done.2
  90.9 1.9 %copy-done = f32[1536,512]{1,0:T(8,128)S(1)} copy-done((f32[1536,512]{1,0:T(8,128)S(1)}, f32[1536,512]{1,0:T(8,128)}, u32[]{:S(2)}) %copy-start) | copy-done | bytes 3145752
  92.8 3.0 %shard_map.48 = (f32[1536,256]{1,0:T(8,128)}, bf16[4,384,256]{2,1,0:T(8,128)(2,1)S(1)}) custom-call(s32[1]{0:T(128)} %bitcast.here_ref, bf16[1536,6144]{1,0:T(8,128)(2,1)S(1)} %get-tuple-element.27.held, f32[1536,512]{1,0:T(8,128)S(1)} %copy-done, f32[1536,128]{1,0:T(8,128)S(1)} %copy-done.2, bf16[4,384,256]{2,1,0:T(8,128)(2,1)S(1)} %add.57.refs_0_), custom_call_target="tpu_custom_call" | custom-call | tf_op jit(solution)/shard_map/pallas_call | solution.py:251
  95.8 2.3 %collective-permute-done.20 = bf16[4,384,256]{2,1,0:T(8,128)(2,1)S(1)} collective-permute-done((bf16[4,384,256]{2,1,0:T(8,128)(2,1)S(1)}, bf16[4,384,256]{2,1,0:T(8,128)(2,1)S(1)}, u32[]{:S(2)}, u32[]{:S(2)}) %collective-permute-start.20) | collective-permute-done | bytes 786464 | tf_op jit(solution)/shard_map/ppermute | solution.py:29
  98.1 0.0 collective-permute-done.18
  98.1 0.0 collective-permute-done.17.refs_0_
  98.1 0.2 fusion.4
  98.3 1.0 collective-permute-start.21
  99.3 0.3 collective-permute-start.19
  99.7 4.0 %shard_map.49.refs_3_ = bf16[1536,512]{1,0:T(8,128)(2,1)} custom-call(s32[1]{0:T(128)} %bitcast.here_ref, bf16[1536,6144]{1,0:T(8,128)(2,1)S(1)} %get-tuple-element.27.held, f32[1536,256]{1,0:T(8,128)S(1)} %copy-done.3, f32[1536,128]{1,0:T(8,128)S(1)} %copy-done.2, bf16[4,384,256]{2,1,0:T(8,128)(2,1)S(1)} %get-tuple-element.36.refs_0_, ...), custom_call_target="tpu_custom_call" | custom-call | tf_op jit(solution)/shard_map/pallas_call | solution.py:251
  103.7 0.0 collective-permute-done.21.refs_2_
  103.7 0.0 collective-permute-done.19.refs_1_
  103.7 5.4 %shard_map.50 = bf16[1536,512]{1,0:T(8,128)(2,1)} custom-call(s32[1]{0:T(128)} %bitcast.here_ref, bf16[1536,6144]{1,0:T(8,128)(2,1)S(1)} %get-tuple-element.27.held, f32[1536,512]{1,0:T(8,128)S(1)} %copy-done.1, f32[1536,128]{1,0:T(8,128)S(1)} %copy-done.2, bf16[4,384,256]{2,1,0:T(8,128)(2,1)S(1)} %collective-permute-done.17.refs_0_, ...), custom_call_target="tpu_custom_call", output_to_operand_aliasing={{}: (7, {})} | custom-call | tf_op jit(solution)/shard_map/pallas_call | solution.py:251
  (7 shorter events, 0.1 us)
Async XLA Ops:
  1.3 0.7 copy-start.4
  16.8 3.4 %collective-permute-start.1 = (bf16[4,384,256]{2,1,0:T(8,128)(2,1)S(1)}, bf16[4,384,256]{2,1,0:T(8,128)(2,1)S(1)}, u32[]{:S(2)}, u32[]{:S(2)}) collective-permute-start(bf16[4,384,256]{2,1,0:T(8,128)(2,1)S(1)} %get-tuple-element.22), channel_id=1, source_target_pairs={{0,1},{1,0},{2,3},{3,2},{4,5},{5,4},{6,7},{7,6},{8,9},{9,8},{10,11... | collective-permute-start | bytes 2359304 | tf_op jit(solution)/shard_map/ppermute | solution.py:29
  18.3 5.9 %collective-permute-start.3 = (bf16[4,384,256]{2,1,0:T(8,128)(2,1)S(1)}, bf16[4,384,256]{2,1,0:T(8,128)(2,1)S(1)}, u32[]{:S(2)}, u32[]{:S(2)}) collective-permute-start(bf16[4,384,256]{2,1,0:T(8,128)(2,1)S(1)} %get-tuple-element.24), channel_id=1, source_target_pairs={{0,1},{1,0},{2,3},{3,2},{4,5},{5,4},{6,7},{7,6},{8,9},{9,8},{10,11... | collective-permute-start | bytes 2359304 | tf_op jit(solution)/shard_map/ppermute | solution.py:29
  18.4 6.8 %collective-permute-start.5 = (bf16[4,384,256]{2,1,0:T(8,128)(2,1)S(1)}, bf16[4,384,256]{2,1,0:T(8,128)(2,1)S(1)}, u32[]{:S(2)}, u32[]{:S(2)}) collective-permute-start(bf16[4,384,256]{2,1,0:T(8,128)(2,1)S(1)} %get-tuple-element.26), channel_id=1, source_target_pairs={{0,1},{1,0},{2,3},{3,2},{4,5},{5,4},{6,7},{7,6},{8,9},{9,8},{10,11... | collective-permute-start | bytes 2359304 | tf_op jit(solution)/shard_map/ppermute | solution.py:29
  18.8 8.8 %collective-permute-start = (bf16[4,384,256]{2,1,0:T(8,128)(2,1)S(1)}, bf16[4,384,256]{2,1,0:T(8,128)(2,1)S(1)}, u32[]{:S(2)}, u32[]{:S(2)}) collective-permute-start(bf16[4,384,256]{2,1,0:T(8,128)(2,1)S(1)} %get-tuple-element.20), channel_id=1, source_target_pairs={{0,1},{1,0},{2,3},{3,2},{4,5},{5,4},{6,7},{7,6},{8,9},{9,8},{10,11... | collective-permute-start | bytes 2359304 | tf_op jit(solution)/shard_map/ppermute | solution.py:29
  20.4 4.8 %copy-start.5 = (bf16[4,384,256]{2,1,0:T(8,128)(2,1)S(1)}, bf16[4,384,256]{2,1,0:T(8,128)(2,1)}, u32[]{:S(2)}) copy-start(bf16[4,384,256]{2,1,0:T(8,128)(2,1)} %get-tuple-element.25) | copy-start | bytes 2359300
  20.4 13.5 %collective-permute-start.2 = (bf16[4,384,256]{2,1,0:T(8,128)(2,1)S(1)}, bf16[4,384,256]{2,1,0:T(8,128)(2,1)S(1)}, u32[]{:S(2)}, u32[]{:S(2)}) collective-permute-start(bf16[4,384,256]{2,1,0:T(8,128)(2,1)S(1)} %add_convert_fusion.2), channel_id=1, source_target_pairs={{0,4},{1,17},{2,6},{3,19},{4,0},{5,21},{6,2},{7,23},{8,12},{9,25},... | collective-permute-start | bytes 2359304 | tf_op jit(solution)/shard_map/ppermute | solution.py:29
  24.4 17.9 %collective-permute-start.4 = (bf16[4,384,256]{2,1,0:T(8,128)(2,1)S(1)}, bf16[4,384,256]{2,1,0:T(8,128)(2,1)S(1)}, u32[]{:S(2)}, u32[]{:S(2)}) collective-permute-start(bf16[4,384,256]{2,1,0:T(8,128)(2,1)S(1)} %add_convert_fusion.1), channel_id=1, source_target_pairs={{0,2},{1,9},{2,4},{3,11},{4,6},{5,13},{6,0},{7,15},{8,10},{9,17},{... | collective-permute-start | bytes 2359304 | tf_op jit(solution)/shard_map/ppermute | solution.py:29
  25.4 17.4 %collective-permute-start.6 = (bf16[4,384,256]{2,1,0:T(8,128)(2,1)S(1)}, bf16[4,384,256]{2,1,0:T(8,128)(2,1)S(1)}, u32[]{:S(2)}, u32[]{:S(2)}) collective-permute-start(bf16[4,384,256]{2,1,0:T(8,128)(2,1)S(1)} %add_convert_fusion), channel_id=1, source_target_pairs={{0,6},{1,25},{2,0},{3,27},{4,2},{5,29},{6,4},{7,31},{8,14},{9,1},{... | collective-permute-start | bytes 2359304 | tf_op jit(solution)/shard_map/ppermute | solution.py:29
  43.4 6.1 %collective-permute-start.7 = (bf16[384,256]{1,0:T(8,128)(2,1)S(1)}, bf16[384,256]{1,0:T(8,128)(2,1)S(1)}, u32[]{:S(2)}, u32[]{:S(2)}) collective-permute-start(bf16[384,256]{1,0:T(8,128)(2,1)S(1)} %get-tuple-element.37), channel_id=1, source_target_pairs={{0,8},{1,3},{2,10},{3,5},{4,12},{5,7},{6,14},{7,1},{8,16},{9,11},{... | collective-permute-start | bytes 589832 | tf_op jit(solution)/shard_map/ppermute | solution.py:29
  44.6 7.9 %collective-permute-start.9 = (bf16[384,256]{1,0:T(8,128)(2,1)S(1)}, bf16[384,256]{1,0:T(8,128)(2,1)S(1)}, u32[]{:S(2)}, u32[]{:S(2)}) collective-permute-start(bf16[384,256]{1,0:T(8,128)(2,1)S(1)} %get-tuple-element.38), channel_id=1, source_target_pairs={{0,16},{1,5},{2,18},{3,7},{4,20},{5,1},{6,22},{7,3},{8,24},{9,13},... | collective-permute-start | bytes 589832 | tf_op jit(solution)/shard_map/ppermute | solution.py:29
  47.1 5.5 %collective-permute-start.8 = (bf16[384,256]{1,0:T(8,128)(2,1)S(1)}, bf16[384,256]{1,0:T(8,128)(2,1)S(1)}, u32[]{:S(2)}, u32[]{:S(2)}) collective-permute-start(bf16[384,256]{1,0:T(8,128)(2,1)S(1)} %get-tuple-element.39), channel_id=1, source_target_pairs={{0,24},{1,7},{2,26},{3,1},{4,28},{5,3},{6,30},{7,5},{8,0},{9,15},{... | collective-permute-start | bytes 589832 | tf_op jit(solution)/shard_map/ppermute | solution.py:29
  52.7 6.1 %collective-permute-start.11 = (bf16[384,256]{1,0:T(8,128)(2,1)S(1)}, bf16[384,256]{1,0:T(8,128)(2,1)S(1)}, u32[]{:S(2)}, u32[]{:S(2)}) collective-permute-start(bf16[384,256]{1,0:T(8,128)(2,1)S(1)} %fusion.3), channel_id=1, source_target_pairs={{0,64},{1,65},{2,66},{3,67},{4,68},{5,69},{6,70},{7,71},{8,72},{9,... | collective-permute-start | bytes 589832 | tf_op jit(solution)/shard_map/ppermute | solution.py:29
  55.7 9.2 %collective-permute-start.10 = (bf16[384,256]{1,0:T(8,128)(2,1)S(1)}, bf16[384,256]{1,0:T(8,128)(2,1)S(1)}, u32[]{:S(2)}, u32[]{:S(2)}) collective-permute-start(bf16[384,256]{1,0:T(8,128)(2,1)S(1)} %fusion.3), channel_id=1, source_target_pairs={{0,96},{1,97},{2,98},{3,99},{4,100},{5,101},{6,102},{7,103},{8,104... | collective-permute-start | bytes 589832 | tf_op jit(solution)/shard_map/ppermute | solution.py:29
  64.9 8.0 %collective-permute-start.14 = (bf16[384,256]{1,0:T(8,128)(2,1)S(1)}, bf16[384,256]{1,0:T(8,128)(2,1)S(1)}, u32[]{:S(2)}, u32[]{:S(2)}) collective-permute-start(bf16[384,256]{1,0:T(8,128)(2,1)S(1)} %multiply_convert_fusion), channel_id=1, source_target_pairs={{0,8},{1,3},{2,10},{3,5},{4,12},{5,7},{6,14},{7,1},{8,16},{9,11},{... | collective-permute-start | bytes 589832 | tf_op jit(solution)/shard_map/ppermute | solution.py:29
  65.9 7.0 %collective-permute-start.13 = (bf16[384,256]{1,0:T(8,128)(2,1)S(1)}, bf16[384,256]{1,0:T(8,128)(2,1)S(1)}, u32[]{:S(2)}, u32[]{:S(2)}) collective-permute-start(bf16[384,256]{1,0:T(8,128)(2,1)S(1)} %multiply_convert_fusion), channel_id=1, source_target_pairs={{0,16},{1,5},{2,18},{3,7},{4,20},{5,1},{6,22},{7,3},{8,24},{9,13},... | collective-permute-start | bytes 589832 | tf_op jit(solution)/shard_map/ppermute | solution.py:29
  67.6 6.1 %collective-permute-start.12 = (bf16[384,256]{1,0:T(8,128)(2,1)S(1)}, bf16[384,256]{1,0:T(8,128)(2,1)S(1)}, u32[]{:S(2)}, u32[]{:S(2)}) collective-permute-start(bf16[384,256]{1,0:T(8,128)(2,1)S(1)} %multiply_convert_fusion), channel_id=1, source_target_pairs={{0,24},{1,7},{2,26},{3,1},{4,28},{5,3},{6,30},{7,5},{8,0},{9,15},{... | collective-permute-start | bytes 589832 | tf_op jit(solution)/shard_map/ppermute | solution.py:29
  73.8 6.8 %collective-permute-start.15 = (bf16[4,384,256]{2,1,0:T(8,128)(2,1)S(1)}, bf16[4,384,256]{2,1,0:T(8,128)(2,1)S(1)}, u32[]{:S(2)}, u32[]{:S(2)}) collective-permute-start(bf16[4,384,256]{2,1,0:T(8,128)(2,1)S(1)} %pad_maximum_fusion.own_ref), channel_id=1, source_target_pairs={{0,1},{1,0},{2,3},{3,2},{4,5},{5,4},{6,7},{7,6},{8,9},{9,8},{10,11... | collective-permute-start | bytes 2359304 | tf_op jit(solution)/shard_map/ppermute | solution.py:29
  76.5 12.9 %collective-permute-start.16 = (bf16[4,384,256]{2,1,0:T(8,128)(2,1)S(1)}, bf16[4,384,256]{2,1,0:T(8,128)(2,1)S(1)}, u32[]{:S(2)}, u32[]{:S(2)}) collective-permute-start(bf16[4,384,256]{2,1,0:T(8,128)(2,1)S(1)} %pad_maximum_fusion.own_ref), channel_id=1, source_target_pairs={{0,2},{1,9},{2,4},{3,11},{4,6},{5,13},{6,0},{7,15},{8,10},{9,17},{... | collective-permute-start | bytes 2359304 | tf_op jit(solution)/shard_map/ppermute | solution.py:29
  77.9 20.2 %collective-permute-start.20 = (bf16[4,384,256]{2,1,0:T(8,128)(2,1)S(1)}, bf16[4,384,256]{2,1,0:T(8,128)(2,1)S(1)}, u32[]{:S(2)}, u32[]{:S(2)}) collective-permute-start(bf16[4,384,256]{2,1,0:T(8,128)(2,1)S(1)} %pad_maximum_fusion.own_ref), channel_id=1, source_target_pairs={{0,4},{1,17},{2,6},{3,19},{4,0},{5,21},{6,2},{7,23},{8,12},{9,25},... | collective-permute-start | bytes 2359304 | tf_op jit(solution)/shard_map/ppermute | solution.py:29
  80.0 18.1 %collective-permute-start.18 = (bf16[4,384,256]{2,1,0:T(8,128)(2,1)S(1)}, bf16[4,384,256]{2,1,0:T(8,128)(2,1)S(1)}, u32[]{:S(2)}, u32[]{:S(2)}) collective-permute-start(bf16[4,384,256]{2,1,0:T(8,128)(2,1)S(1)} %pad_maximum_fusion.own_ref), channel_id=1, source_target_pairs={{0,6},{1,25},{2,0},{3,27},{4,2},{5,29},{6,4},{7,31},{8,14},{9,1},{... | collective-permute-start | bytes 2359304 | tf_op jit(solution)/shard_map/ppermute | solution.py:29
  89.3 1.5 %copy-start.2 = (f32[1536,128]{1,0:T(8,128)S(1)}, f32[1536,128]{1,0:T(8,128)}, u32[]{:S(2)}) copy-start(f32[1536,128]{1,0:T(8,128)} %get-tuple-element.29.f_ref) | copy-start | bytes 2359300
  89.6 8.6 %collective-permute-start.17 = (bf16[4,384,256]{2,1,0:T(8,128)(2,1)S(1)}, bf16[4,384,256]{2,1,0:T(8,128)(2,1)S(1)}, u32[]{:S(2)}, u32[]{:S(2)}) collective-permute-start(bf16[4,384,256]{2,1,0:T(8,128)(2,1)S(1)} %add.57.refs_0_), channel_id=1, source_target_pairs={{0,1},{1,0},{2,3},{3,2},{4,5},{5,4},{6,7},{7,6},{8,9},{9,8},{10,11... | collective-permute-start | bytes 2359304 | tf_op jit(solution)/shard_map/ppermute | solution.py:29
  90.9 1.9 %copy-start = (f32[1536,512]{1,0:T(8,128)S(1)}, f32[1536,512]{1,0:T(8,128)}, u32[]{:S(2)}) copy-start(f32[1536,512]{1,0:T(8,128)} %get-tuple-element.28.before_ref) | copy-start | bytes 9437188
  98.1 1.5 %copy-start.3 = (f32[1536,256]{1,0:T(8,128)S(1)}, f32[1536,256]{1,0:T(8,128)}, u32[]{:S(2)}) copy-start(f32[1536,256]{1,0:T(8,128)} %get-tuple-element.32.before_ref) | copy-start | bytes 4718596
  98.3 5.4 %collective-permute-start.21 = (bf16[4,384,256]{2,1,0:T(8,128)(2,1)S(1)}, bf16[4,384,256]{2,1,0:T(8,128)(2,1)S(1)}, u32[]{:S(2)}, u32[]{:S(2)}) collective-permute-start(bf16[4,384,256]{2,1,0:T(8,128)(2,1)S(1)} %get-tuple-element.35.refs_1_), channel_id=1, source_target_pairs={{0,1},{1,0},{2,3},{3,2},{4,5},{5,4},{6,7},{7,6},{8,9},{9,8},{10,11... | collective-permute-start | bytes 2359304 | tf_op jit(solution)/shard_map/ppermute | solution.py:29
  99.3 4.4 %collective-permute-start.19 = (bf16[4,384,256]{2,1,0:T(8,128)(2,1)S(1)}, bf16[4,384,256]{2,1,0:T(8,128)(2,1)S(1)}, u32[]{:S(2)}, u32[]{:S(2)}) collective-permute-start(bf16[4,384,256]{2,1,0:T(8,128)(2,1)S(1)} %get-tuple-element.36.refs_0_), channel_id=1, source_target_pairs={{0,1},{1,0},{2,3},{3,2},{4,5},{5,4},{6,7},{7,6},{8,9},{9,8},{10,11... | collective-permute-start | bytes 2359304 | tf_op jit(solution)/shard_map/ppermute | solution.py:29
  99.6 4.1 %copy-start.1 = (f32[1536,512]{1,0:T(8,128)S(1)}, f32[1536,512]{1,0:T(8,128)}, u32[]{:S(2)}) copy-start(f32[1536,512]{1,0:T(8,128)} %get-tuple-element.28.before_ref) | copy-start | bytes 9437188
